TPU v7x, 512 devices: a whole 4x8x8 slice. The times are simulated.
512 devices in a mesh: ctx: 128 (over y, z, core), head: 4 (over x).
Axes of the slice: x: 4, y: 8, z: 8, core: 2. Of those that a mesh axis runs over, the one named last changes fastest.
Arguments:
- queries: bfloat16 [65536, 32, 128], P(('ctx', 'head')), may hold values from -6 to 6
- key_states: bfloat16 [65536, 4, 128], P(('ctx', 'head')), may hold values from -6 to 6
- value_states: bfloat16 [65536, 4, 128], P(('ctx', 'head')), may hold values from -6 to 6
- out_grad: bfloat16 [65536, 32, 128], P(('ctx', 'head')), may hold values from -6 to 6
- log_sums: float32 [32, 65536], P('head', 'ctx'), may hold values from 3 to 6
- row_deltas: float32 [32, 65536], P('head', 'ctx'), may hold values from -10 to 10
- block_pairs: int32 [1024, 4], replicated, may hold values from 0 to 1023, as said below
- pair_kinds: int32 [1024, 4], replicated, may hold values from 0 to 2, as said below
Outputs:
- query_grad: bfloat16 [65536, 32, 128], P(('ctx', 'head'))
- key_grad: bfloat16 [65536, 4, 128], P(('ctx', 'head'))
- value_grad: bfloat16 [65536, 4, 128], P(('ctx', 'head'))
Inputs may be any that keep to these rules, and one draw needn't show every extreme that they name: `block_pairs`: row g lists the key blocks of query block g. Slot 0 names g itself, slot 1 names g - 1, slot 2 names key block 0; slots 3 and up name blocks of shards at least two shards before the shard of g, never of shard 0. The blocks of the live slots of a row are distinct and none is later than g; a slot of kind 0 names block 0. Counting shards of 8 consecutive query blocks, the query blocks of one shard name at most one key block held by any other single shard, and this is reached. `pair_kinds`: 1 marks a full block pair, 2 the pair of a block with itself, 0 an unused slot. Slot 0 is always 2 and no other slot is 2; slot 1 is 0 only for g = 0; slot 2 is 0 exactly for g < 2 and for the query blocks of the second shard.
All inputs are finite; a program needn't handle non-finite values.
Results may differ from a plain program's by a relative error of at most 0.0012.
The roundings to bfloat16 on the way count: a program that leaves them out, or rounds other values in their place, can miss the bound.
Values may be sent and summed in bfloat16 or wider, within the bound.
No kernel may reach another device: no remote copies, remote signals or barrier semaphores. Data moves between devices by JAX's collectives and lax.ppermute only.
A program may use at most 64 MiB of HBM per device.

v0:
```python
from functools import partial

import jax
import jax.numpy as jnp
from jax import lax
from jax.sharding import PartitionSpec as P

BLOCK = 64


def tile_terms(
    query_part, grad_part, log_part, delta_part, key_tile, value_tile, slot_kinds, causal, lead_axis
):
    query_form = lead_axis + "bgd"
    score_scale = key_tile.shape[-1] ** (-0.5)
    scores = (
        jnp.einsum(
            query_form + ",nkd->ngbk", query_part, key_tile, preferred_element_type=jnp.float32
        )
        * score_scale
    )
    weights = jnp.exp(scores - log_part[..., None])
    full_pair = (slot_kinds == 1)[:, None, None, None]
    diagonal_pair = (slot_kinds == 2)[:, None, None, None]
    weights = jnp.where(full_pair | diagonal_pair & causal, weights, 0.0)
    value_term = jnp.einsum(
        "ngbk," + query_form + "->nkd",
        weights.astype(jnp.bfloat16),
        grad_part,
        preferred_element_type=jnp.float32,
    )
    prob_grad = jnp.einsum(
        query_form + ",nkd->ngbk", grad_part, value_tile, preferred_element_type=jnp.float32
    )
    dscore = (weights * (prob_grad - delta_part[..., None])).astype(jnp.bfloat16)
    query_term = (
        jnp.einsum("ngbk,nkd->" + query_form, dscore, key_tile, preferred_element_type=jnp.float32)
        * score_scale
    )
    key_term = (
        jnp.einsum(
            "ngbk," + query_form + "->nkd", dscore, query_part, preferred_element_type=jnp.float32
        )
        * score_scale
    )
    return (query_term, key_term, value_term)


def block_step(pair_acc, column, kv_table, causal):
    query_part, grad_part, log_part, delta_part, slot_index, slot_kinds = column
    tile_pair = kv_table[slot_index]
    query_term, key_term, value_term = tile_terms(
        query_part,
        grad_part,
        log_part,
        delta_part,
        tile_pair[:, :, 0],
        tile_pair[:, :, 1],
        slot_kinds,
        causal,
        "",
    )
    pair_acc = pair_acc.at[slot_index].add(jnp.stack([key_term, value_term], axis=2))
    return (pair_acc, query_term)


def shards(
    queries, key_states, value_states, out_grad, log_sums, row_deltas, block_pairs, pair_kinds
):
    head_queries, head_grads, head_keys, head_values = (
        lax.all_to_all(queries, "head", split_axis=1, concat_axis=0, tiled=True),
        lax.all_to_all(out_grad, "head", split_axis=1, concat_axis=0, tiled=True),
        lax.all_to_all(key_states, "head", split_axis=1, concat_axis=0, tiled=True),
        lax.all_to_all(value_states, "head", split_axis=1, concat_axis=0, tiled=True),
    )
    token_rows, head_group, head_width = head_queries.shape
    blocks_here = token_rows // BLOCK
    shard_count = lax.axis_size("ctx")
    my_rank = lax.axis_index("ctx")
    query_blocks = head_queries.reshape(blocks_here, BLOCK, head_group, head_width)
    grad_blocks = head_grads.reshape(blocks_here, BLOCK, head_group, head_width)
    kv_local = jnp.concatenate([head_keys, head_values], axis=1).reshape(
        blocks_here, BLOCK, 2, head_width
    )
    log_blocks = log_sums.reshape(head_group, blocks_here, BLOCK).transpose(1, 0, 2)
    delta_blocks = row_deltas.reshape(head_group, blocks_here, BLOCK).transpose(1, 0, 2)
    causal = jnp.arange(BLOCK)[:, None] >= jnp.arange(BLOCK)[None, :]
    my_pairs = lax.dynamic_slice_in_dim(block_pairs, my_rank * blocks_here, blocks_here, 0)
    my_kinds = lax.dynamic_slice_in_dim(pair_kinds, my_rank * blocks_here, blocks_here, 0)
    pair_owner = my_pairs // blocks_here
    table_index = jnp.where(
        pair_owner == my_rank, my_pairs - my_rank * blocks_here, blocks_here + pair_owner
    )
    every_owner = block_pairs // blocks_here
    asking_shard = (jnp.arange(block_pairs.shape[0], dtype=jnp.int32) // blocks_here)[:, None]
    is_asked = (pair_kinds > 0) & (every_owner == my_rank) & (asking_shard != my_rank)
    local_id = jnp.where(is_asked, block_pairs - my_rank * blocks_here, -1)
    wanted = jnp.max(local_id.reshape(shard_count, -1), axis=1)
    outgoing = kv_local[jnp.maximum(wanted, 0)]
    pair_acc = jnp.zeros((blocks_here + shard_count, BLOCK, 2, head_width), jnp.float32)
    first_slot = 0
    arrived = lax.all_to_all(outgoing, "ctx", split_axis=0, concat_axis=0, tiled=True)
    kv_table = jnp.concatenate([kv_local, arrived], axis=0)
    pair_acc, query_sums = lax.scan(
        partial(block_step, kv_table=kv_table, causal=causal),
        pair_acc,
        (query_blocks, grad_blocks, log_blocks, delta_blocks, table_index, my_kinds),
    )
    remote_sums = pair_acc[blocks_here:]
    returned = lax.all_to_all(remote_sums, "ctx", split_axis=0, concat_axis=0, tiled=True)
    chosen = (wanted[:, None] == jnp.arange(blocks_here, dtype=jnp.int32)[None, :]).astype(
        jnp.float32
    )
    kv_sums = pair_acc[:blocks_here] + jnp.einsum(
        "rl,rbcd->lbcd", chosen, returned, precision=lax.Precision.HIGHEST
    )
    key_out = kv_sums[:, :, 0].reshape(token_rows, 1, head_width).astype(jnp.bfloat16)
    value_out = kv_sums[:, :, 1].reshape(token_rows, 1, head_width).astype(jnp.bfloat16)
    query_out = query_sums.reshape(token_rows, head_group, head_width).astype(jnp.bfloat16)
    return (
        lax.all_to_all(query_out, "head", split_axis=0, concat_axis=1, tiled=True),
        lax.all_to_all(key_out, "head", split_axis=0, concat_axis=1, tiled=True),
        lax.all_to_all(value_out, "head", split_axis=0, concat_axis=1, tiled=True),
    )


def solution(mesh):
    in_specs = (
        P(("ctx", "head"), None, None),
        P(("ctx", "head"), None, None),
        P(("ctx", "head"), None, None),
        P(("ctx", "head"), None, None),
        P("head", "ctx"),
        P("head", "ctx"),
        P(),
        P(),
    )
    out_specs = (
        P(("ctx", "head"), None, None),
        P(("ctx", "head"), None, None),
        P(("ctx", "head"), None, None),
    )
    return jax.shard_map(shards, mesh=mesh, in_specs=in_specs, out_specs=out_specs, check_vma=False)
```

profile of v0, /device:TPU:1, one launch (start us, length us, event | category | flops | bytes accessed | tf_op | source)
XLA Modules:
  0.0 513.8 jit_solution(12273406897241032288)
XLA Ops:
  2.2 4.8 all-to-all-start.1
  8.7 3.2 all-to-all-done.1
  11.9 3.3 all-to-all-start
  20.0 3.5 all-to-all-start.3
  26.2 7.1 %all-to-all-done.3 = bf16[128,32,128]{2,0,1:T(8,128)(2,1)S(1)} async-done(((bf16[128,32,128]{2,0,1:T(8,128)(2,1)}), bf16[128,32,128]{2,0,1:T(8,128)(2,1)S(1)}, u32[]{:S(2)}, u32[]{:S(2)}) %all-to-all-start.3) | async-done | bytes 1048608 | tf_op jit(solution)/shard_map/all_to_all | solution.py:71
  33.3 3.5 all-to-all-start.4
  37.2 3.1 gather_fusion.1
  40.2 6.8 %all-to-all-done.4 = bf16[128,32,128]{2,0,1:T(8,128)(2,1)S(1)} async-done(((bf16[128,32,128]{2,0,1:T(8,128)(2,1)}), bf16[128,32,128]{2,0,1:T(8,128)(2,1)S(1)}, u32[]{:S(2)}, u32[]{:S(2)}) %all-to-all-start.4) | async-done | bytes 1048608 | tf_op jit(solution)/shard_map/all_to_all | solution.py:72
  47.0 25.0 %all-to-all-start.2 = ((bf16[128,64,2,128]{3,1,2,0:T(8,128)(2,1)}), bf16[128,64,2,128]{3,1,2,0:T(8,128)(2,1)}, u32[]{:S(2)}, u32[]{:S(2)}) async-start(bf16[128,64,2,128]{3,1,2,0:T(8,128)(2,1)} %gather_fusion.1), calls=%async_computation.2 | async-start | bytes 8388608 | tf_op jit(solution)/shard_map/all_to_all | solution.py:102
  74.9 92.7 %all-to-all-done.2 = bf16[128,64,2,128]{3,1,2,0:T(8,128)(2,1)} async-done(((bf16[128,64,2,128]{3,1,2,0:T(8,128)(2,1)}), bf16[128,64,2,128]{3,1,2,0:T(8,128)(2,1)}, u32[]{:S(2)}, u32[]{:S(2)}) %all-to-all-start.2) | async-done | bytes 4194336 | tf_op jit(solution)/shard_map/all_to_all | solution.py:102
  167.6 6.3 %pad_maximum_fusion.1 = bf16[136,64,2,128]{3,1,2,0:T(8,128)(2,1)} fusion(bf16[128,64,2,128]{3,1,2,0:T(8,128)(2,1)} %all-to-all-done.2, bf16[8,64,1,128]{3,1,0,2:T(8,128)(2,1)S(1)} %bitcast.184, bf16[8,64,1,128]{3,1,0,2:T(8,128)(2,1)S(1)} %bitcast.186), kind=kLoop, calls=%fused_computation.43 | loop fusion | flops 9043968 | bytes 8912896 | tf_op jit(solution)/shard_map/concatenate | solution.py:103
  173.8 4.6 broadcast_in_dim.21
  178.4 69.2 %while.13 = (s32[]{:T(128)}, f32[136,64,2,128]{3,1,2,0:T(8,128)}, bf16[8,64,8,128]{3,2,1,0:T(8,128)(2,1)}, s32[8,4]{1,0:T(8,128)S(1)}, s32[8,4]{1,0:T(8,128)S(1)...) while((s32[]{:T(128)}, f32[136,64,2,128]{3,1,2,0:T(8,128)}, ...), condition=%wide.region_4.5_spmd.clone, body=%wide.region_2.4_spmd.clone.sunk | while | flops 169022480 | bytes 7221497 | solution.py:104
  196.8 2.8 gather_fusion
  205.5 2.8 gather_fusion
  222.8 2.8 gather_fusion
  247.7 15.2 %copy.84 = f32[136,64,2,128]{3,2,1,0:T(2,128)S(1)} copy(f32[136,64,2,128]{3,1,2,0:T(8,128)} %get-tuple-element.62) | data formatting | bytes 17825792 | tf_op jit(solution)/shard_map/while | solution.py:104
  263.7 209.3 %all_to_all.124 = f32[128,64,2,128]{3,2,1,0:T(2,128)} all-to-all(f32[128,64,2,128]{3,2,1,0:T(2,128)S(1)} %slice.33), channel_id=1, replica_groups=mesh['ctx'=128,'head'=4] {'ctx'}, dimensions={0} | all-to-all | bytes 16777216 | tf_op jit(solution)/shard_map/all_to_all | solution.py:110
  473.0 3.7 all-to-all-start.5
  476.7 8.8 %copy.83 = f32[136,64,2,128]{3,0,2,1:T(8,128)S(1)} copy(f32[136,64,2,128]{3,1,2,0:T(8,128)} %get-tuple-element.62) | data formatting | bytes 17825792 | tf_op jit(solution)/shard_map/while | solution.py:104
  485.5 7.7 %fusion.21 = bf16[8,64,2,128]{3,0,2,1:T(8,128)(2,1)S(1)} fusion(f32[128,64,2,128]{3,2,1,0:T(2,128)S(1)} %copy-done, f32[136,64,2,128]{3,0,2,1:T(8,128)S(1)} %copy.83, s32[128]{0:T(128)S(1)} %reduce_max.18), kind=kOutput, calls=%fused_computation.45 | convolution fusion | flops 201589760 | bytes 9175552 | tf_op jit(solution)/shard_map/rl,rbcd->lbcd/dot_general | solution.py:114
  495.2 4.0 all-to-all-start.7
  500.6 4.1 all-to-all-done.7
  504.7 3.3 all-to-all-start.8
  (183 shorter events, 83.5 us)
Async XLA Ops:
  0.6 36.2 %copy-start.1 = (s32[1024,4]{0,1:T(4,128)S(1)}, s32[1024,4]{0,1:T(4,128)}, u32[]{:S(2)}) copy-start(s32[1024,4]{0,1:T(4,128)} %param.16) | copy-start | bytes 49156
  0.6 36.2 %copy-start.2 = (s32[1024,4]{0,1:T(4,128)S(1)}, s32[1024,4]{0,1:T(4,128)}, u32[]{:S(2)}) copy-start(s32[1024,4]{0,1:T(4,128)} %param.17) | copy-start | bytes 49156
  2.2 9.7 %all-to-all-start.1 = ((bf16[128,4,128]{2,0,1:T(8,128)(2,1)}), bf16[128,4,128]{2,0,1:T(8,128)(2,1)S(1)}, u32[]{:S(2)}, u32[]{:S(2)}) async-start(bf16[128,4,128]{2,0,1:T(8,128)(2,1)} %copy.69), calls=%async_computation.1 | async-start | bytes 262144 | tf_op jit(solution)/shard_map/all_to_all | solution.py:74
  11.9 8.1 %all-to-all-start = ((bf16[128,4,128]{2,0,1:T(8,128)(2,1)}), bf16[128,4,128]{2,0,1:T(8,128)(2,1)S(1)}, u32[]{:S(2)}, u32[]{:S(2)}) async-start(bf16[128,4,128]{2,0,1:T(8,128)(2,1)} %copy.68), calls=%async_computation | async-start | bytes 262144 | tf_op jit(solution)/shard_map/all_to_all | solution.py:73
  20.0 13.2 %all-to-all-start.3 = ((bf16[128,32,128]{2,0,1:T(8,128)(2,1)}), bf16[128,32,128]{2,0,1:T(8,128)(2,1)S(1)}, u32[]{:S(2)}, u32[]{:S(2)}) async-start(bf16[128,32,128]{2,0,1:T(8,128)(2,1)} %copy.71), calls=%async_computation.3 | async-start | bytes 2097152 | tf_op jit(solution)/shard_map/all_to_all | solution.py:71
  33.3 13.7 %all-to-all-start.4 = ((bf16[128,32,128]{2,0,1:T(8,128)(2,1)}), bf16[128,32,128]{2,0,1:T(8,128)(2,1)S(1)}, u32[]{:S(2)}, u32[]{:S(2)}) async-start(bf16[128,32,128]{2,0,1:T(8,128)(2,1)} %copy.74), calls=%async_computation.4 | async-start | bytes 2097152 | tf_op jit(solution)/shard_map/all_to_all | solution.py:72
  37.1 35.2 %copy-start.3 = (f32[8,512]{1,0:T(8,128)S(1)}, f32[8,512]{1,0:T(8,128)}, u32[]{:S(2)}) copy-start(f32[8,512]{1,0:T(8,128)} %param.14) | copy-start | bytes 49156
  37.2 35.3 %copy-start.4 = (f32[8,512]{1,0:T(8,128)S(1)}, f32[8,512]{1,0:T(8,128)}, u32[]{:S(2)}) copy-start(f32[8,512]{1,0:T(8,128)} %param.15) | copy-start | bytes 49156
  47.0 120.6 %all-to-all-start.2 = ((bf16[128,64,2,128]{3,1,2,0:T(8,128)(2,1)}), bf16[128,64,2,128]{3,1,2,0:T(8,128)(2,1)}, u32[]{:S(2)}, u32[]{:S(2)}) async-start(bf16[128,64,2,128]{3,1,2,0:T(8,128)(2,1)} %gather_fusion.1), calls=%async_computation.2 | async-start | bytes 8388608 | tf_op jit(solution)/shard_map/all_to_all | solution.py:102
  473.0 22.3 %all-to-all-start.5 = ((bf16[512,8,128]{2,1,0:T(8,128)(2,1)}), bf16[512,8,128]{2,1,0:T(8,128)(2,1)S(1)}, u32[]{:S(2)}, u32[]{:S(2)}) async-start(bf16[512,8,128]{2,1,0:T(8,128)(2,1)} %bitcast.16), calls=%async_computation.5 | async-start | bytes 2097152 | tf_op jit(solution)/shard_map/all_to_all | solution.py:121
  476.7 8.9 %copy-start = (f32[128,64,2,128]{3,2,1,0:T(2,128)S(1)}, f32[128,64,2,128]{3,2,1,0:T(2,128)}, u32[]{:S(2)}) copy-start(f32[128,64,2,128]{3,2,1,0:T(2,128)} %all_to_all.124) | copy-start | bytes 25165828
  495.2 9.5 %all-to-all-start.7 = ((bf16[4,2,8192]{2,1,0:T(2,128)(2,1)}), bf16[4,2,8192]{2,1,0:T(2,128)(2,1)S(1)}, u32[]{:S(2)}, u32[]{:S(2)}) async-start(bf16[4,2,8192]{2,1,0:T(2,128)(2,1)} %reshape.179), calls=%async_computation.7 | async-start | bytes 262144 | tf_op jit(solution)/shard_map/all_to_all | solution.py:122
  504.7 8.1 %all-to-all-start.8 = ((bf16[4,2,8192]{2,1,0:T(2,128)(2,1)}), bf16[4,2,8192]{2,1,0:T(2,128)(2,1)S(1)}, u32[]{:S(2)}, u32[]{:S(2)}) async-start(bf16[4,2,8192]{2,1,0:T(2,128)(2,1)} %reshape.181), calls=%async_computation.8 | async-start | bytes 262144 | tf_op jit(solution)/shard_map/all_to_all | solution.py:123
where the time goes:
time: 523 us; the launch traced here: 514 us
  blocking collectives  209 us (40%)
  waiting for transfers between devices  119 us (23%)
  local copies, waits for them, and re-layouts  85 us (16%)
  starting transfers between devices  51.3 us (10%)
  other arithmetic  27.3 us (5%)
  matrix products  20.5 us (4%)
    all_to_all x1, blocking collectives, shards(): lax.all_to_all(remote_sums, 'ctx', split_axis=0, concat_axis=0, tiled=True)  209 us
    all_to_all x1, waiting for transfers between devices, shards(): lax.all_to_all(outgoing, 'ctx', split_axis=0, concat_axis=0, tiled=True)  92.7 us
    all_to_all x1, starting transfers between devices, shards(): lax.all_to_all(outgoing, 'ctx', split_axis=0, concat_axis=0, tiled=True)  25 us
    while x2, local copies, waits for them, and re-layouts, shards(): lax.scan(partial(block_step, kv_table=kv_table, causal=causal), pair_acc,...  24 us
    gather x8, local copies, waits for them, and re-layouts, block_step(): tile_pair = kv_table[slot_index]  22.7 us
    scatter-add x8, other arithmetic, block_step(): pair_acc.at[slot_index].add(jnp.stack([key_term, value_term], axis=2))  18.2 us
    unnamed x24, local copies, waits for them, and re-layouts  11.7 us
  transfers between devices with their start and end apart: 8, of which 7 were waited for; matrix products, arithmetic and copies ran while one was open for 7% of the time, Pallas kernels for 0%

commit v1 on v0

v1 whole, which is shorter than its diff:
```python
import jax
import jax.numpy as jnp
from jax import lax
from jax.experimental import pallas as pl
from jax.experimental.pallas import tpu as pltpu
from jax.sharding import PartitionSpec as P

BLOCK = 64
WIDTH = 128
AXES = ("ctx", "head")
VMEM_BYTES = 48 * 1024 * 1024


def dot(left, right, contract):
    return lax.dot_general(
        left, right, (contract, ((), ())), preferred_element_type=jnp.float32
    )


def attend(kinds, q_ref, g_ref, own_ref, got_ref, log_ref, delta_ref, dq_ref, down_ref, dprev_ref, dfar_ref):
    group = q_ref.shape[1]
    rows = BLOCK * group
    scale = WIDTH ** (-0.5)
    key_at = lax.broadcasted_iota(jnp.int32, (BLOCK, rows), 0)
    token_at = lax.broadcasted_iota(jnp.int32, (BLOCK, rows), 1) // group
    causal = key_at <= token_at
    terms = []
    for blk in range(2):
        mine = slice(blk * BLOCK, (blk + 1) * BLOCK)
        tables = []
        for kv in range(2):
            before = own_ref[kv, 0, :BLOCK] if blk else got_ref[3, kv, 0]
            tables.append(
                jnp.concatenate(
                    [own_ref[kv, 0, mine], before, got_ref[2, kv, 0], got_ref[blk, kv, 0]], axis=0
                )
            )
        keys, values = tables
        queries = q_ref[mine].reshape(rows, WIDTH)
        grads = g_ref[mine].reshape(rows, WIDTH)
        scores = dot(keys, queries, ((1,), (1,))) * scale
        weights = jnp.exp(scores - log_ref[blk, 0])
        parts = [jnp.where(causal, weights[:BLOCK], 0.0)]
        for slot in range(1, 4):
            live = kinds[blk, slot] > 0
            parts.append(jnp.where(live, weights[slot * BLOCK : (slot + 1) * BLOCK], 0.0))
        weights = jnp.concatenate(parts, axis=0)
        prob_grad = dot(values, grads, ((1,), (1,)))
        dscore = (weights * (prob_grad - delta_ref[blk, 0])).astype(jnp.bfloat16)
        dvalue = dot(weights.astype(jnp.bfloat16), grads, ((1,), (0,)))
        dkey = dot(dscore, queries, ((1,), (0,))) * scale
        dquery = dot(dscore, keys, ((0,), (0,))) * scale
        dq_ref[mine] = dquery.reshape(BLOCK, group, WIDTH).astype(dq_ref.dtype)
        terms.append((dkey, dvalue))
    for kv in range(2):
        first, second = terms[0][kv], terms[1][kv]
        down_ref[kv, 0, :BLOCK] = first[:BLOCK] + second[BLOCK : 2 * BLOCK]
        down_ref[kv, 0, BLOCK:] = second[:BLOCK]
        dprev_ref[kv, 0] = first[BLOCK : 2 * BLOCK]
        dfar_ref[0, kv, 0] = first[3 * BLOCK :]
        dfar_ref[1, kv, 0] = second[3 * BLOCK :]
        dfar_ref[2, kv, 0] = first[2 * BLOCK : 3 * BLOCK] + second[2 * BLOCK : 3 * BLOCK]


def attention(kinds, queries, grads, own, got, logs, deltas):
    tokens, heads, _ = queries.shape
    key_heads = own.shape[1]
    group = heads // key_heads
    token_spec = pl.BlockSpec((tokens, group, WIDTH), lambda k: (0, k, 0))
    own_spec = pl.BlockSpec((2, 1, tokens, WIDTH), lambda k: (0, k, 0, 0))
    got_spec = pl.BlockSpec((4, 2, 1, BLOCK, WIDTH), lambda k: (0, 0, k, 0, 0))
    stat_spec = pl.BlockSpec((2, 1, 1, BLOCK * group), lambda k: (0, k, 0, 0))
    prev_spec = pl.BlockSpec((2, 1, BLOCK, WIDTH), lambda k: (0, k, 0, 0))
    far_spec = pl.BlockSpec((3, 2, 1, BLOCK, WIDTH), lambda k: (0, 0, k, 0, 0))
    return pl.pallas_call(
        attend,
        grid=(key_heads,),
        in_specs=[
            pl.BlockSpec(memory_space=pltpu.SMEM),
            token_spec, token_spec, own_spec, got_spec, stat_spec, stat_spec,
        ],
        out_specs=[token_spec, own_spec, prev_spec, far_spec],
        out_shape=[
            jax.ShapeDtypeStruct(queries.shape, jnp.bfloat16),
            jax.ShapeDtypeStruct(own.shape, jnp.float32),
            jax.ShapeDtypeStruct((2, key_heads, BLOCK, WIDTH), jnp.float32),
            jax.ShapeDtypeStruct((3, 2, key_heads, BLOCK, WIDTH), jnp.float32),
        ],
        compiler_params=pltpu.CompilerParams(vmem_limit_bytes=VMEM_BYTES),
    )(kinds, queries, grads, own, got, logs, deltas)


def add_rows(index_ref, far_ref, hub_ref, out_ref):
    rows = far_ref[...]
    high = rows.astype(jnp.bfloat16)
    rest = rows - high.astype(jnp.float32)
    middle = rest.astype(jnp.bfloat16)
    low = (rest - middle.astype(jnp.float32)).astype(jnp.bfloat16)
    chunk = 256
    hub = jnp.sum(hub_ref[...], axis=0, keepdims=True)
    for start in range(0, out_ref.shape[0], chunk):
        block_at = lax.broadcasted_iota(jnp.int32, (chunk, rows.shape[0]), 0) + start
        chosen = jnp.where(block_at == index_ref[...], 1.0, 0.0).astype(jnp.bfloat16)
        total = sum(dot(chosen, part, ((1,), (0,))) for part in (high, middle, low))
        if start == 0:
            row_at = lax.broadcasted_iota(jnp.int32, total.shape, 0)
            total = total + jnp.where(row_at == 0, hub, 0.0)
        out_ref[start : start + chunk] = total


def scatter_rows(index, far, hub, blocks):
    return pl.pallas_call(
        add_rows,
        out_shape=jax.ShapeDtypeStruct((blocks, WIDTH), jnp.float32),
        compiler_params=pltpu.CompilerParams(vmem_limit_bytes=VMEM_BYTES),
    )(index, far, hub)


def shards(
    queries, key_states, value_states, out_grad, log_sums, row_deltas, block_pairs, pair_kinds
):
    devices = lax.axis_size("ctx") * lax.axis_size("head")
    tokens, key_heads, width = key_states.shape
    heads = queries.shape[1]
    group = heads // key_heads
    blocks = block_pairs.shape[0]
    rank = lax.axis_index("ctx") * lax.axis_size("head") + lax.axis_index("head")
    kinds = lax.dynamic_slice_in_dim(pair_kinds, rank * 2, 2, 0)

    stats = jnp.stack([log_sums, row_deltas])
    stats = lax.all_to_all(stats, "head", split_axis=2, concat_axis=1, tiled=True)
    stats = stats.reshape(2, key_heads, group, 2, BLOCK).transpose(0, 3, 1, 4, 2)
    stats = stats.reshape(2, 2, key_heads, 1, BLOCK * group)

    own = jnp.stack([key_states, value_states]).transpose(0, 2, 1, 3)
    pieces = own.reshape(2, key_heads, 2, BLOCK, width).transpose(0, 1, 3, 2, 4)
    pieces = pieces.reshape(devices, 2, width)
    rows = lax.all_to_all(pieces, AXES, split_axis=0, concat_axis=0, tiled=True)
    rows = rows.reshape(blocks, width)
    far = block_pairs[:, 3].reshape(devices, 2)
    before = jnp.maximum(2 * jnp.arange(devices, dtype=jnp.int32) - 1, 0)
    asked = jnp.stack([far[:, 0], far[:, 1], jnp.zeros_like(before), before], axis=1)
    chosen = (asked.reshape(-1)[:, None] == jnp.arange(blocks, dtype=jnp.int32)[None, :]).astype(
        jnp.bfloat16
    )
    picked = jnp.dot(chosen, rows, preferred_element_type=jnp.float32).astype(jnp.bfloat16)
    picked = picked.reshape(devices, 4, width)
    got = lax.all_to_all(picked, AXES, split_axis=0, concat_axis=0, tiled=True)
    got = got.transpose(1, 0, 2).reshape(4, 2, key_heads, BLOCK, width)

    dquery, down, dprev, dfar = attention(kinds, queries, out_grad, own, got, stats[0], stats[1])

    dprev = lax.ppermute(dprev, AXES, [(d, d - 1) for d in range(1, devices)])
    sent = dfar.reshape(3, devices, width).transpose(1, 0, 2)
    back = lax.all_to_all(sent, AXES, split_axis=0, concat_axis=0, tiled=True)
    sums = scatter_rows(
        block_pairs[:, 3].reshape(1, blocks), back[:, :2].reshape(blocks, width), back[:, 2], blocks
    )
    sums = sums.reshape(devices, 2, width)
    home = lax.all_to_all(sums, AXES, split_axis=0, concat_axis=0, tiled=True)
    home = home.reshape(2, key_heads, BLOCK, 2, width).transpose(0, 1, 3, 2, 4)
    total = down.reshape(home.shape) + home
    total = total.at[:, :, 1].add(dprev)
    total = total.reshape(2, key_heads, tokens, width).transpose(0, 2, 1, 3).astype(jnp.bfloat16)
    return dquery, total[0], total[1]


def solution(mesh):
    tokens = P(("ctx", "head"), None, None)
    stats = P("head", "ctx")
    return jax.shard_map(
        shards,
        mesh=mesh,
        in_specs=(tokens, tokens, tokens, tokens, stats, stats, P(), P()),
        out_specs=(tokens, tokens, tokens),
        check_vma=False,
    )
```

time: 523 us -> 167 us (0.32); the launches traced: 514 us -> 166 us
  blocking collectives: 209 us -> 42.3 us
  local copies, waits for them, and re-layouts: 85 us -> 10 us
  waiting for transfers between devices: 119 us -> 50.9 us
  other arithmetic: 27.3 us -> 1.07 us
  matrix products: 20.5 us -> 2.39 us
  Pallas kernels: 0 us -> 8.27 us
    all_to_all x1, blocking collectives: 209 us -> 42.3 us  [shards(): back = lax.all_to_all(sent, AXES, split_axis=0, concat_axis=0, tiled=True)]
    all_to_all x8 -> x4, waiting for transfers between devices: 119 us -> 50.9 us  [the longest x1 18.9 us: shards(): got = lax.all_to_all(picked, AXES, split_axis=0, concat_axis=0, tiled=True)]
    gather x9 -> x0, local copies, waits for them, and re-layouts: 25.7 us -> none  [the longest x8 22.7 us: block_step(): tile_pair = kv_table[slot_index]]
    while x2 -> x0, local copies, waits for them, and re-layouts: 24 us -> none  [shards(): lax.scan(partial(block_step, kv_table=kv_table, causal=causal), pair_acc,...]
    scatter-add x8 -> x1, other arithmetic: 18.2 us -> 0.06 us  [shards(): total = total.at[:, :, 1].add(dprev)]
    dot_general x41 -> x1, matrix products: 20.5 us -> 2.39 us  [shards(): jnp.dot(chosen, rows, preferred_element_type=jnp.float32)]
    pallas_call x0 -> x2, Pallas kernels: none -> 8.27 us  [the longest x1 5.65 us: attention(): pl.pallas_call(attend, grid=(key_heads,), in_specs=[pl.BlockSpec(memory_s...]
    unnamed x24 -> x15, local copies, waits for them, and re-layouts: 11.7 us -> 3.84 us
  transfers between devices with their start and end apart: 8 -> 5, of which waited for: 7 -> 4; matrix products, arithmetic and copies ran while one was open for 7% -> 5% of each run, Pallas kernels for 0% -> 0%
where the time goes in v1:
time: 167 us; the launch traced here: 166 us
  waiting for transfers between devices  50.9 us (30%)
  starting transfers between devices  50.4 us (30%)
  blocking collectives  42.3 us (25%)
  local copies, waits for them, and re-layouts  10 us (6%)
  Pallas kernels  8.27 us (5%)
  matrix products  2.39 us (1%)
    all_to_all x1, blocking collectives, shards(): back = lax.all_to_all(sent, AXES, split_axis=0, concat_axis=0, tiled=True)  42.3 us
    all_to_all x1, starting transfers between devices, shards(): rows = lax.all_to_all(pieces, AXES, split_axis=0, concat_axis=0, tiled=True)  22.2 us
    all_to_all x1, waiting for transfers between devices, shards(): got = lax.all_to_all(picked, AXES, split_axis=0, concat_axis=0, tiled=True)  18.9 us
    all_to_all x1, waiting for transfers between devices, shards(): home = lax.all_to_all(sums, AXES, split_axis=0, concat_axis=0, tiled=True)  17.2 us
    all_to_all x1, waiting for transfers between devices, shards(): rows = lax.all_to_all(pieces, AXES, split_axis=0, concat_axis=0, tiled=True)  13 us
    all_to_all x1, starting transfers between devices, shards(): got = lax.all_to_all(picked, AXES, split_axis=0, concat_axis=0, tiled=True)  10.9 us
    all_to_all x1, starting transfers between devices, shards(): home = lax.all_to_all(sums, AXES, split_axis=0, concat_axis=0, tiled=True)  9.29 us
    pallas_call x1, Pallas kernels, attention(): pl.pallas_call(attend, grid=(key_heads,), in_specs=[pl.BlockSpec(memory_s...  5.65 us
  transfers between devices with their start and end apart: 5, of which 4 were waited for; matrix products, arithmetic and copies ran while one was open for 5% of the time, Pallas kernels for 0%

profile of v1, /device:TPU:1, one launch (start us, length us, event | category | flops | bytes accessed | tf_op | source)
XLA Modules:
  0.0 166.3 jit_solution(2579284679458074979)
XLA Ops:
  0.6 1.0 copy_bitcast_fusion.1
  1.7 1.0 copy.115
  2.7 22.2 %all-to-all-start = ((bf16[512,2,128]{2,1,0:T(2,128)(2,1)}), bf16[512,2,128]{2,1,0:T(2,128)(2,1)S(1)}, u32[]{:S(2)}, u32[]{:S(2)}) async-start(bf16[512,2,128]{2,1,0:T(2,128)(2,1)} %copy.115), calls=%async_computation | async-start | bytes 524288 | tf_op jit(solution)/shard_map/all_to_all | solution.py:138
  25.1 0.7 slice_bitcast_fusion.2
  26.6 1.4 reshape.123
  28.0 13.0 %all-to-all-done = bf16[512,2,128]{2,1,0:T(2,128)(2,1)S(1)} async-done(((bf16[512,2,128]{2,1,0:T(2,128)(2,1)}), bf16[512,2,128]{2,1,0:T(2,128)(2,1)S(1)}, u32[]{:S(2)}, u32[]{:S(2)}) %all-to-all-start) | async-done | bytes 262176 | tf_op jit(solution)/shard_map/all_to_all | solution.py:138
  41.1 3.3 %all-to-all-start.2 = ((f32[4,1,2048]{2,1,0:T(1,128)}), f32[4,1,2048]{2,1,0:T(1,128)S(1)}, u32[]{:S(2)}, u32[]{:S(2)}) async-start(f32[4,1,2048]{2,1,0:T(1,128)} %reshape.123), calls=%async_computation.2 | async-start | bytes 65536 | tf_op jit(solution)/shard_map/all_to_all | solution.py:131
  44.3 2.4 %fusion.2 = bf16[2048,128]{1,0:T(8,128)(2,1)} fusion(bf16[1024,128]{1,0:T(8,128)(2,1)S(1)} %bitcast.67, s32[2048]{0:T(1024)S(1)} %eq.15), kind=kOutput, calls=%fused_computation.3 | convolution fusion | flops 539230208 | bytes 794624 | tf_op jit(solution)/shard_map/dot_general | solution.py:146
  46.7 1.9 %all-to-all-done.2 = f32[4,1,2048]{2,1,0:T(1,128)S(1)} async-done(((f32[4,1,2048]{2,1,0:T(1,128)}), f32[4,1,2048]{2,1,0:T(1,128)S(1)}, u32[]{:S(2)}, u32[]{:S(2)}) %all-to-all-start.2) | async-done | bytes 32800 | tf_op jit(solution)/shard_map/all_to_all | solution.py:131
  48.6 10.9 %all-to-all-start.1 = ((bf16[512,4,128]{2,1,0:T(4,128)(2,1)}), bf16[512,4,128]{2,1,0:T(4,128)(2,1)S(1)}, u32[]{:S(2)}, u32[]{:S(2)}) async-start(bf16[512,4,128]{2,1,0:T(4,128)(2,1)} %bitcast.7), calls=%async_computation.1 | async-start | bytes 1048576 | tf_op jit(solution)/shard_map/all_to_all | solution.py:148
  59.7 0.5 broadcast.50
  60.3 0.7 reduce.6
  61.0 0.8 reshape.124
  62.8 18.9 %all-to-all-done.1 = bf16[512,4,128]{2,1,0:T(4,128)(2,1)S(1)} async-done(((bf16[512,4,128]{2,1,0:T(4,128)(2,1)}), bf16[512,4,128]{2,1,0:T(4,128)(2,1)S(1)}, u32[]{:S(2)}, u32[]{:S(2)}) %all-to-all-start.1) | async-done | bytes 524320 | tf_op jit(solution)/shard_map/all_to_all | solution.py:148
  81.7 5.6 %shard_map.103 = (bf16[128,32,128]{2,1,0:T(8,128)(2,1)}, f32[2,4,128,128]{3,2,1,0:T(8,128)S(1)}, f32[2,4,64,128]{3,2,1,0:T(8,128)S(1)}, f32[3,2,4,64,128]{4,3,2,1,0:T(8,128)S(1)}) custom-call(s32[2,4]{1,0:T(2,128)S(1)} %copy.130.kinds, bf16[128,32,128]{2,1,0:T(8,128)(2,1)S(1)} %copy-done.1, bf16[128,32,128]{2,1,0:T(8,128)(2,1)S(1)} %copy-done.2, ...), custom_call_target="tpu_custom_call" | custom-call | tf_op jit(solution)/shard_map/pallas_call | solution.py:75
  87.4 0.5 copy.139
  87.9 42.3 %all_to_all.35 = f32[512,3,128]{2,1,0:T(4,128)S(1)} all-to-all(f32[512,3,128]{2,1,0:T(4,128)S(1)} %bitcast.59), channel_id=1, replica_groups=mesh['ctx'=128,'head'=4] {'ctx','head'}, dimensions={0} | all-to-all | bytes 1572864 | tf_op jit(solution)/shard_map/all_to_all | solution.py:155
  130.2 0.3 slice.70
  130.6 2.6 %shard_map.104 = f32[1024,128]{1,0:T(8,128)} custom-call(s32[1,1024]{1,0:T(1,128)S(1)} %get-tuple-element.47.index_ref, f32[1024,128]{1,0:T(8,128)S(1)} %bitcast.54, f32[512,128]{1,0:T(8,128)S(1)} %bitcast.56), custom_call_target="tpu_custom_call" | custom-call | tf_op jit(solution)/shard_map/pallas_call | solution.py:112
  133.3 9.3 %all-to-all-start.4 = ((f32[512,2,128]{2,1,0:T(2,128)}), f32[512,2,128]{2,1,0:T(2,128)S(1)}, u32[]{:S(2)}, u32[]{:S(2)}) async-start(f32[512,2,128]{2,1,0:T(2,128)} %bitcast.21), calls=%async_computation.4 | async-start | bytes 1048576 | tf_op jit(solution)/shard_map/all_to_all | solution.py:160
  142.6 4.8 %collective-permute-start = (f32[2,4,64,128]{3,2,1,0:T(8,128)S(1)}, f32[2,4,64,128]{3,2,1,0:T(8,128)S(1)}, u32[]{:S(2)}, u32[]{:S(2)}) collective-permute-start(f32[2,4,64,128]{3,2,1,0:T(8,128)S(1)} %get-tuple-element.22), channel_id=1, source_target_pairs={{1,0},{2,1},{3,2},{4,3},{5,4},{6,5},{7,6},{8,7},{9,8},{10,9},{11,1... | collective-permute-start | bytes 786440 | tf_op jit(solution)/shard_map/ppermute | solution.py:153
  147.3 17.2 %all-to-all-done.4 = f32[512,2,128]{2,1,0:T(2,128)S(1)} async-done(((f32[512,2,128]{2,1,0:T(2,128)}), f32[512,2,128]{2,1,0:T(2,128)S(1)}, u32[]{:S(2)}, u32[]{:S(2)}) %all-to-all-start.4) | async-done | bytes 524320 | tf_op jit(solution)/shard_map/all_to_all | solution.py:160
  164.8 0.8 copy.129
  165.5 0.8 copy.128
  (38 shorter events, 2.6 us)
Async XLA Ops:
  0.6 58.9 %copy-start = (s32[1024,4]{0,1:T(4,128)S(1)}, s32[1024,4]{0,1:T(4,128)}, u32[]{:S(2)}) copy-start(s32[1024,4]{0,1:T(4,128)} %param.17) | copy-start | bytes 49156
  2.7 23.7 %copy-start.3 = (f32[8,512]{1,0:T(8,128)S(1)}, f32[8,512]{1,0:T(8,128)}, u32[]{:S(2)}) copy-start(f32[8,512]{1,0:T(8,128)} %param.15) | copy-start | bytes 49156
  2.7 23.7 %copy-start.4 = (f32[8,512]{1,0:T(8,128)S(1)}, f32[8,512]{1,0:T(8,128)}, u32[]{:S(2)}) copy-start(f32[8,512]{1,0:T(8,128)} %param.14) | copy-start | bytes 49156
  2.7 38.4 %all-to-all-start = ((bf16[512,2,128]{2,1,0:T(2,128)(2,1)}), bf16[512,2,128]{2,1,0:T(2,128)(2,1)S(1)}, u32[]{:S(2)}, u32[]{:S(2)}) async-start(bf16[512,2,128]{2,1,0:T(2,128)(2,1)} %copy.115), calls=%async_computation | async-start | bytes 524288 | tf_op jit(solution)/shard_map/all_to_all | solution.py:138
  41.1 7.5 %all-to-all-start.2 = ((f32[4,1,2048]{2,1,0:T(1,128)}), f32[4,1,2048]{2,1,0:T(1,128)S(1)}, u32[]{:S(2)}, u32[]{:S(2)}) async-start(f32[4,1,2048]{2,1,0:T(1,128)} %reshape.123), calls=%async_computation.2 | async-start | bytes 65536 | tf_op jit(solution)/shard_map/all_to_all | solution.py:131
  48.6 33.0 %all-to-all-start.1 = ((bf16[512,4,128]{2,1,0:T(4,128)(2,1)}), bf16[512,4,128]{2,1,0:T(4,128)(2,1)S(1)}, u32[]{:S(2)}, u32[]{:S(2)}) async-start(bf16[512,4,128]{2,1,0:T(4,128)(2,1)} %bitcast.7), calls=%async_computation.1 | async-start | bytes 1048576 | tf_op jit(solution)/shard_map/all_to_all | solution.py:148
  62.1 19.6 %copy-start.1 = (bf16[128,32,128]{2,1,0:T(8,128)(2,1)S(1)}, bf16[128,32,128]{2,1,0:T(8,128)(2,1)}, u32[]{:S(2)}) copy-start(bf16[128,32,128]{2,1,0:T(8,128)(2,1)} %q_ref.1) | copy-start | bytes 3145732
  62.1 19.6 %copy-start.2 = (bf16[128,32,128]{2,1,0:T(8,128)(2,1)S(1)}, bf16[128,32,128]{2,1,0:T(8,128)(2,1)}, u32[]{:S(2)}) copy-start(bf16[128,32,128]{2,1,0:T(8,128)(2,1)} %g_ref.1) | copy-start | bytes 3145732
  133.3 31.2 %all-to-all-start.4 = ((f32[512,2,128]{2,1,0:T(2,128)}), f32[512,2,128]{2,1,0:T(2,128)S(1)}, u32[]{:S(2)}, u32[]{:S(2)}) async-start(f32[512,2,128]{2,1,0:T(2,128)} %bitcast.21), calls=%async_computation.4 | async-start | bytes 1048576 | tf_op jit(solution)/shard_map/all_to_all | solution.py:160
  142.6 22.0 %collective-permute-start = (f32[2,4,64,128]{3,2,1,0:T(8,128)S(1)}, f32[2,4,64,128]{3,2,1,0:T(8,128)S(1)}, u32[]{:S(2)}, u32[]{:S(2)}) collective-permute-start(f32[2,4,64,128]{3,2,1,0:T(8,128)S(1)} %get-tuple-element.22), channel_id=1, source_target_pairs={{1,0},{2,1},{3,2},{4,3},{5,4},{6,5},{7,6},{8,7},{9,8},{10,9},{11,1... | collective-permute-start | bytes 786440 | tf_op jit(solution)/shard_map/ppermute | solution.py:153

commit v2 on v1

v2 whole, which is shorter than its diff:
```python
import jax
import jax.numpy as jnp
from jax import lax
from jax.experimental import pallas as pl
from jax.experimental.pallas import tpu as pltpu
from jax.sharding import PartitionSpec as P

BLOCK = 64
WIDTH = 128
AXES = ("ctx", "head")
SPLIT = 4
PAIR = 2
SLOTS = SPLIT * PAIR + 2
HUB, BEFORE = SLOTS - 2, SLOTS - 1
VMEM_BYTES = 20 * 1024 * 1024
SLOW = pl.CostEstimate(flops=20_000_000_000, bytes_accessed=60_000_000, transcendentals=0)


def dot(left, right, contract=((1,), (0,))):
    return lax.dot_general(
        left, right, (contract, ((), ())), preferred_element_type=jnp.float32
    )


def strided(slot, kv):
    return pl.ds(kv * BLOCK * SLOTS + slot, BLOCK, stride=SLOTS)


def pack(head_ref, q_ref, g_ref, k_ref, v_ref, *rest):
    out_refs, pieces_ref, wide_ref = rest[:SPLIT], rest[SPLIT], rest[SPLIT + 1]
    tokens = q_ref.shape[0]
    half = wide_ref.shape[0] // 4
    for kv, ref in enumerate((k_ref, v_ref)):
        wide = ref[...].astype(jnp.float32).reshape(2 * half, WIDTH)
        for blk in range(PAIR):
            start = 2 * kv * half + blk
            wide_ref[pl.ds(start, half, stride=PAIR)] = wide[blk * half : (blk + 1) * half]
    pieces_ref[...] = wide_ref[...].astype(jnp.bfloat16)
    group = q_ref.shape[1] // SPLIT
    rows = tokens * group
    for k in range(SPLIT):
        for to in range(SPLIT):

            @pl.when(lax.rem(head_ref[0] + k, SPLIT) == to)
            def _(k=k, to=to):
                heads = slice(to * group, (to + 1) * group)
                out_refs[k][:rows] = q_ref[:, heads, :].reshape(rows, WIDTH)
                out_refs[k][rows : 2 * rows] = g_ref[:, heads, :].reshape(rows, WIDTH)
                out_refs[k][2 * rows : 2 * rows + tokens] = k_ref[:, to, :]
                out_refs[k][2 * rows + tokens :] = v_ref[:, to, :]


def packed(head, queries, grads, keys, values):
    tokens, heads, width = queries.shape
    part = jax.ShapeDtypeStruct((2 * tokens * (heads // SPLIT + 1), width), jnp.bfloat16)
    both = (2 * tokens * keys.shape[1], width)
    vmem = pl.BlockSpec(memory_space=pltpu.VMEM)
    return pl.pallas_call(
        pack,
        in_specs=[pl.BlockSpec(memory_space=pltpu.SMEM)] + [vmem] * 4,
        out_specs=[vmem] * (SPLIT + 1),
        out_shape=[part] * SPLIT + [jax.ShapeDtypeStruct(both, jnp.bfloat16)],
        scratch_shapes=[pltpu.VMEM(both, jnp.float32)],
        compiler_params=pltpu.CompilerParams(vmem_limit_bytes=VMEM_BYTES),
        cost_estimate=SLOW,
    )(head, queries, grads, keys, values)


def attend(head_ref, kinds, *refs):
    parts, (got_ref, log_ref, delta_ref), (dq_ref, own_ref, sent_ref) = refs[:4], refs[4:7], refs[7:10]
    wide_ref = refs[10]
    wide_ref[...] = got_ref[...].astype(jnp.float32)
    tokens = PAIR * BLOCK
    group = (parts[0].shape[0] - 2 * tokens) // (2 * tokens)
    rows = BLOCK * group
    scale = WIDTH ** (-0.5)
    key_at = lax.broadcasted_iota(jnp.int32, (BLOCK, rows), 0)
    token_at = lax.broadcasted_iota(jnp.int32, (BLOCK, rows), 1) // group
    causal = key_at <= token_at
    table_at = 2 * tokens * group

    def own(sender, kv, blk):
        start = table_at + kv * tokens + blk * BLOCK
        return parts[sender][start : start + BLOCK]

    def got(slot, kv):
        return wide_ref[strided(slot, kv)].astype(jnp.bfloat16)

    owner = [lax.rem(head_ref[0] + SPLIT - k, SPLIT) for k in range(SPLIT)]
    terms = {}
    for k in range(SPLIT):
        for blk in range(PAIR):
            at = owner[k] * PAIR + blk
            tables = []
            for kv in range(2):
                if blk:
                    before = own(k, kv, 0)
                else:
                    before = jnp.where(owner[k] == 0, got(BEFORE, kv), own((k + 1) % SPLIT, kv, 1))
                tables.append(
                    jnp.concatenate([own(k, kv, blk), before, got(HUB, kv), got(at, kv)], axis=0)
                )
            keys, values = tables
            queries = parts[k][blk * rows : (blk + 1) * rows]
            grads = parts[k][tokens * group + blk * rows : tokens * group + (blk + 1) * rows]
            scores = dot(keys, queries, ((1,), (1,))) * scale
            weights = jnp.exp(scores - log_ref[at])
            masked = [jnp.where(causal, weights[:BLOCK], 0.0)]
            for slot in range(1, 4):
                live = kinds[at, slot] > 0
                masked.append(jnp.where(live, weights[slot * BLOCK : (slot + 1) * BLOCK], 0.0))
            weights = jnp.concatenate(masked, axis=0)
            prob_grad = dot(values, grads, ((1,), (1,)))
            dscore = (weights * (prob_grad - delta_ref[at])).astype(jnp.bfloat16)
            dvalue = dot(weights.astype(jnp.bfloat16), grads)
            dkey = dot(dscore, queries) * scale
            dquery = dot(dscore, keys, ((0,), (0,))) * scale
            dq_ref[k, blk * rows : (blk + 1) * rows] = dquery.astype(jnp.bfloat16)
            terms[k, blk] = (dkey, dvalue)
    for kv in range(2):

        def piece(k, blk, slot):
            return terms[k, blk][kv][slot * BLOCK : (slot + 1) * BLOCK]

        hub = 0.0
        outside = 0.0
        for k in range(SPLIT):
            for blk in range(PAIR):
                sent_ref[strided(owner[k] * PAIR + blk, kv)] = piece(k, blk, 3)
                hub = hub + piece(k, blk, 2)
            outside = outside + jnp.where(owner[k] == 0, piece(k, 0, 1), 0.0)
            later = (k + SPLIT - 1) % SPLIT
            own_ref[k, kv, :BLOCK] = piece(k, 0, 0) + piece(k, 1, 1)
            own_ref[k, kv, BLOCK:] = piece(k, 1, 0) + jnp.where(
                owner[later] == 0, 0.0, piece(later, 0, 1)
            )
        sent_ref[strided(HUB, kv)] = hub
        sent_ref[strided(BEFORE, kv)] = outside


def attention(head, kinds, parts, got, logs, deltas):
    tokens = PAIR * BLOCK
    group = (parts[0].shape[0] - 2 * tokens) // (2 * tokens)
    vmem = pl.BlockSpec(memory_space=pltpu.VMEM)
    smem = pl.BlockSpec(memory_space=pltpu.SMEM)
    return pl.pallas_call(
        attend,
        in_specs=[smem, smem] + [vmem] * (SPLIT + 3),
        out_specs=[vmem] * 3,
        out_shape=[
            jax.ShapeDtypeStruct((SPLIT, tokens * group, WIDTH), jnp.bfloat16),
            jax.ShapeDtypeStruct((SPLIT, 2, tokens, WIDTH), jnp.float32),
            jax.ShapeDtypeStruct(got.shape, jnp.float32),
        ],
        scratch_shapes=[pltpu.VMEM(got.shape, jnp.float32)],
        compiler_params=pltpu.CompilerParams(vmem_limit_bytes=VMEM_BYTES),
        cost_estimate=pl.CostEstimate(
            flops=1_400_000_000, bytes_accessed=8_000_000, transcendentals=1_000_000
        ),
    )(head, kinds, *parts, got, logs, deltas)


def pack_back(dq_ref, own_ref, *out_refs):
    rows, tokens = dq_ref.shape[1], own_ref.shape[2]
    for k in range(SPLIT):
        out_refs[k][:rows] = dq_ref[k]
        for kv in range(2):
            total = own_ref[k, kv]
            high = total.astype(jnp.bfloat16)
            low = (total - high.astype(jnp.float32)).astype(jnp.bfloat16)
            start = rows + kv * tokens
            out_refs[k][start : start + tokens] = high
            start = start + 2 * tokens
            out_refs[k][start : start + tokens] = low


def packed_back(dquery, own):
    part = jax.ShapeDtypeStruct((dquery.shape[1] + 4 * own.shape[2], WIDTH), jnp.bfloat16)
    vmem = pl.BlockSpec(memory_space=pltpu.VMEM)
    return pl.pallas_call(
        pack_back,
        in_specs=[vmem] * 2,
        out_specs=[vmem] * SPLIT,
        out_shape=[part] * SPLIT,
        compiler_params=pltpu.CompilerParams(vmem_limit_bytes=VMEM_BYTES),
        cost_estimate=SLOW,
    )(dquery, own)


def unpack(head_ref, *refs):
    parts, (dq_ref, own_ref) = refs[:SPLIT], refs[SPLIT:]
    tokens = dq_ref.shape[0]
    group = dq_ref.shape[1] // SPLIT
    rows = tokens * group
    for k in range(SPLIT):
        for source in range(SPLIT):

            @pl.when(lax.rem(head_ref[0] + k, SPLIT) == source)
            def _(k=k, source=source):
                heads = slice(source * group, (source + 1) * group)
                dq_ref[:, heads, :] = parts[k][:rows].reshape(tokens, group, WIDTH)
                for kv in range(2):
                    start = rows + kv * tokens
                    high = parts[k][start : start + tokens].astype(jnp.float32)
                    start = start + 2 * tokens
                    low = parts[k][start : start + tokens].astype(jnp.float32)
                    own_ref[kv, :, source, :] = high + low


def unpacked(head, parts, queries, keys):
    vmem = pl.BlockSpec(memory_space=pltpu.VMEM)
    return pl.pallas_call(
        unpack,
        in_specs=[pl.BlockSpec(memory_space=pltpu.SMEM)] + [vmem] * SPLIT,
        out_specs=[vmem] * 2,
        out_shape=[
            jax.ShapeDtypeStruct(queries.shape, jnp.bfloat16),
            jax.ShapeDtypeStruct((2,) + keys.shape, jnp.float32),
        ],
        compiler_params=pltpu.CompilerParams(vmem_limit_bytes=VMEM_BYTES),
        cost_estimate=SLOW,
    )(head, *parts)


def finish(home_ref, own_ref, *out_refs):
    rows = own_ref.shape[0] // 2
    half = rows // PAIR
    for kv in range(2):
        for blk in range(PAIR):
            start = blk * half
            total = home_ref[pl.ds(kv * rows + blk, half, stride=PAIR)]
            total = total + own_ref[kv * rows + start : kv * rows + start + half]
            out_refs[kv][start : start + half] = total.astype(jnp.bfloat16)


def finished(home, own):
    out = jax.ShapeDtypeStruct((own.shape[0] // 2, WIDTH), jnp.bfloat16)
    return pl.pallas_call(
        finish,
        out_shape=[out] * 2,
        compiler_params=pltpu.CompilerParams(vmem_limit_bytes=VMEM_BYTES),
    )(home, own)


def pick_rows(index_ref, rows_ref, out_ref):
    blocks = rows_ref.shape[0]
    chunk = 256
    block_at = lax.broadcasted_iota(jnp.int32, (chunk, blocks), 1)
    rows = rows_ref[...]
    for start in range(0, out_ref.shape[0], chunk):
        here = slice(start, start + chunk)
        chosen = jnp.where(block_at == index_ref[here], 1.0, 0.0).astype(jnp.bfloat16)
        out_ref[here] = dot(chosen, rows).astype(jnp.bfloat16)


def gather_rows(index, rows):
    return pl.pallas_call(
        pick_rows,
        out_shape=jax.ShapeDtypeStruct((index.shape[0], WIDTH), jnp.bfloat16),
        compiler_params=pltpu.CompilerParams(vmem_limit_bytes=VMEM_BYTES),
    )(index, rows)


def add_rows(index_ref, rows_ref, out_ref):
    rows = rows_ref[...]
    high = rows.astype(jnp.bfloat16)
    rest = rows - high.astype(jnp.float32)
    middle = rest.astype(jnp.bfloat16)
    low = (rest - middle.astype(jnp.float32)).astype(jnp.bfloat16)
    chunk = 256
    for start in range(0, out_ref.shape[0], chunk):
        block_at = lax.broadcasted_iota(jnp.int32, (chunk, rows.shape[0]), 0) + start
        chosen = jnp.where(block_at == index_ref[...], 1.0, 0.0).astype(jnp.bfloat16)
        out_ref[start : start + chunk] = dot(chosen, high) + dot(chosen, middle) + dot(chosen, low)


def scatter_rows(index, rows, blocks):
    return pl.pallas_call(
        add_rows,
        out_shape=jax.ShapeDtypeStruct((blocks, WIDTH), jnp.float32),
        compiler_params=pltpu.CompilerParams(vmem_limit_bytes=VMEM_BYTES),
    )(index, rows)


def shards(
    queries, key_states, value_states, out_grad, log_sums, row_deltas, block_pairs, pair_kinds
):
    shard_count = lax.axis_size("ctx")
    devices = shard_count * SPLIT
    tokens, key_heads, width = key_states.shape
    heads = queries.shape[1]
    group = heads // key_heads
    blocks = block_pairs.shape[0]
    here = SPLIT * PAIR
    rank, head = lax.axis_index("ctx"), lax.axis_index("head")
    head_at = head.reshape(1)
    wire = (shard_count, SLOTS // 2, 2, width)

    def exchange(array, axes):
        return lax.all_to_all(array, axes, split_axis=0, concat_axis=0, tiled=True)

    *parts, pieces = packed(head_at, queries, out_grad, key_states, value_states)
    rows = exchange(pieces.reshape(devices, PAIR, width), AXES).reshape(blocks, width)

    far = block_pairs[:, 3].reshape(shard_count, here)
    before = jnp.maximum(here * jnp.arange(shard_count, dtype=jnp.int32) - 1, 0)
    index = jnp.concatenate([far, jnp.zeros_like(before)[:, None], before[:, None]], axis=1)
    kinds = lax.dynamic_slice_in_dim(pair_kinds, rank * here, here, 0)
    stats = jnp.stack([log_sums, row_deltas]).transpose(0, 2, 1)
    stats = stats.reshape(2, here, 1, BLOCK * group)
    index, kinds, logs, deltas = lax.optimization_barrier((index, kinds, stats[0], stats[1]))
    got = exchange(gather_rows(index.reshape(-1, 1), rows).reshape(wire), "ctx")

    for k in (2, 1, 3):
        if k == 1:
            parts = list(lax.optimization_barrier(parts))
        parts[k] = lax.ppermute(parts[k], "head", [(i, (i + k) % SPLIT) for i in range(SPLIT)])
    dquery, own, sent = attention(head_at, kinds, parts, got.reshape(-1, width), logs, deltas)

    back = exchange(sent.reshape(wire), "ctx")
    sums = scatter_rows(index.reshape(1, -1), back.reshape(-1, width), blocks)
    home = exchange(sums.reshape(devices, PAIR, width), AXES)

    parts = list(packed_back(dquery, own))
    for k in range(1, SPLIT):
        parts[k] = lax.ppermute(parts[k], "head", [(i, (i - k) % SPLIT) for i in range(SPLIT)])
    dquery, own = unpacked(head_at, parts, queries, key_states)

    dkey, dvalue = finished(home.reshape(-1, width), own.reshape(-1, width))
    return dquery, dkey.reshape(key_states.shape), dvalue.reshape(key_states.shape)


def solution(mesh):
    tokens = P(("ctx", "head"), None, None)
    stats = P("head", "ctx")
    return jax.shard_map(
        shards,
        mesh=mesh,
        in_specs=(tokens, tokens, tokens, tokens, stats, stats, P(), P()),
        out_specs=(tokens, tokens, tokens),
        check_vma=False,
    )
```

time: 167 us -> 156 us (0.934)
  blocking collectives: 42.3 us -> 0 us
  starting transfers between devices: 50.4 us -> 77.2 us
  Pallas kernels: 8.27 us -> 14 us
  local copies, waits for them, and re-layouts: 10 us -> 13.7 us
  matrix products: 2.39 us -> 0 us
    all_to_all x1 -> x0, blocking collectives: 42.3 us -> none  [shards(): back = lax.all_to_all(sent, AXES, split_axis=0, concat_axis=0, tiled=True)]
    ppermute x1 -> x6, starting transfers between devices: 4.75 us -> 21.3 us  [the longest x3 11.5 us: shards(): lax.ppermute(parts[k], 'head', [(i, (i + k) % SPLIT) for i in range(SPLIT)])]
    all_to_all x4, starting transfers between devices: 45.7 us -> 55.9 us  [exchange(): return lax.all_to_all(array, axes, split_axis=0, concat_axis=0, tiled=True)]
    unnamed x15 -> x30, local copies, waits for them, and re-layouts: 3.84 us -> 11.5 us
    pallas_call x1 -> x6, Pallas kernels: 5.65 us -> 11 us  [the longest x1 4.96 us: attention(): pl.pallas_call(attend, in_specs=[smem, smem] + [vmem] * (SPLIT + 3), out_...]
    all_to_all x4, waiting for transfers between devices: 50.9 us -> 47 us  [exchange(): return lax.all_to_all(array, axes, split_axis=0, concat_axis=0, tiled=True)]
    ppermute x1 -> x6, waiting for transfers between devices: 0.01 us -> 2.41 us  [the longest x3 2.4 us: shards(): lax.ppermute(parts[k], 'head', [(i, (i + k) % SPLIT) for i in range(SPLIT)])]
    dot_general x1 -> x0, matrix products: 2.39 us -> none  [shards(): jnp.dot(chosen, rows, preferred_element_type=jnp.float32)]
  transfers between devices with their start and end apart: 5 -> 10, of which waited for: 4 -> 6; matrix products, arithmetic and copies ran while one was open for 5% -> 1% of each run, Pallas kernels for 0% -> 4%
where the time goes in v2:
time: 156 us; the launch traced here: 155 us
  starting transfers between devices  77.2 us (49%)
  waiting for transfers between devices  49.5 us (32%)
  Pallas kernels  14 us (9%)
  local copies, waits for them, and re-layouts  13.7 us (9%)
    all_to_all x4, starting transfers between devices, exchange(): return lax.all_to_all(array, axes, split_axis=0, concat_axis=0, tiled=True)  55.9 us
    all_to_all x4, waiting for transfers between devices, exchange(): return lax.all_to_all(array, axes, split_axis=0, concat_axis=0, tiled=True)  47 us
    unnamed x30, local copies, waits for them, and re-layouts  11.5 us
    ppermute x3, starting transfers between devices, shards(): lax.ppermute(parts[k], 'head', [(i, (i + k) % SPLIT) for i in range(SPLIT)])  11.5 us
    ppermute x3, starting transfers between devices, shards(): lax.ppermute(parts[k], 'head', [(i, (i - k) % SPLIT) for i in range(SPLIT)])  9.81 us
    pallas_call x1, Pallas kernels, attention(): pl.pallas_call(attend, in_specs=[smem, smem] + [vmem] * (SPLIT + 3), out_...  4.96 us
  transfers between devices with their start and end apart: 10, of which 6 were waited for; matrix products, arithmetic and copies ran while one was open for 1% of the time, Pallas kernels for 4%

profile of v2, /device:TPU:1, one launch (start us, length us, event | category | flops | bytes accessed | tf_op | source)
XLA Modules:
  0.0 155.2 jit_solution(11870360924852779590)
XLA Ops:
  0.7 1.2 copy-done.1
  1.9 1.2 copy-done.2
  4.9 1.9 %shard_map.103 = (bf16[2304,128]{1,0:T(8,128)(2,1)S(1)}, bf16[2304,128]{1,0:T(8,128)(2,1)S(1)}, bf16[2304,128]{1,0:T(8,128)(2,1)S(1)}, bf16[2304,128]{1,0:T(8,128)(2,1)S(1)}, bf16[1024,128]{1,0:T(8,128)(2,1)}) custom-call(s32[1]{0:T(128)} %bitcast.head_ref, bf16[128,32,128]{2,1,0:T(8,128)(2,1)S(1)} %copy-done.1, bf16[128,32,128]{2,1,0:T(8,128)(2,1)S(1)} %copy-done.2, ...), custom_call_target="tpu_custom_call" | custom-call | flops 20000000000 | bytes 60000000 | tf_op jit(solution)/shard_map/pallas_call | solution.py:58
  7.7 22.2 %all-to-all-start = ((bf16[512,2,128]{2,1,0:T(2,128)(2,1)}), bf16[512,2,128]{2,1,0:T(2,128)(2,1)S(1)}, u32[]{:S(2)}, u32[]{:S(2)}) async-start(bf16[512,2,128]{2,1,0:T(2,128)(2,1)} %bitcast.4), calls=%async_computation | async-start | bytes 524288 | tf_op jit(solution)/shard_map/all_to_all | solution.py:300
  29.8 4.8 %collective-permute-start = (bf16[2304,128]{1,0:T(8,128)(2,1)S(1)}, bf16[2304,128]{1,0:T(8,128)(2,1)S(1)}, u32[]{:S(2)}, u32[]{:S(2)}) collective-permute-start(bf16[2304,128]{1,0:T(8,128)(2,1)S(1)} %get-tuple-element.30), channel_id=1, source_target_pairs={{0,2},{1,3},{2,0},{3,1},{4,6},{5,7},{6,4},{7,5},{8,10},{9,11},{10,... | collective-permute-start | bytes 1769480 | tf_op jit(solution)/shard_map/ppermute | solution.py:317
  37.3 8.7 %all-to-all-done = bf16[512,2,128]{2,1,0:T(2,128)(2,1)S(1)} async-done(((bf16[512,2,128]{2,1,0:T(2,128)(2,1)}), bf16[512,2,128]{2,1,0:T(2,128)(2,1)S(1)}, u32[]{:S(2)}, u32[]{:S(2)}) %all-to-all-start) | async-done | bytes 262176 | tf_op jit(solution)/shard_map/all_to_all | solution.py:300
  46.1 1.6 %shard_map.104 = bf16[1280,128]{1,0:T(8,128)(2,1)} custom-call(s32[1280,1]{1,0:T(8,128)S(1)} %reshape.80.index_ref, bf16[1024,128]{1,0:T(8,128)(2,1)S(1)} %bitcast.18), custom_call_target="tpu_custom_call" | custom-call | tf_op jit(solution)/shard_map/pallas_call | solution.py:257
  47.7 7.1 %all-to-all-start.1 = ((bf16[128,5,2,128]{3,2,1,0:T(2,128)(2,1)}), bf16[128,5,2,128]{3,2,1,0:T(2,128)(2,1)S(1)}, u32[]{:S(2)}, u32[]{:S(2)}) async-start(bf16[128,5,2,128]{3,2,1,0:T(2,128)(2,1)} %bitcast.6), calls=%async_computation.1 | async-start | bytes 655360 | tf_op jit(solution)/shard_map/all_to_all | solution.py:300
  54.8 2.2 %collective-permute-start.1 = (bf16[2304,128]{1,0:T(8,128)(2,1)S(1)}, bf16[2304,128]{1,0:T(8,128)(2,1)S(1)}, u32[]{:S(2)}, u32[]{:S(2)}) collective-permute-start(bf16[2304,128]{1,0:T(8,128)(2,1)S(1)} %get-tuple-element.33), channel_id=1, source_target_pairs={{0,1},{1,2},{2,3},{3,0},{4,5},{5,6},{6,7},{7,4},{8,9},{9,10},{10,1... | collective-permute-start | bytes 1769480 | tf_op jit(solution)/shard_map/ppermute | solution.py:317
  57.0 4.5 %collective-permute-start.2 = (bf16[2304,128]{1,0:T(8,128)(2,1)S(1)}, bf16[2304,128]{1,0:T(8,128)(2,1)}, u32[]{:S(2)}, u32[]{:S(2)}) collective-permute-start(bf16[2304,128]{1,0:T(8,128)(2,1)S(1)} %get-tuple-element.35), channel_id=1, source_target_pairs={{0,3},{1,0},{2,1},{3,2},{4,7},{5,4},{6,5},{7,6},{8,11},{9,8},{10,9... | collective-permute-start | bytes 1769480 | tf_op jit(solution)/shard_map/ppermute | solution.py:317
  61.5 8.8 %all-to-all-done.1 = bf16[128,5,2,128]{3,2,1,0:T(2,128)(2,1)S(1)} async-done(((bf16[128,5,2,128]{3,2,1,0:T(2,128)(2,1)}), bf16[128,5,2,128]{3,2,1,0:T(2,128)(2,1)S(1)}, u32[]{:S(2)}, u32[]{:S(2)}) %all-to-all-start.1) | async-done | bytes 327712 | tf_op jit(solution)/shard_map/all_to_all | solution.py:300
  70.3 1.5 collective-permute-done.1.refs_1_
  72.7 1.1 copy-done.8
  73.8 5.0 %shard_map.105 = (bf16[4,1024,128]{2,1,0:T(8,128)(2,1)S(1)}, f32[4,2,128,128]{3,2,1,0:T(8,128)S(1)}, f32[1280,128]{1,0:T(8,128)}) custom-call(s32[1]{0:T(128)} %bitcast.head_ref, s32[8,4]{1,0:T(8,128)S(1)} %copy.29.kinds, bf16[2304,128]{1,0:T(8,128)(2,1)S(1)} %copy-done.8, bf16[2304,128]{1,0:T(8,128)(2,1)S(1)} %collective-permute-done.1.refs_1_, ...), custom_call_target="tpu_custom_call" | custom-call | flops 1400000000 | bytes 8000000 | tf_op jit(solution)/shard_map/pallas_call | solution.py:146
  80.5 15.6 %all-to-all-start.2 = ((f32[128,5,2,128]{3,2,1,0:T(2,128)}), f32[128,5,2,128]{3,2,1,0:T(2,128)S(1)}, u32[]{:S(2)}, u32[]{:S(2)}) async-start(f32[128,5,2,128]{3,2,1,0:T(2,128)} %bitcast.8), calls=%async_computation.2 | async-start | bytes 1310720 | tf_op jit(solution)/shard_map/all_to_all | solution.py:300
  96.1 1.2 copy-done.6
  98.2 5.4 %collective-permute-start.3 = (bf16[1536,128]{1,0:T(8,128)(2,1)S(1)}, bf16[1536,128]{1,0:T(8,128)(2,1)S(1)}, u32[]{:S(2)}, u32[]{:S(2)}) collective-permute-start(bf16[1536,128]{1,0:T(8,128)(2,1)S(1)} %get-tuple-element.43), channel_id=1, source_target_pairs={{0,3},{1,0},{2,1},{3,2},{4,7},{5,4},{6,5},{7,6},{8,11},{9,8},{10,9... | collective-permute-start | bytes 1179656 | tf_op jit(solution)/shard_map/ppermute | solution.py:326
  103.6 1.9 %collective-permute-start.4 = (bf16[1536,128]{1,0:T(8,128)(2,1)S(1)}, bf16[1536,128]{1,0:T(8,128)(2,1)S(1)}, u32[]{:S(2)}, u32[]{:S(2)}) collective-permute-start(bf16[1536,128]{1,0:T(8,128)(2,1)S(1)} %get-tuple-element.44), channel_id=1, source_target_pairs={{0,2},{1,3},{2,0},{3,1},{4,6},{5,7},{6,4},{7,5},{8,10},{9,11},{10,... | collective-permute-start | bytes 1179656 | tf_op jit(solution)/shard_map/ppermute | solution.py:326
  105.6 2.5 %collective-permute-start.5 = (bf16[1536,128]{1,0:T(8,128)(2,1)S(1)}, bf16[1536,128]{1,0:T(8,128)(2,1)S(1)}, u32[]{:S(2)}, u32[]{:S(2)}) collective-permute-start(bf16[1536,128]{1,0:T(8,128)(2,1)S(1)} %get-tuple-element.45), channel_id=1, source_target_pairs={{0,1},{1,2},{2,3},{3,0},{4,5},{5,6},{6,7},{7,4},{8,9},{9,10},{10,1... | collective-permute-start | bytes 1179656 | tf_op jit(solution)/shard_map/ppermute | solution.py:326
  108.2 10.3 %all-to-all-done.2 = f32[128,5,2,128]{3,2,1,0:T(2,128)S(1)} async-done(((f32[128,5,2,128]{3,2,1,0:T(2,128)}), f32[128,5,2,128]{3,2,1,0:T(2,128)S(1)}, u32[]{:S(2)}, u32[]{:S(2)}) %all-to-all-start.2) | async-done | bytes 655392 | tf_op jit(solution)/shard_map/all_to_all | solution.py:300
  118.5 3.0 %shard_map.108 = f32[1024,128]{1,0:T(8,128)} custom-call(s32[1,1280]{1,0:T(1,128)S(1)} %reshape.72.index_ref, f32[1280,128]{1,0:T(8,128)S(1)} %bitcast.16), custom_call_target="tpu_custom_call" | custom-call | tf_op jit(solution)/shard_map/pallas_call | solution.py:278
  121.5 11.1 %all-to-all-start.3 = ((f32[512,2,128]{2,1,0:T(2,128)}), f32[512,2,128]{2,1,0:T(2,128)S(1)}, u32[]{:S(2)}, u32[]{:S(2)}) async-start(f32[512,2,128]{2,1,0:T(2,128)} %bitcast.10), calls=%async_computation.3 | async-start | bytes 1048576 | tf_op jit(solution)/shard_map/all_to_all | solution.py:300
  133.6 1.6 %shard_map.107 = (bf16[128,32,128]{2,1,0:T(8,128)(2,1)}, f32[2,128,4,128]{3,2,1,0:T(4,128)S(1)}) custom-call(s32[1]{0:T(128)} %bitcast.head_ref, bf16[1536,128]{1,0:T(8,128)(2,1)S(1)} %copy-done.12, bf16[1536,128]{1,0:T(8,128)(2,1)S(1)} %collective-permute-done.3.refs_1_, bf16[1536,128]{1,0:T(8,128)(2,1)S(1)} %collective-permute-done.4.refs_2_, ...), custom_call_target="tpu_custom_call" | custom-call | flops 20000000000 | bytes 60000000 | tf_op jit(solution)/shard_map/pallas_call | solution.py:212
  135.2 19.3 %all-to-all-done.3 = f32[512,2,128]{2,1,0:T(2,128)S(1)} async-done(((f32[512,2,128]{2,1,0:T(2,128)}), f32[512,2,128]{2,1,0:T(2,128)S(1)}, u32[]{:S(2)}, u32[]{:S(2)}) %all-to-all-start.3) | async-done | bytes 524320 | tf_op jit(solution)/shard_map/all_to_all | solution.py:300
  (52 shorter events, 10.7 us)
Async XLA Ops:
  0.6 34.0 %copy-start = (s32[1024,4]{0,1:T(4,128)S(1)}, s32[1024,4]{0,1:T(4,128)}, u32[]{:S(2)}) copy-start(s32[1024,4]{0,1:T(4,128)} %param.15) | copy-start | bytes 49156
  0.7 1.2 copy-start.1
  1.9 1.2 copy-start.2
  3.1 0.9 copy-start.3
  4.0 0.9 copy-start.4
  6.8 0.8 copy-start.7
  7.7 38.4 %all-to-all-start = ((bf16[512,2,128]{2,1,0:T(2,128)(2,1)}), bf16[512,2,128]{2,1,0:T(2,128)(2,1)S(1)}, u32[]{:S(2)}, u32[]{:S(2)}) async-start(bf16[512,2,128]{2,1,0:T(2,128)(2,1)} %bitcast.4), calls=%async_computation | async-start | bytes 524288 | tf_op jit(solution)/shard_map/all_to_all | solution.py:300
  29.8 24.9 %collective-permute-start = (bf16[2304,128]{1,0:T(8,128)(2,1)S(1)}, bf16[2304,128]{1,0:T(8,128)(2,1)S(1)}, u32[]{:S(2)}, u32[]{:S(2)}) collective-permute-start(bf16[2304,128]{1,0:T(8,128)(2,1)S(1)} %get-tuple-element.30), channel_id=1, source_target_pairs={{0,2},{1,3},{2,0},{3,1},{4,6},{5,7},{6,4},{7,5},{8,10},{9,11},{10,... | collective-permute-start | bytes 1769480 | tf_op jit(solution)/shard_map/ppermute | solution.py:317
  35.6 0.7 copy-start.14
  47.7 22.6 %all-to-all-start.1 = ((bf16[128,5,2,128]{3,2,1,0:T(2,128)(2,1)}), bf16[128,5,2,128]{3,2,1,0:T(2,128)(2,1)S(1)}, u32[]{:S(2)}, u32[]{:S(2)}) async-start(bf16[128,5,2,128]{3,2,1,0:T(2,128)(2,1)} %bitcast.6), calls=%async_computation.1 | async-start | bytes 655360 | tf_op jit(solution)/shard_map/all_to_all | solution.py:300
  54.8 17.0 %collective-permute-start.1 = (bf16[2304,128]{1,0:T(8,128)(2,1)S(1)}, bf16[2304,128]{1,0:T(8,128)(2,1)S(1)}, u32[]{:S(2)}, u32[]{:S(2)}) collective-permute-start(bf16[2304,128]{1,0:T(8,128)(2,1)S(1)} %get-tuple-element.33), channel_id=1, source_target_pairs={{0,1},{1,2},{2,3},{3,0},{4,5},{5,6},{6,7},{7,4},{8,9},{9,10},{10,1... | collective-permute-start | bytes 1769480 | tf_op jit(solution)/shard_map/ppermute | solution.py:317
  57.0 15.7 %collective-permute-start.2 = (bf16[2304,128]{1,0:T(8,128)(2,1)S(1)}, bf16[2304,128]{1,0:T(8,128)(2,1)}, u32[]{:S(2)}, u32[]{:S(2)}) collective-permute-start(bf16[2304,128]{1,0:T(8,128)(2,1)S(1)} %get-tuple-element.35), channel_id=1, source_target_pairs={{0,3},{1,0},{2,1},{3,2},{4,7},{5,4},{6,5},{7,6},{8,11},{9,8},{10,9... | collective-permute-start | bytes 1769480 | tf_op jit(solution)/shard_map/ppermute | solution.py:317
  72.7 1.1 copy-start.8
  78.7 1.0 copy-start.5
  79.7 0.8 copy-start.9
  80.5 15.6 %copy-start.10 = (f32[4,2,128,128]{3,2,1,0:T(8,128)S(1)}, f32[4,2,128,128]{3,2,1,0:T(8,128)}, u32[]{:S(2)}) copy-start(f32[4,2,128,128]{3,2,1,0:T(8,128)} %copy-done.9) | copy-start | bytes 1572868
  80.5 37.9 %all-to-all-start.2 = ((f32[128,5,2,128]{3,2,1,0:T(2,128)}), f32[128,5,2,128]{3,2,1,0:T(2,128)S(1)}, u32[]{:S(2)}, u32[]{:S(2)}) async-start(f32[128,5,2,128]{3,2,1,0:T(2,128)} %bitcast.8), calls=%async_computation.2 | async-start | bytes 1310720 | tf_op jit(solution)/shard_map/all_to_all | solution.py:300
  96.1 1.2 copy-start.6
  97.5 0.7 copy-start.11
  98.2 34.3 %collective-permute-start.3 = (bf16[1536,128]{1,0:T(8,128)(2,1)S(1)}, bf16[1536,128]{1,0:T(8,128)(2,1)S(1)}, u32[]{:S(2)}, u32[]{:S(2)}) collective-permute-start(bf16[1536,128]{1,0:T(8,128)(2,1)S(1)} %get-tuple-element.43), channel_id=1, source_target_pairs={{0,3},{1,0},{2,1},{3,2},{4,7},{5,4},{6,5},{7,6},{8,11},{9,8},{10,9... | collective-permute-start | bytes 1179656 | tf_op jit(solution)/shard_map/ppermute | solution.py:326
  103.6 28.9 %collective-permute-start.4 = (bf16[1536,128]{1,0:T(8,128)(2,1)S(1)}, bf16[1536,128]{1,0:T(8,128)(2,1)S(1)}, u32[]{:S(2)}, u32[]{:S(2)}) collective-permute-start(bf16[1536,128]{1,0:T(8,128)(2,1)S(1)} %get-tuple-element.44), channel_id=1, source_target_pairs={{0,2},{1,3},{2,0},{3,1},{4,6},{5,7},{6,4},{7,5},{8,10},{9,11},{10,... | collective-permute-start | bytes 1179656 | tf_op jit(solution)/shard_map/ppermute | solution.py:326
  105.6 27.0 %collective-permute-start.5 = (bf16[1536,128]{1,0:T(8,128)(2,1)S(1)}, bf16[1536,128]{1,0:T(8,128)(2,1)S(1)}, u32[]{:S(2)}, u32[]{:S(2)}) collective-permute-start(bf16[1536,128]{1,0:T(8,128)(2,1)S(1)} %get-tuple-element.45), channel_id=1, source_target_pairs={{0,1},{1,2},{2,3},{3,0},{4,5},{5,6},{6,7},{7,4},{8,9},{9,10},{10,1... | collective-permute-start | bytes 1179656 | tf_op jit(solution)/shard_map/ppermute | solution.py:326
  121.5 33.0 %all-to-all-start.3 = ((f32[512,2,128]{2,1,0:T(2,128)}), f32[512,2,128]{2,1,0:T(2,128)S(1)}, u32[]{:S(2)}, u32[]{:S(2)}) async-start(f32[512,2,128]{2,1,0:T(2,128)} %bitcast.10), calls=%async_computation.3 | async-start | bytes 1048576 | tf_op jit(solution)/shard_map/all_to_all | solution.py:300
  132.6 1.0 copy-start.12
  (1 other events, 0.7 us)

commit v3 on v2

--- a/solution.py
+++ b/solution.py
@@ -1,3 +1,5 @@
+import functools
+
 import jax
 import jax.numpy as jnp
 from jax import lax
@@ -26,41 +28,50 @@
     return pl.ds(kv * BLOCK * SLOTS + slot, BLOCK, stride=SLOTS)
 
 
-def pack(head_ref, q_ref, g_ref, k_ref, v_ref, *rest):
-    out_refs, pieces_ref, wide_ref = rest[:SPLIT], rest[SPLIT], rest[SPLIT + 1]
-    tokens = q_ref.shape[0]
+def interleave(k_ref, v_ref, pieces_ref, wide_ref):
     half = wide_ref.shape[0] // 4
     for kv, ref in enumerate((k_ref, v_ref)):
-        wide = ref[...].astype(jnp.float32).reshape(2 * half, WIDTH)
+        wide = ref[...].astype(jnp.float32)
         for blk in range(PAIR):
             start = 2 * kv * half + blk
             wide_ref[pl.ds(start, half, stride=PAIR)] = wide[blk * half : (blk + 1) * half]
     pieces_ref[...] = wide_ref[...].astype(jnp.bfloat16)
+
+
+def interleaved(keys, values):
+    both = (2 * keys.shape[0], WIDTH)
+    return pl.pallas_call(
+        interleave,
+        out_shape=jax.ShapeDtypeStruct(both, jnp.bfloat16),
+        scratch_shapes=[pltpu.VMEM(both, jnp.float32)],
+        compiler_params=pltpu.CompilerParams(vmem_limit_bytes=VMEM_BYTES),
+    )(keys, values)
+
+
+def pack(steps, head_ref, q_ref, g_ref, k_ref, v_ref, *out_refs):
+    tokens = q_ref.shape[0]
     group = q_ref.shape[1] // SPLIT
     rows = tokens * group
-    for k in range(SPLIT):
+    for out_ref, k in zip(out_refs, steps):
         for to in range(SPLIT):
 
             @pl.when(lax.rem(head_ref[0] + k, SPLIT) == to)
-            def _(k=k, to=to):
+            def _(out_ref=out_ref, to=to):
                 heads = slice(to * group, (to + 1) * group)
-                out_refs[k][:rows] = q_ref[:, heads, :].reshape(rows, WIDTH)
-                out_refs[k][rows : 2 * rows] = g_ref[:, heads, :].reshape(rows, WIDTH)
-                out_refs[k][2 * rows : 2 * rows + tokens] = k_ref[:, to, :]
-                out_refs[k][2 * rows + tokens :] = v_ref[:, to, :]
-
-
-def packed(head, queries, grads, keys, values):
+                out_ref[:rows] = q_ref[:, heads, :].reshape(rows, WIDTH)
+                out_ref[rows : 2 * rows] = g_ref[:, heads, :].reshape(rows, WIDTH)
+                out_ref[2 * rows : 2 * rows + tokens] = k_ref[:, to, :]
+                out_ref[2 * rows + tokens :] = v_ref[:, to, :]
+
+
+def packed(steps, head, queries, grads, keys, values):
     tokens, heads, width = queries.shape
     part = jax.ShapeDtypeStruct((2 * tokens * (heads // SPLIT + 1), width), jnp.bfloat16)
-    both = (2 * tokens * keys.shape[1], width)
-    vmem = pl.BlockSpec(memory_space=pltpu.VMEM)
-    return pl.pallas_call(
-        pack,
-        in_specs=[pl.BlockSpec(memory_space=pltpu.SMEM)] + [vmem] * 4,
-        out_specs=[vmem] * (SPLIT + 1),
-        out_shape=[part] * SPLIT + [jax.ShapeDtypeStruct(both, jnp.bfloat16)],
-        scratch_shapes=[pltpu.VMEM(both, jnp.float32)],
+    return pl.pallas_call(
+        functools.partial(pack, steps),
+        in_specs=[pl.BlockSpec(memory_space=pltpu.SMEM)] + [pl.BlockSpec()] * 4,
+        out_specs=[pl.BlockSpec()] * len(steps),
+        out_shape=[part] * len(steps),
         compiler_params=pltpu.CompilerParams(vmem_limit_bytes=VMEM_BYTES),
         cost_estimate=SLOW,
     )(head, queries, grads, keys, values)
@@ -258,6 +269,7 @@
         pick_rows,
         out_shape=jax.ShapeDtypeStruct((index.shape[0], WIDTH), jnp.bfloat16),
         compiler_params=pltpu.CompilerParams(vmem_limit_bytes=VMEM_BYTES),
+        cost_estimate=pl.CostEstimate(flops=5_000_000_000, bytes_accessed=15_000_000, transcendentals=0),
     )(index, rows)
 
 
@@ -299,7 +311,7 @@
     def exchange(array, axes):
         return lax.all_to_all(array, axes, split_axis=0, concat_axis=0, tiled=True)
 
-    *parts, pieces = packed(head_at, queries, out_grad, key_states, value_states)
+    pieces = interleaved(key_states.reshape(-1, width), value_states.reshape(-1, width))
     rows = exchange(pieces.reshape(devices, PAIR, width), AXES).reshape(blocks, width)
 
     far = block_pairs[:, 3].reshape(shard_count, here)
@@ -308,16 +320,22 @@
     kinds = lax.dynamic_slice_in_dim(pair_kinds, rank * here, here, 0)
     stats = jnp.stack([log_sums, row_deltas]).transpose(0, 2, 1)
     stats = stats.reshape(2, here, 1, BLOCK * group)
-    index, kinds, logs, deltas = lax.optimization_barrier((index, kinds, stats[0], stats[1]))
+    later = lax.optimization_barrier((pieces, queries, out_grad, key_states, value_states))
+    parts = packed((1, 2, 3), head_at, *later[1:])
+    index, kinds, logs, deltas, *parts = lax.optimization_barrier(
+        (index, kinds, stats[0], stats[1], *parts)
+    )
     got = exchange(gather_rows(index.reshape(-1, 1), rows).reshape(wire), "ctx")
 
+    ready = lax.optimization_barrier((rows, queries, out_grad, key_states, value_states))
+    parts = [*packed((0,), head_at, *ready[1:]), *parts]
     for k in (2, 1, 3):
         if k == 1:
-            parts = list(lax.optimization_barrier(parts))
+            parts[1:] = lax.optimization_barrier(parts[1:])
         parts[k] = lax.ppermute(parts[k], "head", [(i, (i + k) % SPLIT) for i in range(SPLIT)])
     dquery, own, sent = attention(head_at, kinds, parts, got.reshape(-1, width), logs, deltas)
 
-    back = exchange(sent.reshape(wire), "ctx")
+    back = exchange(sent.reshape(shard_count, 1, SLOTS * width), "ctx")
     sums = scatter_rows(index.reshape(1, -1), back.reshape(-1, width), blocks)
     home = exchange(sums.reshape(devices, PAIR, width), AXES)
 

time: 156 us -> 156 us (level)
  waiting for transfers between devices: 49.5 us -> 43.3 us
  starting transfers between devices: 77.2 us -> 82.1 us
    all_to_all x4, waiting for transfers between devices: 47 us -> 40.8 us  [exchange(): return lax.all_to_all(array, axes, split_axis=0, concat_axis=0, tiled=True)]
    all_to_all x4, starting transfers between devices: 55.9 us -> 61 us  [exchange(): return lax.all_to_all(array, axes, split_axis=0, concat_axis=0, tiled=True)]
    unnamed x30 -> x40, local copies, waits for them, and re-layouts: 11.5 us -> 11.8 us
  transfers between devices with their start and end apart: 10 -> 10, of which waited for: 6 -> 6; matrix products, arithmetic and copies ran while one was open for 1% -> 1% of each run, Pallas kernels for 4% -> 5%
where the time goes in v3:
time: 156 us; the launch traced here: 155 us
  starting transfers between devices  82.1 us (53%)
  waiting for transfers between devices  43.3 us (28%)
  Pallas kernels  15.3 us (10%)
  local copies, waits for them, and re-layouts  13.9 us (9%)
    all_to_all x4, starting transfers between devices, exchange(): return lax.all_to_all(array, axes, split_axis=0, concat_axis=0, tiled=True)  61 us
    all_to_all x4, waiting for transfers between devices, exchange(): return lax.all_to_all(array, axes, split_axis=0, concat_axis=0, tiled=True)  40.8 us
    unnamed x40, local copies, waits for them, and re-layouts  11.8 us
    ppermute x3, starting transfers between devices, shards(): lax.ppermute(parts[k], 'head', [(i, (i + k) % SPLIT) for i in range(SPLIT)])  11.3 us
    ppermute x3, starting transfers between devices, shards(): lax.ppermute(parts[k], 'head', [(i, (i - k) % SPLIT) for i in range(SPLIT)])  9.81 us
    pallas_call x1, Pallas kernels, attention(): pl.pallas_call(attend, in_specs=[smem, smem] + [vmem] * (SPLIT + 3), out_...  5.3 us
  transfers between devices with their start and end apart: 10, of which 6 were waited for; matrix products, arithmetic and copies ran while one was open for 1% of the time, Pallas kernels for 5%

profile of v3, /device:TPU:1, one launch (start us, length us, event | category | flops | bytes accessed | tf_op | source)
XLA Modules:
  0.0 155.5 jit_solution(12614480380625074730)
XLA Ops:
  3.2 22.2 %all-to-all-start = ((bf16[512,2,128]{2,1,0:T(2,128)(2,1)}), bf16[512,2,128]{2,1,0:T(2,128)(2,1)S(1)}, u32[]{:S(2)}, u32[]{:S(2)}) async-start(bf16[512,2,128]{2,1,0:T(2,128)(2,1)} %bitcast.6), calls=%async_computation | async-start | bytes 524288 | tf_op jit(solution)/shard_map/all_to_all | solution.py:312
  27.2 1.2 copy-done.5
  28.4 1.2 copy-done.7
  29.6 1.7 %shard_map.104 = (bf16[2304,128]{1,0:T(8,128)(2,1)S(1)}, bf16[2304,128]{1,0:T(8,128)(2,1)}, bf16[2304,128]{1,0:T(8,128)(2,1)S(1)}) custom-call(s32[1]{0:T(128)} %bitcast.head_ref, bf16[128,32,128]{2,1,0:T(8,128)(2,1)S(1)} %copy-done.5, bf16[128,32,128]{2,1,0:T(8,128)(2,1)S(1)} %copy-done.7, bf16[128,4,128]{2,1,0:T(4,128)(2,1)S(1)} %copy-done.2, ...), custom_call_target="tpu_custom_call" | custom-call | flops 20000000000 | bytes 60000000 | tf_op jit(solution)/shard_map/pallas_call | solution.py:70
  32.9 4.8 %collective-permute-start = (bf16[2304,128]{1,0:T(8,128)(2,1)}, bf16[2304,128]{1,0:T(8,128)(2,1)}, u32[]{:S(2)}, u32[]{:S(2)}) collective-permute-start(bf16[2304,128]{1,0:T(8,128)(2,1)} %get-tuple-element.48), channel_id=1, source_target_pairs={{0,2},{1,3},{2,0},{3,1},{4,6},{5,7},{6,4},{7,5},{8,10},{9,11},{10,... | collective-permute-start | bytes 1769480 | tf_op jit(solution)/shard_map/ppermute | solution.py:335
  38.1 3.6 %all-to-all-done = bf16[512,2,128]{2,1,0:T(2,128)(2,1)S(1)} async-done(((bf16[512,2,128]{2,1,0:T(2,128)(2,1)}), bf16[512,2,128]{2,1,0:T(2,128)(2,1)S(1)}, u32[]{:S(2)}, u32[]{:S(2)}) %all-to-all-start) | async-done | bytes 262176 | tf_op jit(solution)/shard_map/all_to_all | solution.py:312
  41.7 1.6 %shard_map.106 = bf16[1280,128]{1,0:T(8,128)(2,1)} custom-call(s32[1280,1]{1,0:T(8,128)S(1)} %reshape.88.index_ref, bf16[1024,128]{1,0:T(8,128)(2,1)S(1)} %bitcast.22), custom_call_target="tpu_custom_call" | custom-call | flops 5000000000 | bytes 15000000 | tf_op jit(solution)/shard_map/pallas_call | solution.py:268
  43.3 12.3 %all-to-all-start.1 = ((bf16[128,5,2,128]{3,2,1,0:T(2,128)(2,1)}), bf16[128,5,2,128]{3,2,1,0:T(2,128)(2,1)S(1)}, u32[]{:S(2)}, u32[]{:S(2)}) async-start(bf16[128,5,2,128]{3,2,1,0:T(2,128)(2,1)} %bitcast.8), calls=%async_computation.1 | async-start | bytes 655360 | tf_op jit(solution)/shard_map/all_to_all | solution.py:312
  55.6 2.2 %collective-permute-start.1 = (bf16[2304,128]{1,0:T(8,128)(2,1)}, bf16[2304,128]{1,0:T(8,128)(2,1)}, u32[]{:S(2)}, u32[]{:S(2)}) collective-permute-start(bf16[2304,128]{1,0:T(8,128)(2,1)} %copy-done.11), channel_id=1, source_target_pairs={{0,1},{1,2},{2,3},{3,0},{4,5},{5,6},{6,7},{7,4},{8,9},{9,10},{10,1... | collective-permute-start | bytes 1769480 | tf_op jit(solution)/shard_map/ppermute | solution.py:335
  57.9 4.3 %collective-permute-start.2 = (bf16[2304,128]{1,0:T(8,128)(2,1)S(1)}, bf16[2304,128]{1,0:T(8,128)(2,1)}, u32[]{:S(2)}, u32[]{:S(2)}) collective-permute-start(bf16[2304,128]{1,0:T(8,128)(2,1)S(1)} %copy-done.10), channel_id=1, source_target_pairs={{0,3},{1,0},{2,1},{3,2},{4,7},{5,4},{6,5},{7,6},{8,11},{9,8},{10,9... | collective-permute-start | bytes 1769480 | tf_op jit(solution)/shard_map/ppermute | solution.py:335
  63.5 7.7 %all-to-all-done.1 = bf16[128,5,2,128]{3,2,1,0:T(2,128)(2,1)S(1)} async-done(((bf16[128,5,2,128]{3,2,1,0:T(2,128)(2,1)}), bf16[128,5,2,128]{3,2,1,0:T(2,128)(2,1)S(1)}, u32[]{:S(2)}, u32[]{:S(2)}) %all-to-all-start.1) | async-done | bytes 327712 | tf_op jit(solution)/shard_map/all_to_all | solution.py:312
  71.2 1.8 %collective-permute-done.1.refs_1_ = bf16[2304,128]{1,0:T(8,128)(2,1)} collective-permute-done((bf16[2304,128]{1,0:T(8,128)(2,1)}, bf16[2304,128]{1,0:T(8,128)(2,1)}, u32[]{:S(2)}, u32[]{:S(2)}) %collective-permute-start.1) | collective-permute-done | bytes 589856 | tf_op jit(solution)/shard_map/ppermute | solution.py:335
  73.6 1.1 copy-done.15
  74.7 5.3 %shard_map.107 = (bf16[4,1024,128]{2,1,0:T(8,128)(2,1)S(1)}, f32[4,2,128,128]{3,2,1,0:T(8,128)S(1)}, f32[1280,128]{1,0:T(8,128)}) custom-call(s32[1]{0:T(128)} %bitcast.head_ref, s32[8,4]{1,0:T(8,128)S(1)} %copy.30.kinds, bf16[2304,128]{1,0:T(8,128)(2,1)S(1)} %copy-done.15, bf16[2304,128]{1,0:T(8,128)(2,1)} %collective-permute-done.1.refs_1_, ...), custom_call_target="tpu_custom_call" | custom-call | flops 1400000000 | bytes 8000000 | tf_op jit(solution)/shard_map/pallas_call | solution.py:157
  80.9 15.5 %all-to-all-start.2 = ((f32[128,1,1280]{2,1,0:T(1,128)}), f32[128,1,1280]{2,1,0:T(1,128)S(1)}, u32[]{:S(2)}, u32[]{:S(2)}) async-start(f32[128,1,1280]{2,1,0:T(1,128)} %bitcast.10), calls=%async_computation.2 | async-start | bytes 1310720 | tf_op jit(solution)/shard_map/all_to_all | solution.py:312
  96.4 1.2 copy-done.13
  98.5 5.4 %collective-permute-start.3 = (bf16[1536,128]{1,0:T(8,128)(2,1)S(1)}, bf16[1536,128]{1,0:T(8,128)(2,1)S(1)}, u32[]{:S(2)}, u32[]{:S(2)}) collective-permute-start(bf16[1536,128]{1,0:T(8,128)(2,1)S(1)} %get-tuple-element.59), channel_id=1, source_target_pairs={{0,3},{1,0},{2,1},{3,2},{4,7},{5,4},{6,5},{7,6},{8,11},{9,8},{10,9... | collective-permute-start | bytes 1179656 | tf_op jit(solution)/shard_map/ppermute | solution.py:344
  103.9 1.9 %collective-permute-start.4 = (bf16[1536,128]{1,0:T(8,128)(2,1)S(1)}, bf16[1536,128]{1,0:T(8,128)(2,1)S(1)}, u32[]{:S(2)}, u32[]{:S(2)}) collective-permute-start(bf16[1536,128]{1,0:T(8,128)(2,1)S(1)} %get-tuple-element.60), channel_id=1, source_target_pairs={{0,2},{1,3},{2,0},{3,1},{4,6},{5,7},{6,4},{7,5},{8,10},{9,11},{10,... | collective-permute-start | bytes 1179656 | tf_op jit(solution)/shard_map/ppermute | solution.py:344
  105.8 2.5 %collective-permute-start.5 = (bf16[1536,128]{1,0:T(8,128)(2,1)S(1)}, bf16[1536,128]{1,0:T(8,128)(2,1)S(1)}, u32[]{:S(2)}, u32[]{:S(2)}) collective-permute-start(bf16[1536,128]{1,0:T(8,128)(2,1)S(1)} %get-tuple-element.61), channel_id=1, source_target_pairs={{0,1},{1,2},{2,3},{3,0},{4,5},{5,6},{6,7},{7,4},{8,9},{9,10},{10,1... | collective-permute-start | bytes 1179656 | tf_op jit(solution)/shard_map/ppermute | solution.py:344
  108.5 10.3 %all-to-all-done.2 = f32[128,1,1280]{2,1,0:T(1,128)S(1)} async-done(((f32[128,1,1280]{2,1,0:T(1,128)}), f32[128,1,1280]{2,1,0:T(1,128)S(1)}, u32[]{:S(2)}, u32[]{:S(2)}) %all-to-all-start.2) | async-done | bytes 655392 | tf_op jit(solution)/shard_map/all_to_all | solution.py:312
  118.7 3.0 %shard_map.110 = f32[1024,128]{1,0:T(8,128)} custom-call(s32[1,1280]{1,0:T(1,128)S(1)} %reshape.80.index_ref, f32[1280,128]{1,0:T(8,128)S(1)} %bitcast.18), custom_call_target="tpu_custom_call" | custom-call | tf_op jit(solution)/shard_map/pallas_call | solution.py:290
  121.8 11.0 %all-to-all-start.3 = ((f32[512,2,128]{2,1,0:T(2,128)}), f32[512,2,128]{2,1,0:T(2,128)S(1)}, u32[]{:S(2)}, u32[]{:S(2)}) async-start(f32[512,2,128]{2,1,0:T(2,128)} %bitcast.12), calls=%async_computation.3 | async-start | bytes 1048576 | tf_op jit(solution)/shard_map/all_to_all | solution.py:312
  133.8 1.6 %shard_map.109 = (bf16[128,32,128]{2,1,0:T(8,128)(2,1)}, f32[2,128,4,128]{3,2,1,0:T(4,128)S(1)}) custom-call(s32[1]{0:T(128)} %bitcast.head_ref, bf16[1536,128]{1,0:T(8,128)(2,1)S(1)} %copy-done.17, bf16[1536,128]{1,0:T(8,128)(2,1)S(1)} %collective-permute-done.3.refs_1_, bf16[1536,128]{1,0:T(8,128)(2,1)S(1)} %collective-permute-done.4.refs_2_, ...), custom_call_target="tpu_custom_call" | custom-call | flops 20000000000 | bytes 60000000 | tf_op jit(solution)/shard_map/pallas_call | solution.py:223
  135.5 19.3 %all-to-all-done.3 = f32[512,2,128]{2,1,0:T(2,128)S(1)} async-done(((f32[512,2,128]{2,1,0:T(2,128)}), f32[512,2,128]{2,1,0:T(2,128)S(1)}, u32[]{:S(2)}, u32[]{:S(2)}) %all-to-all-start.3) | async-done | bytes 524320 | tf_op jit(solution)/shard_map/all_to_all | solution.py:312
  (64 shorter events, 11.9 us)
Async XLA Ops:
  0.6 24.8 %copy-start = (s32[1024,4]{0,1:T(4,128)S(1)}, s32[1024,4]{0,1:T(4,128)}, u32[]{:S(2)}) copy-start(s32[1024,4]{0,1:T(4,128)} %param.15) | copy-start | bytes 49156
  0.6 0.9 copy-start.1
  1.6 0.9 copy-start.3
  3.2 23.9 %copy-start.4 = (bf16[128,4,128]{2,1,0:T(4,128)(2,1)S(1)}, bf16[128,4,128]{2,1,0:T(4,128)(2,1)}, u32[]{:S(2)}) copy-start(bf16[128,4,128]{2,1,0:T(4,128)(2,1)} %v_ref.1) | copy-start | bytes 393220
  3.2 38.4 %all-to-all-start = ((bf16[512,2,128]{2,1,0:T(2,128)(2,1)}), bf16[512,2,128]{2,1,0:T(2,128)(2,1)S(1)}, u32[]{:S(2)}, u32[]{:S(2)}) async-start(bf16[512,2,128]{2,1,0:T(2,128)(2,1)} %bitcast.6), calls=%async_computation | async-start | bytes 524288 | tf_op jit(solution)/shard_map/all_to_all | solution.py:312
  25.4 1.8 %copy-start.2 = (bf16[128,4,128]{2,1,0:T(4,128)(2,1)S(1)}, bf16[128,4,128]{2,1,0:T(4,128)(2,1)}, u32[]{:S(2)}) copy-start(bf16[128,4,128]{2,1,0:T(4,128)(2,1)} %k_ref.1) | copy-start | bytes 393220
  27.2 1.2 copy-start.5
  28.4 1.2 copy-start.7
  32.9 22.7 %collective-permute-start = (bf16[2304,128]{1,0:T(8,128)(2,1)}, bf16[2304,128]{1,0:T(8,128)(2,1)}, u32[]{:S(2)}, u32[]{:S(2)}) collective-permute-start(bf16[2304,128]{1,0:T(8,128)(2,1)} %get-tuple-element.48), channel_id=1, source_target_pairs={{0,2},{1,3},{2,0},{3,1},{4,6},{5,7},{6,4},{7,5},{8,10},{9,11},{10,... | collective-permute-start | bytes 1769480 | tf_op jit(solution)/shard_map/ppermute | solution.py:335
  41.7 20.5 %copy-start.6 = (bf16[128,32,128]{2,1,0:T(8,128)(2,1)S(1)}, bf16[128,32,128]{2,1,0:T(8,128)(2,1)}, u32[]{:S(2)}) copy-start(bf16[128,32,128]{2,1,0:T(8,128)(2,1)} %q_ref.1) | copy-start | bytes 3145732
  41.7 20.5 %copy-start.8 = (bf16[128,32,128]{2,1,0:T(8,128)(2,1)S(1)}, bf16[128,32,128]{2,1,0:T(8,128)(2,1)}, u32[]{:S(2)}) copy-start(bf16[128,32,128]{2,1,0:T(8,128)(2,1)} %g_ref.1) | copy-start | bytes 3145732
  43.3 14.6 %copy-start.10 = (bf16[2304,128]{1,0:T(8,128)(2,1)S(1)}, bf16[2304,128]{1,0:T(8,128)(2,1)}, u32[]{:S(2)}) copy-start(bf16[2304,128]{1,0:T(8,128)(2,1)} %copy-done.9) | copy-start | bytes 1769476
  43.3 27.9 %all-to-all-start.1 = ((bf16[128,5,2,128]{3,2,1,0:T(2,128)(2,1)}), bf16[128,5,2,128]{3,2,1,0:T(2,128)(2,1)S(1)}, u32[]{:S(2)}, u32[]{:S(2)}) async-start(bf16[128,5,2,128]{3,2,1,0:T(2,128)(2,1)} %bitcast.8), calls=%async_computation.1 | async-start | bytes 655360 | tf_op jit(solution)/shard_map/all_to_all | solution.py:312
  55.6 17.4 %collective-permute-start.1 = (bf16[2304,128]{1,0:T(8,128)(2,1)}, bf16[2304,128]{1,0:T(8,128)(2,1)}, u32[]{:S(2)}, u32[]{:S(2)}) collective-permute-start(bf16[2304,128]{1,0:T(8,128)(2,1)} %copy-done.11), channel_id=1, source_target_pairs={{0,1},{1,2},{2,3},{3,0},{4,5},{5,6},{6,7},{7,4},{8,9},{9,10},{10,1... | collective-permute-start | bytes 1769480 | tf_op jit(solution)/shard_map/ppermute | solution.py:335
  57.9 15.7 %collective-permute-start.2 = (bf16[2304,128]{1,0:T(8,128)(2,1)S(1)}, bf16[2304,128]{1,0:T(8,128)(2,1)}, u32[]{:S(2)}, u32[]{:S(2)}) collective-permute-start(bf16[2304,128]{1,0:T(8,128)(2,1)S(1)} %copy-done.10), channel_id=1, source_target_pairs={{0,3},{1,0},{2,1},{3,2},{4,7},{5,4},{6,5},{7,6},{8,11},{9,8},{10,9... | collective-permute-start | bytes 1769480 | tf_op jit(solution)/shard_map/ppermute | solution.py:335
  73.6 1.1 copy-start.15
  80.0 1.0 copy-start.12
  80.9 37.8 %all-to-all-start.2 = ((f32[128,1,1280]{2,1,0:T(1,128)}), f32[128,1,1280]{2,1,0:T(1,128)S(1)}, u32[]{:S(2)}, u32[]{:S(2)}) async-start(f32[128,1,1280]{2,1,0:T(1,128)} %bitcast.10), calls=%async_computation.2 | async-start | bytes 1310720 | tf_op jit(solution)/shard_map/all_to_all | solution.py:312
  96.4 1.2 copy-start.13
  98.5 34.3 %collective-permute-start.3 = (bf16[1536,128]{1,0:T(8,128)(2,1)S(1)}, bf16[1536,128]{1,0:T(8,128)(2,1)S(1)}, u32[]{:S(2)}, u32[]{:S(2)}) collective-permute-start(bf16[1536,128]{1,0:T(8,128)(2,1)S(1)} %get-tuple-element.59), channel_id=1, source_target_pairs={{0,3},{1,0},{2,1},{3,2},{4,7},{5,4},{6,5},{7,6},{8,11},{9,8},{10,9... | collective-permute-start | bytes 1179656 | tf_op jit(solution)/shard_map/ppermute | solution.py:344
  103.9 28.9 %collective-permute-start.4 = (bf16[1536,128]{1,0:T(8,128)(2,1)S(1)}, bf16[1536,128]{1,0:T(8,128)(2,1)S(1)}, u32[]{:S(2)}, u32[]{:S(2)}) collective-permute-start(bf16[1536,128]{1,0:T(8,128)(2,1)S(1)} %get-tuple-element.60), channel_id=1, source_target_pairs={{0,2},{1,3},{2,0},{3,1},{4,6},{5,7},{6,4},{7,5},{8,10},{9,11},{10,... | collective-permute-start | bytes 1179656 | tf_op jit(solution)/shard_map/ppermute | solution.py:344
  105.8 27.0 %collective-permute-start.5 = (bf16[1536,128]{1,0:T(8,128)(2,1)S(1)}, bf16[1536,128]{1,0:T(8,128)(2,1)S(1)}, u32[]{:S(2)}, u32[]{:S(2)}) collective-permute-start(bf16[1536,128]{1,0:T(8,128)(2,1)S(1)} %get-tuple-element.61), channel_id=1, source_target_pairs={{0,1},{1,2},{2,3},{3,0},{4,5},{5,6},{6,7},{7,4},{8,9},{9,10},{10,1... | collective-permute-start | bytes 1179656 | tf_op jit(solution)/shard_map/ppermute | solution.py:344
  121.8 33.0 %all-to-all-start.3 = ((f32[512,2,128]{2,1,0:T(2,128)}), f32[512,2,128]{2,1,0:T(2,128)S(1)}, u32[]{:S(2)}, u32[]{:S(2)}) async-start(f32[512,2,128]{2,1,0:T(2,128)} %bitcast.12), calls=%async_computation.3 | async-start | bytes 1048576 | tf_op jit(solution)/shard_map/all_to_all | solution.py:312
  132.8 1.0 copy-start.17
  (6 other events, 4.6 us)

commit v4 on v3

--- a/solution.py
+++ b/solution.py
@@ -1,5 +1,3 @@
-import functools
-
 import jax
 import jax.numpy as jnp
 from jax import lax
@@ -15,6 +13,7 @@
 SLOTS = SPLIT * PAIR + 2
 HUB, BEFORE = SLOTS - 2, SLOTS - 1
 VMEM_BYTES = 20 * 1024 * 1024
+WHOLE_VMEM = 60 * 1024 * 1024
 SLOW = pl.CostEstimate(flops=20_000_000_000, bytes_accessed=60_000_000, transcendentals=0)
 
 
@@ -22,6 +21,13 @@
     return lax.dot_general(
         left, right, (contract, ((), ())), preferred_element_type=jnp.float32
     )
+
+
+def three_parts(rows):
+    high = rows.astype(jnp.bfloat16)
+    rest = rows - high.astype(jnp.float32)
+    middle = rest.astype(jnp.bfloat16)
+    return high, middle, (rest - middle.astype(jnp.float32)).astype(jnp.bfloat16)
 
 
 def strided(slot, kv):
@@ -44,37 +50,69 @@
         interleave,
         out_shape=jax.ShapeDtypeStruct(both, jnp.bfloat16),
         scratch_shapes=[pltpu.VMEM(both, jnp.float32)],
-        compiler_params=pltpu.CompilerParams(vmem_limit_bytes=VMEM_BYTES),
+        compiler_params=pltpu.CompilerParams(vmem_limit_bytes=WHOLE_VMEM),
     )(keys, values)
 
 
-def pack(steps, head_ref, q_ref, g_ref, k_ref, v_ref, *out_refs):
+def pack(head_ref, q_ref, g_ref, k_ref, v_ref, *out_refs):
     tokens = q_ref.shape[0]
     group = q_ref.shape[1] // SPLIT
     rows = tokens * group
-    for out_ref, k in zip(out_refs, steps):
+    for k in range(SPLIT):
         for to in range(SPLIT):
 
             @pl.when(lax.rem(head_ref[0] + k, SPLIT) == to)
-            def _(out_ref=out_ref, to=to):
+            def _(k=k, to=to):
                 heads = slice(to * group, (to + 1) * group)
-                out_ref[:rows] = q_ref[:, heads, :].reshape(rows, WIDTH)
-                out_ref[rows : 2 * rows] = g_ref[:, heads, :].reshape(rows, WIDTH)
-                out_ref[2 * rows : 2 * rows + tokens] = k_ref[:, to, :]
-                out_ref[2 * rows + tokens :] = v_ref[:, to, :]
-
-
-def packed(steps, head, queries, grads, keys, values):
+                out_refs[k][:rows] = q_ref[:, heads, :].reshape(rows, WIDTH)
+                out_refs[k][rows : 2 * rows] = g_ref[:, heads, :].reshape(rows, WIDTH)
+                out_refs[k][2 * rows : 2 * rows + tokens] = k_ref[:, to, :]
+                out_refs[k][2 * rows + tokens :] = v_ref[:, to, :]
+
+
+def packed(head, queries, grads, keys, values):
     tokens, heads, width = queries.shape
     part = jax.ShapeDtypeStruct((2 * tokens * (heads // SPLIT + 1), width), jnp.bfloat16)
     return pl.pallas_call(
-        functools.partial(pack, steps),
+        pack,
         in_specs=[pl.BlockSpec(memory_space=pltpu.SMEM)] + [pl.BlockSpec()] * 4,
-        out_specs=[pl.BlockSpec()] * len(steps),
-        out_shape=[part] * len(steps),
-        compiler_params=pltpu.CompilerParams(vmem_limit_bytes=VMEM_BYTES),
+        out_specs=[pl.BlockSpec()] * SPLIT,
+        out_shape=[part] * SPLIT,
+        compiler_params=pltpu.CompilerParams(vmem_limit_bytes=WHOLE_VMEM),
         cost_estimate=SLOW,
     )(head, queries, grads, keys, values)
+
+
+def spread(*refs):
+    stat_refs, row_refs = refs[:2], refs[2:]
+    group = stat_refs[0].shape[0]
+    columns = BLOCK * group
+    stats = jnp.concatenate([ref[...] for ref in stat_refs], axis=0)
+    stats = jnp.concatenate(three_parts(stats), axis=0)
+    token_at = lax.broadcasted_iota(jnp.int32, (BLOCK, columns), 0)
+    column_at = lax.broadcasted_iota(jnp.int32, (BLOCK, columns), 1)
+    copies = jnp.where(token_at == column_at // group, 1.0, 0.0).astype(jnp.bfloat16)
+    head_at = lax.broadcasted_iota(jnp.int32, (group, columns), 0)
+    mine = head_at == lax.broadcasted_iota(jnp.int32, (group, columns), 1) % group
+    for at in range(SPLIT * PAIR):
+        wide = dot(stats[:, at * BLOCK : (at + 1) * BLOCK], copies)
+        for which, row_ref in enumerate(row_refs):
+            starts = [(2 * part + which) * group for part in range(3)]
+            value = sum(wide[start : start + group] for start in starts)
+            row_ref[at] = jnp.sum(jnp.where(mine, value, 0.0), axis=0, keepdims=True)
+
+
+def spread_rows(*stats):
+    vmem = pl.BlockSpec(memory_space=pltpu.VMEM)
+    row = jax.ShapeDtypeStruct((SPLIT * PAIR, 1, BLOCK * stats[0].shape[0]), jnp.float32)
+    return pl.pallas_call(
+        spread,
+        in_specs=[vmem] * 2,
+        out_specs=[vmem] * 2,
+        out_shape=[row, row],
+        compiler_params=pltpu.CompilerParams(vmem_limit_bytes=VMEM_BYTES),
+        cost_estimate=SLOW,
+    )(*stats)
 
 
 def attend(head_ref, kinds, *refs):
@@ -275,10 +313,7 @@
 
 def add_rows(index_ref, rows_ref, out_ref):
     rows = rows_ref[...]
-    high = rows.astype(jnp.bfloat16)
-    rest = rows - high.astype(jnp.float32)
-    middle = rest.astype(jnp.bfloat16)
-    low = (rest - middle.astype(jnp.float32)).astype(jnp.bfloat16)
+    high, middle, low = three_parts(rows)
     chunk = 256
     for start in range(0, out_ref.shape[0], chunk):
         block_at = lax.broadcasted_iota(jnp.int32, (chunk, rows.shape[0]), 0) + start
@@ -318,21 +353,15 @@
     before = jnp.maximum(here * jnp.arange(shard_count, dtype=jnp.int32) - 1, 0)
     index = jnp.concatenate([far, jnp.zeros_like(before)[:, None], before[:, None]], axis=1)
     kinds = lax.dynamic_slice_in_dim(pair_kinds, rank * here, here, 0)
-    stats = jnp.stack([log_sums, row_deltas]).transpose(0, 2, 1)
-    stats = stats.reshape(2, here, 1, BLOCK * group)
     later = lax.optimization_barrier((pieces, queries, out_grad, key_states, value_states))
-    parts = packed((1, 2, 3), head_at, *later[1:])
-    index, kinds, logs, deltas, *parts = lax.optimization_barrier(
-        (index, kinds, stats[0], stats[1], *parts)
-    )
+    parts = packed(head_at, *later[1:])
+    index, *parts = lax.optimization_barrier((index, *parts))
     got = exchange(gather_rows(index.reshape(-1, 1), rows).reshape(wire), "ctx")
 
-    ready = lax.optimization_barrier((rows, queries, out_grad, key_states, value_states))
-    parts = [*packed((0,), head_at, *ready[1:]), *parts]
-    for k in (2, 1, 3):
-        if k == 1:
-            parts[1:] = lax.optimization_barrier(parts[1:])
+    for k in range(1, SPLIT):
         parts[k] = lax.ppermute(parts[k], "head", [(i, (i + k) % SPLIT) for i in range(SPLIT)])
+    log_sums, row_deltas, *parts = lax.optimization_barrier((log_sums, row_deltas, *parts))
+    logs, deltas = spread_rows(log_sums, row_deltas)
     dquery, own, sent = attention(head_at, kinds, parts, got.reshape(-1, width), logs, deltas)
 
     back = exchange(sent.reshape(shard_count, 1, SLOTS * width), "ctx")

time: 156 us -> 147 us (0.942)
  starting transfers between devices: 82.1 us -> 74.3 us
  local copies, waits for them, and re-layouts: 13.9 us -> 6.25 us
  waiting for transfers between devices: 43.3 us -> 47 us
  Pallas kernels: 15.3 us -> 17.8 us
    unnamed x40 -> x21, local copies, waits for them, and re-layouts: 11.8 us -> 4.84 us
    all_to_all x4, starting transfers between devices: 61 us -> 55.8 us  [exchange(): return lax.all_to_all(array, axes, split_axis=0, concat_axis=0, tiled=True)]
    all_to_all x4, waiting for transfers between devices: 40.8 us -> 43.4 us  [exchange(): return lax.all_to_all(array, axes, split_axis=0, concat_axis=0, tiled=True)]
    pallas_call x2, Pallas kernels: 2.12 us -> 4.44 us  [the longest x1 4.12 us: packed(): pl.pallas_call(pack, in_specs=[pl.BlockSpec(memory_space=pltpu.SMEM)] + [...]
    ppermute x3, starting transfers between devices: 9.81 us -> 7.81 us  [shards(): lax.ppermute(parts[k], 'head', [(i, (i - k) % SPLIT) for i in range(SPLIT)])]
  transfers between devices with their start and end apart: 10 -> 10, of which waited for: 6 -> 5; matrix products, arithmetic and copies ran while one was open for 1% -> 1% of each run, Pallas kernels for 5% -> 7%
where the time goes in v4:
time: 147 us; the launch traced here: 146 us
  starting transfers between devices  74.3 us (51%)
  waiting for transfers between devices  47 us (32%)
  Pallas kernels  17.8 us (12%)
  local copies, waits for them, and re-layouts  6.25 us (4%)
    all_to_all x4, starting transfers between devices, exchange(): return lax.all_to_all(array, axes, split_axis=0, concat_axis=0, tiled=True)  55.8 us
    all_to_all x4, waiting for transfers between devices, exchange(): return lax.all_to_all(array, axes, split_axis=0, concat_axis=0, tiled=True)  43.4 us
    ppermute x3, starting transfers between devices, shards(): lax.ppermute(parts[k], 'head', [(i, (i + k) % SPLIT) for i in range(SPLIT)])  10.7 us
    ppermute x3, starting transfers between devices, shards(): lax.ppermute(parts[k], 'head', [(i, (i - k) % SPLIT) for i in range(SPLIT)])  7.81 us
    unnamed x21, local copies, waits for them, and re-layouts  4.84 us
    pallas_call x1, Pallas kernels, attention(): pl.pallas_call(attend, in_specs=[smem, smem] + [vmem] * (SPLIT + 3), out_...  4.47 us
    pallas_call x1, Pallas kernels, packed(): pl.pallas_call(pack, in_specs=[pl.BlockSpec(memory_space=pltpu.SMEM)] + [...  4.12 us
    ppermute x3, waiting for transfers between devices, shards(): lax.ppermute(parts[k], 'head', [(i, (i + k) % SPLIT) for i in range(SPLIT)])  3.59 us
  transfers between devices with their start and end apart: 10, of which 5 were waited for; matrix products, arithmetic and copies ran while one was open for 1% of the time, Pallas kernels for 7%

profile of v4, /device:TPU:1, one launch (start us, length us, event | category | flops | bytes accessed | tf_op | source)
XLA Modules:
  0.0 146.2 jit_solution(14946093244984376499)
XLA Ops:
  0.6 1.7 %shard_map.103 = bf16[1024,128]{1,0:T(8,128)(2,1)} custom-call(bf16[512,128]{1,0:T(8,128)(2,1)} %bitcast.20, bf16[512,128]{1,0:T(8,128)(2,1)} %bitcast.21), custom_call_target="tpu_custom_call" | custom-call | tf_op jit(solution)/shard_map/pallas_call | solution.py:49
  2.4 22.2 %all-to-all-start = ((bf16[512,2,128]{2,1,0:T(2,128)(2,1)}), bf16[512,2,128]{2,1,0:T(2,128)(2,1)S(1)}, u32[]{:S(2)}, u32[]{:S(2)}) async-start(bf16[512,2,128]{2,1,0:T(2,128)(2,1)} %bitcast.19), calls=%async_computation | async-start | bytes 524288 | tf_op jit(solution)/shard_map/all_to_all | solution.py:347
  24.5 4.1 %shard_map.104 = (bf16[2304,128]{1,0:T(8,128)(2,1)}, bf16[2304,128]{1,0:T(8,128)(2,1)}, bf16[2304,128]{1,0:T(8,128)(2,1)}, bf16[2304,128]{1,0:T(8,128)(2,1)}) custom-call(s32[1]{0:T(128)} %bitcast.head_ref, bf16[128,32,128]{2,1,0:T(8,128)(2,1)} %q_ref, bf16[128,32,128]{2,1,0:T(8,128)(2,1)} %g_ref, bf16[128,4,128]{2,1,0:T(4,128)(2,1)} %k_ref, ...), custom_call_target="tpu_custom_call" | custom-call | flops 20000000000 | bytes 60000000 | tf_op jit(solution)/shard_map/pallas_call | solution.py:76
  29.6 3.3 %collective-permute-start = (bf16[2304,128]{1,0:T(8,128)(2,1)}, bf16[2304,128]{1,0:T(8,128)(2,1)S(1)}, u32[]{:S(2)}, u32[]{:S(2)}) collective-permute-start(bf16[2304,128]{1,0:T(8,128)(2,1)} %get-tuple-element.44), channel_id=1, source_target_pairs={{0,1},{1,2},{2,3},{3,0},{4,5},{5,6},{6,7},{7,4},{8,9},{9,10},{10,1... | collective-permute-start | bytes 1769480 | tf_op jit(solution)/shard_map/ppermute | solution.py:362
  32.9 4.3 %collective-permute-start.1 = (bf16[2304,128]{1,0:T(8,128)(2,1)}, bf16[2304,128]{1,0:T(8,128)(2,1)S(1)}, u32[]{:S(2)}, u32[]{:S(2)}) collective-permute-start(bf16[2304,128]{1,0:T(8,128)(2,1)} %get-tuple-element.45), channel_id=1, source_target_pairs={{0,2},{1,3},{2,0},{3,1},{4,6},{5,7},{6,4},{7,5},{8,10},{9,11},{10,... | collective-permute-start | bytes 1769480 | tf_op jit(solution)/shard_map/ppermute | solution.py:362
  37.2 3.1 %collective-permute-start.2 = (bf16[2304,128]{1,0:T(8,128)(2,1)}, bf16[2304,128]{1,0:T(8,128)(2,1)S(1)}, u32[]{:S(2)}, u32[]{:S(2)}) collective-permute-start(bf16[2304,128]{1,0:T(8,128)(2,1)} %get-tuple-element.46), channel_id=1, source_target_pairs={{0,3},{1,0},{2,1},{3,2},{4,7},{5,4},{6,5},{7,6},{8,11},{9,8},{10,9... | collective-permute-start | bytes 1769480 | tf_op jit(solution)/shard_map/ppermute | solution.py:362
  40.8 1.6 %shard_map.105 = bf16[1280,128]{1,0:T(8,128)(2,1)} custom-call(s32[1280,1]{1,0:T(8,128)S(1)} %reshape.83.index_ref, bf16[1024,128]{1,0:T(8,128)(2,1)S(1)} %bitcast.18), custom_call_target="tpu_custom_call" | custom-call | flops 5000000000 | bytes 15000000 | tf_op jit(solution)/shard_map/pallas_call | solution.py:306
  42.4 16.4 %all-to-all-start.1 = ((bf16[128,5,2,128]{3,2,1,0:T(2,128)(2,1)}), bf16[128,5,2,128]{3,2,1,0:T(2,128)(2,1)S(1)}, u32[]{:S(2)}, u32[]{:S(2)}) async-start(bf16[128,5,2,128]{3,2,1,0:T(2,128)(2,1)} %bitcast.5), calls=%async_computation.1 | async-start | bytes 655360 | tf_op jit(solution)/shard_map/all_to_all | solution.py:347
  58.9 3.3 %collective-permute-done.1.refs_2_ = bf16[2304,128]{1,0:T(8,128)(2,1)S(1)} collective-permute-done((bf16[2304,128]{1,0:T(8,128)(2,1)}, bf16[2304,128]{1,0:T(8,128)(2,1)S(1)}, u32[]{:S(2)}, u32[]{:S(2)}) %collective-permute-start.1) | collective-permute-done | bytes 589856 | tf_op jit(solution)/shard_map/ppermute | solution.py:362
  62.8 11.6 %all-to-all-done.1 = bf16[128,5,2,128]{3,2,1,0:T(2,128)(2,1)S(1)} async-done(((bf16[128,5,2,128]{3,2,1,0:T(2,128)(2,1)}), bf16[128,5,2,128]{3,2,1,0:T(2,128)(2,1)S(1)}, u32[]{:S(2)}, u32[]{:S(2)}) %all-to-all-start.1) | async-done | bytes 327712 | tf_op jit(solution)/shard_map/all_to_all | solution.py:347
  74.4 4.5 %shard_map.107 = (bf16[4,1024,128]{2,1,0:T(8,128)(2,1)S(1)}, f32[4,2,128,128]{3,2,1,0:T(8,128)S(1)}, f32[1280,128]{1,0:T(8,128)}) custom-call(s32[1]{0:T(128)} %bitcast.head_ref, s32[8,4]{1,0:T(8,128)S(1)} %copy.20.kinds, bf16[2304,128]{1,0:T(8,128)(2,1)S(1)} %copy-done.5, bf16[2304,128]{1,0:T(8,128)(2,1)S(1)} %collective-permute-done.refs_1_, ...), custom_call_target="tpu_custom_call" | custom-call | flops 1400000000 | bytes 8000000 | tf_op jit(solution)/shard_map/pallas_call | solution.py:195
  78.9 1.0 copy-done.3
  79.8 0.8 copy-done.6
  80.6 7.2 %all-to-all-start.2 = ((f32[128,1,1280]{2,1,0:T(1,128)}), f32[128,1,1280]{2,1,0:T(1,128)S(1)}, u32[]{:S(2)}, u32[]{:S(2)}) async-start(f32[128,1,1280]{2,1,0:T(1,128)} %bitcast.7), calls=%async_computation.2 | async-start | bytes 1310720 | tf_op jit(solution)/shard_map/all_to_all | solution.py:347
  87.8 1.2 copy-done.4
  89.9 2.3 %collective-permute-start.3 = (bf16[1536,128]{1,0:T(8,128)(2,1)S(1)}, bf16[1536,128]{1,0:T(8,128)(2,1)S(1)}, u32[]{:S(2)}, u32[]{:S(2)}) collective-permute-start(bf16[1536,128]{1,0:T(8,128)(2,1)S(1)} %get-tuple-element.59), channel_id=1, source_target_pairs={{0,3},{1,0},{2,1},{3,2},{4,7},{5,4},{6,5},{7,6},{8,11},{9,8},{10,9... | collective-permute-start | bytes 1179656 | tf_op jit(solution)/shard_map/ppermute | solution.py:373
  92.2 3.6 %collective-permute-start.4 = (bf16[1536,128]{1,0:T(8,128)(2,1)S(1)}, bf16[1536,128]{1,0:T(8,128)(2,1)S(1)}, u32[]{:S(2)}, u32[]{:S(2)}) collective-permute-start(bf16[1536,128]{1,0:T(8,128)(2,1)S(1)} %get-tuple-element.60), channel_id=1, source_target_pairs={{0,2},{1,3},{2,0},{3,1},{4,6},{5,7},{6,4},{7,5},{8,10},{9,11},{10,... | collective-permute-start | bytes 1179656 | tf_op jit(solution)/shard_map/ppermute | solution.py:373
  95.8 1.9 %collective-permute-start.5 = (bf16[1536,128]{1,0:T(8,128)(2,1)S(1)}, bf16[1536,128]{1,0:T(8,128)(2,1)S(1)}, u32[]{:S(2)}, u32[]{:S(2)}) collective-permute-start(bf16[1536,128]{1,0:T(8,128)(2,1)S(1)} %get-tuple-element.61), channel_id=1, source_target_pairs={{0,1},{1,2},{2,3},{3,0},{4,5},{5,6},{6,7},{7,4},{8,9},{9,10},{10,1... | collective-permute-start | bytes 1179656 | tf_op jit(solution)/shard_map/ppermute | solution.py:373
  97.9 12.3 %all-to-all-done.2 = f32[128,1,1280]{2,1,0:T(1,128)S(1)} async-done(((f32[128,1,1280]{2,1,0:T(1,128)}), f32[128,1,1280]{2,1,0:T(1,128)S(1)}, u32[]{:S(2)}, u32[]{:S(2)}) %all-to-all-start.2) | async-done | bytes 655392 | tf_op jit(solution)/shard_map/all_to_all | solution.py:347
  110.2 3.0 %shard_map.110 = f32[1024,128]{1,0:T(8,128)} custom-call(s32[1,1280]{1,0:T(1,128)S(1)} %reshape.75.index_ref, f32[1280,128]{1,0:T(8,128)S(1)} %bitcast.14), custom_call_target="tpu_custom_call" | custom-call | tf_op jit(solution)/shard_map/pallas_call | solution.py:325
  113.3 10.1 %all-to-all-start.3 = ((f32[512,2,128]{2,1,0:T(2,128)}), f32[512,2,128]{2,1,0:T(2,128)S(1)}, u32[]{:S(2)}, u32[]{:S(2)}) async-start(f32[512,2,128]{2,1,0:T(2,128)} %bitcast.9), calls=%async_computation.3 | async-start | bytes 1048576 | tf_op jit(solution)/shard_map/all_to_all | solution.py:347
  123.4 1.0 copy-done.9
  124.4 1.6 %shard_map.109 = (bf16[128,32,128]{2,1,0:T(8,128)(2,1)}, f32[2,128,4,128]{3,2,1,0:T(4,128)S(1)}) custom-call(s32[1]{0:T(128)} %bitcast.head_ref, bf16[1536,128]{1,0:T(8,128)(2,1)S(1)} %copy-done.9, bf16[1536,128]{1,0:T(8,128)(2,1)S(1)} %collective-permute-done.3.refs_1_, bf16[1536,128]{1,0:T(8,128)(2,1)S(1)} %collective-permute-done.4.refs_2_, ...), custom_call_target="tpu_custom_call" | custom-call | flops 20000000000 | bytes 60000000 | tf_op jit(solution)/shard_map/pallas_call | solution.py:261
  126.0 19.4 %all-to-all-done.3 = f32[512,2,128]{2,1,0:T(2,128)S(1)} async-done(((f32[512,2,128]{2,1,0:T(2,128)}), f32[512,2,128]{2,1,0:T(2,128)S(1)}, u32[]{:S(2)}, u32[]{:S(2)}) %all-to-all-start.3) | async-done | bytes 524320 | tf_op jit(solution)/shard_map/all_to_all | solution.py:347
  (36 shorter events, 3.8 us)
Async XLA Ops:
  0.6 39.6 %copy-start = (s32[1024,4]{0,1:T(4,128)S(1)}, s32[1024,4]{0,1:T(4,128)}, u32[]{:S(2)}) copy-start(s32[1024,4]{0,1:T(4,128)} %param.15) | copy-start | bytes 49156
  2.4 38.4 %all-to-all-start = ((bf16[512,2,128]{2,1,0:T(2,128)(2,1)}), bf16[512,2,128]{2,1,0:T(2,128)(2,1)S(1)}, u32[]{:S(2)}, u32[]{:S(2)}) async-start(bf16[512,2,128]{2,1,0:T(2,128)(2,1)} %bitcast.19), calls=%async_computation | async-start | bytes 524288 | tf_op jit(solution)/shard_map/all_to_all | solution.py:347
  29.6 29.3 %collective-permute-start = (bf16[2304,128]{1,0:T(8,128)(2,1)}, bf16[2304,128]{1,0:T(8,128)(2,1)S(1)}, u32[]{:S(2)}, u32[]{:S(2)}) collective-permute-start(bf16[2304,128]{1,0:T(8,128)(2,1)} %get-tuple-element.44), channel_id=1, source_target_pairs={{0,1},{1,2},{2,3},{3,0},{4,5},{5,6},{6,7},{7,4},{8,9},{9,10},{10,1... | collective-permute-start | bytes 1769480 | tf_op jit(solution)/shard_map/ppermute | solution.py:362
  32.9 29.3 %collective-permute-start.1 = (bf16[2304,128]{1,0:T(8,128)(2,1)}, bf16[2304,128]{1,0:T(8,128)(2,1)S(1)}, u32[]{:S(2)}, u32[]{:S(2)}) collective-permute-start(bf16[2304,128]{1,0:T(8,128)(2,1)} %get-tuple-element.45), channel_id=1, source_target_pairs={{0,2},{1,3},{2,0},{3,1},{4,6},{5,7},{6,4},{7,5},{8,10},{9,11},{10,... | collective-permute-start | bytes 1769480 | tf_op jit(solution)/shard_map/ppermute | solution.py:362
  37.2 25.3 %collective-permute-start.2 = (bf16[2304,128]{1,0:T(8,128)(2,1)}, bf16[2304,128]{1,0:T(8,128)(2,1)S(1)}, u32[]{:S(2)}, u32[]{:S(2)}) collective-permute-start(bf16[2304,128]{1,0:T(8,128)(2,1)} %get-tuple-element.46), channel_id=1, source_target_pairs={{0,3},{1,0},{2,1},{3,2},{4,7},{5,4},{6,5},{7,6},{8,11},{9,8},{10,9... | collective-permute-start | bytes 1769480 | tf_op jit(solution)/shard_map/ppermute | solution.py:362
  42.4 20.0 %copy-start.1 = (f32[8,512]{1,0:T(8,128)S(1)}, f32[8,512]{1,0:T(8,128)}, u32[]{:S(2)}) copy-start(f32[8,512]{1,0:T(8,128)} %refs_0_) | copy-start | bytes 49156
  42.4 20.0 %copy-start.2 = (f32[8,512]{1,0:T(8,128)S(1)}, f32[8,512]{1,0:T(8,128)}, u32[]{:S(2)}) copy-start(f32[8,512]{1,0:T(8,128)} %refs_1_) | copy-start | bytes 49156
  42.4 32.0 %all-to-all-start.1 = ((bf16[128,5,2,128]{3,2,1,0:T(2,128)(2,1)}), bf16[128,5,2,128]{3,2,1,0:T(2,128)(2,1)S(1)}, u32[]{:S(2)}, u32[]{:S(2)}) async-start(bf16[128,5,2,128]{3,2,1,0:T(2,128)(2,1)} %bitcast.5), calls=%async_computation.1 | async-start | bytes 655360 | tf_op jit(solution)/shard_map/all_to_all | solution.py:347
  58.9 15.5 %copy-start.5 = (bf16[2304,128]{1,0:T(8,128)(2,1)S(1)}, bf16[2304,128]{1,0:T(8,128)(2,1)}, u32[]{:S(2)}) copy-start(bf16[2304,128]{1,0:T(8,128)(2,1)} %get-tuple-element.47.refs_0_) | copy-start | bytes 1769476
  78.9 1.0 copy-start.3
  79.8 0.8 copy-start.6
  80.6 7.2 %copy-start.7 = (f32[4,2,128,128]{3,2,1,0:T(8,128)S(1)}, f32[4,2,128,128]{3,2,1,0:T(8,128)}, u32[]{:S(2)}) copy-start(f32[4,2,128,128]{3,2,1,0:T(8,128)} %copy-done.6) | copy-start | bytes 1572868
  80.6 29.6 %all-to-all-start.2 = ((f32[128,1,1280]{2,1,0:T(1,128)}), f32[128,1,1280]{2,1,0:T(1,128)S(1)}, u32[]{:S(2)}, u32[]{:S(2)}) async-start(f32[128,1,1280]{2,1,0:T(1,128)} %bitcast.7), calls=%async_computation.2 | async-start | bytes 1310720 | tf_op jit(solution)/shard_map/all_to_all | solution.py:347
  87.8 1.2 copy-start.4
  89.2 0.7 copy-start.8
  89.9 33.5 %collective-permute-start.3 = (bf16[1536,128]{1,0:T(8,128)(2,1)S(1)}, bf16[1536,128]{1,0:T(8,128)(2,1)S(1)}, u32[]{:S(2)}, u32[]{:S(2)}) collective-permute-start(bf16[1536,128]{1,0:T(8,128)(2,1)S(1)} %get-tuple-element.59), channel_id=1, source_target_pairs={{0,3},{1,0},{2,1},{3,2},{4,7},{5,4},{6,5},{7,6},{8,11},{9,8},{10,9... | collective-permute-start | bytes 1179656 | tf_op jit(solution)/shard_map/ppermute | solution.py:373
  92.2 31.2 %collective-permute-start.4 = (bf16[1536,128]{1,0:T(8,128)(2,1)S(1)}, bf16[1536,128]{1,0:T(8,128)(2,1)S(1)}, u32[]{:S(2)}, u32[]{:S(2)}) collective-permute-start(bf16[1536,128]{1,0:T(8,128)(2,1)S(1)} %get-tuple-element.60), channel_id=1, source_target_pairs={{0,2},{1,3},{2,0},{3,1},{4,6},{5,7},{6,4},{7,5},{8,10},{9,11},{10,... | collective-permute-start | bytes 1179656 | tf_op jit(solution)/shard_map/ppermute | solution.py:373
  95.8 27.6 %collective-permute-start.5 = (bf16[1536,128]{1,0:T(8,128)(2,1)S(1)}, bf16[1536,128]{1,0:T(8,128)(2,1)S(1)}, u32[]{:S(2)}, u32[]{:S(2)}) collective-permute-start(bf16[1536,128]{1,0:T(8,128)(2,1)S(1)} %get-tuple-element.61), channel_id=1, source_target_pairs={{0,1},{1,2},{2,3},{3,0},{4,5},{5,6},{6,7},{7,4},{8,9},{9,10},{10,1... | collective-permute-start | bytes 1179656 | tf_op jit(solution)/shard_map/ppermute | solution.py:373
  113.3 32.2 %all-to-all-start.3 = ((f32[512,2,128]{2,1,0:T(2,128)}), f32[512,2,128]{2,1,0:T(2,128)S(1)}, u32[]{:S(2)}, u32[]{:S(2)}) async-start(f32[512,2,128]{2,1,0:T(2,128)} %bitcast.9), calls=%async_computation.3 | async-start | bytes 1048576 | tf_op jit(solution)/shard_map/all_to_all | solution.py:347
  123.4 1.0 copy-start.9

commit v5 on v4

--- a/solution.py
+++ b/solution.py
@@ -54,33 +54,55 @@
     )(keys, values)
 
 
-def pack(head_ref, q_ref, g_ref, k_ref, v_ref, *out_refs):
-    tokens = q_ref.shape[0]
-    group = q_ref.shape[1] // SPLIT
+def pack(head_ref, *refs):
+    ins, outs, held, (part_ref, in_sems, out_sems) = refs[:4], refs[4:8], refs[8:12], refs[12:]
+    tokens = held[0].shape[0]
+    group = held[0].shape[1] // SPLIT
     rows = tokens * group
-    for k in range(SPLIT):
-        for to in range(SPLIT):
-
-            @pl.when(lax.rem(head_ref[0] + k, SPLIT) == to)
-            def _(k=k, to=to):
-                heads = slice(to * group, (to + 1) * group)
-                out_refs[k][:rows] = q_ref[:, heads, :].reshape(rows, WIDTH)
-                out_refs[k][rows : 2 * rows] = g_ref[:, heads, :].reshape(rows, WIDTH)
-                out_refs[k][2 * rows : 2 * rows + tokens] = k_ref[:, to, :]
-                out_refs[k][2 * rows + tokens :] = v_ref[:, to, :]
+    loads = [pltpu.make_async_copy(ins[i], held[i], in_sems.at[i]) for i in range(4)]
+    for load in loads:
+        load.start()
+    stores = []
+    start = 0
+    for i, width in enumerate((group, group, 1, 1)):
+        here = slice(start, start + tokens * width)
+        start = start + tokens * width
+        loads[i].wait()
+        for k in range(SPLIT):
+            for to in range(SPLIT):
+
+                @pl.when(lax.rem(head_ref[0] + k, SPLIT) == to)
+                def _(i=i, k=k, to=to, width=width, here=here):
+                    heads = slice(to * width, (to + 1) * width)
+                    part_ref[k, here] = held[i][:, heads, :].reshape(tokens * width, WIDTH)
+
+            stores.append(
+                pltpu.make_async_copy(part_ref.at[k, here], outs[k].at[here], out_sems.at[i, k])
+            )
+            stores[-1].start()
+    for store in stores:
+        store.wait()
 
 
 def packed(head, queries, grads, keys, values):
     tokens, heads, width = queries.shape
-    part = jax.ShapeDtypeStruct((2 * tokens * (heads // SPLIT + 1), width), jnp.bfloat16)
+    part = (2 * tokens * (heads // SPLIT + 1), width)
+    hbm = pl.BlockSpec(memory_space=pltpu.HBM)
+    arrays = (queries, grads, keys, values)
     return pl.pallas_call(
         pack,
-        in_specs=[pl.BlockSpec(memory_space=pltpu.SMEM)] + [pl.BlockSpec()] * 4,
-        out_specs=[pl.BlockSpec()] * SPLIT,
-        out_shape=[part] * SPLIT,
+        in_specs=[pl.BlockSpec(memory_space=pltpu.SMEM)] + [hbm] * 4,
+        out_specs=[hbm] * SPLIT,
+        out_shape=[jax.ShapeDtypeStruct(part, jnp.bfloat16)] * SPLIT,
+        scratch_shapes=[pltpu.VMEM(a.shape, a.dtype) for a in arrays]
+        + [
+            pltpu.VMEM((SPLIT,) + part, jnp.bfloat16),
+            pltpu.SemaphoreType.DMA((4,)),
+            pltpu.SemaphoreType.DMA((4, SPLIT)),
+        ],
         compiler_params=pltpu.CompilerParams(vmem_limit_bytes=WHOLE_VMEM),
         cost_estimate=SLOW,
-    )(head, queries, grads, keys, values)
+    )(head, *arrays)
 
 
 def spread(*refs):
@@ -291,42 +313,76 @@
     )(home, own)
 
 
-def pick_rows(index_ref, rows_ref, out_ref):
+def pick_rows(pairs_ref, rows_ref, out_ref, all_ref, far_ref, wide_ref):
     blocks = rows_ref.shape[0]
+    here = SPLIT * PAIR
+    askers = blocks // here
+    rows = rows_ref[...]
+    all_ref[...] = rows.astype(jnp.float32)
     chunk = 256
-    block_at = lax.broadcasted_iota(jnp.int32, (chunk, blocks), 1)
-    rows = rows_ref[...]
-    for start in range(0, out_ref.shape[0], chunk):
-        here = slice(start, start + chunk)
-        chosen = jnp.where(block_at == index_ref[here], 1.0, 0.0).astype(jnp.bfloat16)
-        out_ref[here] = dot(chosen, rows).astype(jnp.bfloat16)
-
-
-def gather_rows(index, rows):
+    block_at = lax.broadcasted_iota(jnp.int32, (blocks, chunk), 0)
+    for start in range(0, blocks, chunk):
+        chosen = jnp.where(block_at == pairs_ref[3:4, start : start + chunk], 1.0, 0.0)
+        far = dot(rows, chosen.astype(jnp.bfloat16), ((0,), (0,)))
+        far_ref[start : start + chunk] = far.T
+    for slot in range(here):
+        wide_ref[pl.ds(slot, askers, stride=SLOTS)] = far_ref[pl.ds(slot, askers, stride=here)]
+    first = all_ref[:1]
+    wide_ref[pl.ds(HUB, askers, stride=SLOTS)] = jnp.broadcast_to(first, (askers, WIDTH))
+    wide_ref[BEFORE : BEFORE + 1] = first
+    wide_ref[pl.ds(SLOTS + BEFORE, askers, stride=SLOTS)] = all_ref[pl.ds(here - 1, askers, stride=here)]
+    out_ref[...] = wide_ref[: askers * SLOTS].astype(jnp.bfloat16)
+
+
+def gather_rows(pairs, rows):
+    blocks = rows.shape[0]
+    asked = blocks // (SPLIT * PAIR) * SLOTS
     return pl.pallas_call(
         pick_rows,
-        out_shape=jax.ShapeDtypeStruct((index.shape[0], WIDTH), jnp.bfloat16),
-        compiler_params=pltpu.CompilerParams(vmem_limit_bytes=VMEM_BYTES),
-        cost_estimate=pl.CostEstimate(flops=5_000_000_000, bytes_accessed=15_000_000, transcendentals=0),
-    )(index, rows)
-
-
-def add_rows(index_ref, rows_ref, out_ref):
-    rows = rows_ref[...]
-    high, middle, low = three_parts(rows)
+        out_shape=jax.ShapeDtypeStruct((asked, WIDTH), jnp.bfloat16),
+        scratch_shapes=[
+            pltpu.VMEM((blocks, WIDTH), jnp.float32),
+            pltpu.VMEM((blocks, WIDTH), jnp.float32),
+            pltpu.VMEM((asked + 16, WIDTH), jnp.float32),
+        ],
+        compiler_params=pltpu.CompilerParams(vmem_limit_bytes=VMEM_BYTES),
+        cost_estimate=pl.CostEstimate(
+            flops=5_000_000_000, bytes_accessed=15_000_000, transcendentals=0
+        ),
+    )(pairs, rows)
+
+
+def add_rows(pairs_ref, rows_ref, out_ref, far_ref, shift_ref):
+    blocks = out_ref.shape[0]
+    here = SPLIT * PAIR
+    askers = blocks // here
+    for slot in range(here):
+        far_ref[pl.ds(slot, askers, stride=here)] = rows_ref[pl.ds(slot, askers, stride=SLOTS)]
+    high, middle, low = three_parts(far_ref[...])
+    hub = jnp.sum(rows_ref[pl.ds(HUB, askers, stride=SLOTS)], axis=0, keepdims=True)
     chunk = 256
-    for start in range(0, out_ref.shape[0], chunk):
-        block_at = lax.broadcasted_iota(jnp.int32, (chunk, rows.shape[0]), 0) + start
-        chosen = jnp.where(block_at == index_ref[...], 1.0, 0.0).astype(jnp.bfloat16)
+    for start in range(0, blocks, chunk):
+        block_at = lax.broadcasted_iota(jnp.int32, (chunk, blocks), 0) + start
+        chosen = jnp.where(block_at == pairs_ref[3:4, :], 1.0, 0.0).astype(jnp.bfloat16)
         out_ref[start : start + chunk] = dot(chosen, high) + dot(chosen, middle) + dot(chosen, low)
-
-
-def scatter_rows(index, rows, blocks):
+    out_ref[:1] = out_ref[:1] + hub
+    shift_ref[:askers] = rows_ref[pl.ds(BEFORE, askers, stride=SLOTS)]
+    shift_ref[askers:] = jnp.zeros((8, WIDTH), jnp.float32)
+    last = pl.ds(here - 1, askers, stride=here)
+    out_ref[last] = out_ref[last] + shift_ref[1 : askers + 1]
+
+
+def scatter_rows(pairs, rows, blocks):
+    askers = blocks // (SPLIT * PAIR)
     return pl.pallas_call(
         add_rows,
         out_shape=jax.ShapeDtypeStruct((blocks, WIDTH), jnp.float32),
-        compiler_params=pltpu.CompilerParams(vmem_limit_bytes=VMEM_BYTES),
-    )(index, rows)
+        scratch_shapes=[
+            pltpu.VMEM((blocks, WIDTH), jnp.float32),
+            pltpu.VMEM((askers + 8, WIDTH), jnp.float32),
+        ],
+        compiler_params=pltpu.CompilerParams(vmem_limit_bytes=VMEM_BYTES),
+    )(pairs, rows)
 
 
 def shards(
@@ -349,14 +405,11 @@
     pieces = interleaved(key_states.reshape(-1, width), value_states.reshape(-1, width))
     rows = exchange(pieces.reshape(devices, PAIR, width), AXES).reshape(blocks, width)
 
-    far = block_pairs[:, 3].reshape(shard_count, here)
-    before = jnp.maximum(here * jnp.arange(shard_count, dtype=jnp.int32) - 1, 0)
-    index = jnp.concatenate([far, jnp.zeros_like(before)[:, None], before[:, None]], axis=1)
     kinds = lax.dynamic_slice_in_dim(pair_kinds, rank * here, here, 0)
     later = lax.optimization_barrier((pieces, queries, out_grad, key_states, value_states))
     parts = packed(head_at, *later[1:])
-    index, *parts = lax.optimization_barrier((index, *parts))
-    got = exchange(gather_rows(index.reshape(-1, 1), rows).reshape(wire), "ctx")
+    pairs, *parts = lax.optimization_barrier((block_pairs.T, *parts))
+    got = exchange(gather_rows(pairs, rows).reshape(wire), "ctx")
 
     for k in range(1, SPLIT):
         parts[k] = lax.ppermute(parts[k], "head", [(i, (i + k) % SPLIT) for i in range(SPLIT)])
@@ -365,7 +418,7 @@
     dquery, own, sent = attention(head_at, kinds, parts, got.reshape(-1, width), logs, deltas)
 
     back = exchange(sent.reshape(shard_count, 1, SLOTS * width), "ctx")
-    sums = scatter_rows(index.reshape(1, -1), back.reshape(-1, width), blocks)
+    sums = scatter_rows(pairs, back.reshape(-1, width), blocks)
     home = exchange(sums.reshape(devices, PAIR, width), AXES)
 
     parts = list(packed_back(dquery, own))

time: 147 us -> 145 us (0.986)
  waiting for transfers between devices: 47 us -> 48.5 us
    all_to_all x4, starting transfers between devices: 55.8 us -> 54.1 us  [exchange(): return lax.all_to_all(array, axes, split_axis=0, concat_axis=0, tiled=True)]
    unnamed x21 -> x23, local copies, waits for them, and re-layouts: 4.84 us -> 4.84 us
  transfers between devices with their start and end apart: 10 -> 10, of which waited for: 5 -> 6; matrix products, arithmetic and copies ran while one was open for 1% -> 0% of each run, Pallas kernels for 7% -> 7%
where the time goes in v5:
time: 145 us; the launch traced here: 144 us
  starting transfers between devices  72.9 us (50%)
  waiting for transfers between devices  48.5 us (33%)
  Pallas kernels  16.8 us (12%)
  local copies, waits for them, and re-layouts  4.91 us (3%)
    all_to_all x4, starting transfers between devices, exchange(): return lax.all_to_all(array, axes, split_axis=0, concat_axis=0, tiled=True)  54.1 us
    all_to_all x4, waiting for transfers between devices, exchange(): return lax.all_to_all(array, axes, split_axis=0, concat_axis=0, tiled=True)  44.1 us
    ppermute x3, starting transfers between devices, shards(): lax.ppermute(parts[k], 'head', [(i, (i + k) % SPLIT) for i in range(SPLIT)])  10.7 us
    ppermute x3, starting transfers between devices, shards(): lax.ppermute(parts[k], 'head', [(i, (i - k) % SPLIT) for i in range(SPLIT)])  8.11 us
    unnamed x23, local copies, waits for them, and re-layouts  4.84 us
    pallas_call x1, Pallas kernels, attention(): pl.pallas_call(attend, in_specs=[smem, smem] + [vmem] * (SPLIT + 3), out_...  4.46 us
    ppermute x3, waiting for transfers between devices, shards(): lax.ppermute(parts[k], 'head', [(i, (i + k) % SPLIT) for i in range(SPLIT)])  4.34 us
    pallas_call x1, Pallas kernels, packed(): pl.pallas_call(pack, in_specs=[pl.BlockSpec(memory_space=pltpu.SMEM)] + [...  3.66 us
  transfers between devices with their start and end apart: 10, of which 6 were waited for; matrix products, arithmetic and copies ran while one was open for 0% of the time, Pallas kernels for 7%

profile of v5, /device:TPU:1, one launch (start us, length us, event | category | flops | bytes accessed | tf_op | source)
XLA Modules:
  0.0 144.0 jit_solution(14280833801372279941)
XLA Ops:
  0.6 1.7 %shard_map.103 = bf16[1024,128]{1,0:T(8,128)(2,1)} custom-call(bf16[512,128]{1,0:T(8,128)(2,1)} %bitcast.23, bf16[512,128]{1,0:T(8,128)(2,1)} %bitcast.24), custom_call_target="tpu_custom_call" | custom-call | tf_op jit(solution)/shard_map/pallas_call | solution.py:49
  2.4 22.2 %all-to-all-start = ((bf16[512,2,128]{2,1,0:T(2,128)(2,1)}), bf16[512,2,128]{2,1,0:T(2,128)(2,1)S(1)}, u32[]{:S(2)}, u32[]{:S(2)}) async-start(bf16[512,2,128]{2,1,0:T(2,128)(2,1)} %bitcast.22), calls=%async_computation | async-start | bytes 524288 | tf_op jit(solution)/shard_map/all_to_all | solution.py:403
  24.5 3.7 %shard_map.104 = (bf16[2304,128]{1,0:T(8,128)(2,1)}, bf16[2304,128]{1,0:T(8,128)(2,1)}, bf16[2304,128]{1,0:T(8,128)(2,1)}, bf16[2304,128]{1,0:T(8,128)(2,1)}) custom-call(s32[1]{0:T(128)} %bitcast.head_ref, bf16[128,32,128]{2,1,0:T(8,128)(2,1)} %refs_0_, bf16[128,32,128]{2,1,0:T(8,128)(2,1)} %refs_1_, bf16[128,4,128]{2,1,0:T(4,128)(2,1)} %refs_2_, ...), custom_call_target="tpu_custom_call" | custom-call | flops 20000000000 | bytes 60000000 | tf_op jit(solution)/shard_map/pallas_call | solution.py:92
  28.2 3.3 %collective-permute-start = (bf16[2304,128]{1,0:T(8,128)(2,1)}, bf16[2304,128]{1,0:T(8,128)(2,1)S(1)}, u32[]{:S(2)}, u32[]{:S(2)}) collective-permute-start(bf16[2304,128]{1,0:T(8,128)(2,1)} %get-tuple-element.44), channel_id=1, source_target_pairs={{0,1},{1,2},{2,3},{3,0},{4,5},{5,6},{6,7},{7,4},{8,9},{9,10},{10,1... | collective-permute-start | bytes 1769480 | tf_op jit(solution)/shard_map/ppermute | solution.py:415
  31.5 4.3 %collective-permute-start.1 = (bf16[2304,128]{1,0:T(8,128)(2,1)}, bf16[2304,128]{1,0:T(8,128)(2,1)S(1)}, u32[]{:S(2)}, u32[]{:S(2)}) collective-permute-start(bf16[2304,128]{1,0:T(8,128)(2,1)} %get-tuple-element.45), channel_id=1, source_target_pairs={{0,2},{1,3},{2,0},{3,1},{4,6},{5,7},{6,4},{7,5},{8,10},{9,11},{10,... | collective-permute-start | bytes 1769480 | tf_op jit(solution)/shard_map/ppermute | solution.py:415
  35.8 3.1 %collective-permute-start.2 = (bf16[2304,128]{1,0:T(8,128)(2,1)}, bf16[2304,128]{1,0:T(8,128)(2,1)S(1)}, u32[]{:S(2)}, u32[]{:S(2)}) collective-permute-start(bf16[2304,128]{1,0:T(8,128)(2,1)} %get-tuple-element.46), channel_id=1, source_target_pairs={{0,3},{1,0},{2,1},{3,2},{4,7},{5,4},{6,5},{7,6},{8,11},{9,8},{10,9... | collective-permute-start | bytes 1769480 | tf_op jit(solution)/shard_map/ppermute | solution.py:415
  39.1 1.7 %all-to-all-done = bf16[512,2,128]{2,1,0:T(2,128)(2,1)S(1)} async-done(((bf16[512,2,128]{2,1,0:T(2,128)(2,1)}), bf16[512,2,128]{2,1,0:T(2,128)(2,1)S(1)}, u32[]{:S(2)}, u32[]{:S(2)}) %all-to-all-start) | async-done | bytes 262176 | tf_op jit(solution)/shard_map/all_to_all | solution.py:403
  40.8 1.4 shard_map.105
  42.2 14.7 %all-to-all-start.1 = ((bf16[128,5,2,128]{3,2,1,0:T(2,128)(2,1)}), bf16[128,5,2,128]{3,2,1,0:T(2,128)(2,1)S(1)}, u32[]{:S(2)}, u32[]{:S(2)}) async-start(bf16[128,5,2,128]{3,2,1,0:T(2,128)(2,1)} %bitcast.6), calls=%async_computation.1 | async-start | bytes 655360 | tf_op jit(solution)/shard_map/all_to_all | solution.py:403
  57.0 4.2 %collective-permute-done.1.refs_2_ = bf16[2304,128]{1,0:T(8,128)(2,1)S(1)} collective-permute-done((bf16[2304,128]{1,0:T(8,128)(2,1)}, bf16[2304,128]{1,0:T(8,128)(2,1)S(1)}, u32[]{:S(2)}, u32[]{:S(2)}) %collective-permute-start.1) | collective-permute-done | bytes 589856 | tf_op jit(solution)/shard_map/ppermute | solution.py:415
  61.7 10.8 %all-to-all-done.1 = bf16[128,5,2,128]{3,2,1,0:T(2,128)(2,1)S(1)} async-done(((bf16[128,5,2,128]{3,2,1,0:T(2,128)(2,1)}), bf16[128,5,2,128]{3,2,1,0:T(2,128)(2,1)S(1)}, u32[]{:S(2)}, u32[]{:S(2)}) %all-to-all-start.1) | async-done | bytes 327712 | tf_op jit(solution)/shard_map/all_to_all | solution.py:403
  72.5 4.5 %shard_map.107 = (bf16[4,1024,128]{2,1,0:T(8,128)(2,1)S(1)}, f32[4,2,128,128]{3,2,1,0:T(8,128)S(1)}, f32[1280,128]{1,0:T(8,128)}) custom-call(s32[1]{0:T(128)} %bitcast.head_ref, s32[8,4]{1,0:T(8,128)S(1)} %copy.14.kinds, bf16[2304,128]{1,0:T(8,128)(2,1)S(1)} %copy-done.6, bf16[2304,128]{1,0:T(8,128)(2,1)S(1)} %collective-permute-done.refs_1_, ...), custom_call_target="tpu_custom_call" | custom-call | flops 1400000000 | bytes 8000000 | tf_op jit(solution)/shard_map/pallas_call | solution.py:217
  77.0 1.0 copy-done.4
  78.7 7.2 %all-to-all-start.2 = ((f32[128,1,1280]{2,1,0:T(1,128)}), f32[128,1,1280]{2,1,0:T(1,128)S(1)}, u32[]{:S(2)}, u32[]{:S(2)}) async-start(f32[128,1,1280]{2,1,0:T(1,128)} %bitcast.8), calls=%async_computation.2 | async-start | bytes 1310720 | tf_op jit(solution)/shard_map/all_to_all | solution.py:403
  85.9 1.2 copy-done.5
  88.0 2.8 %collective-permute-start.3 = (bf16[1536,128]{1,0:T(8,128)(2,1)S(1)}, bf16[1536,128]{1,0:T(8,128)(2,1)S(1)}, u32[]{:S(2)}, u32[]{:S(2)}) collective-permute-start(bf16[1536,128]{1,0:T(8,128)(2,1)S(1)} %get-tuple-element.59), channel_id=1, source_target_pairs={{0,3},{1,0},{2,1},{3,2},{4,7},{5,4},{6,5},{7,6},{8,11},{9,8},{10,9... | collective-permute-start | bytes 1179656 | tf_op jit(solution)/shard_map/ppermute | solution.py:426
  90.8 3.4 %collective-permute-start.4 = (bf16[1536,128]{1,0:T(8,128)(2,1)S(1)}, bf16[1536,128]{1,0:T(8,128)(2,1)S(1)}, u32[]{:S(2)}, u32[]{:S(2)}) collective-permute-start(bf16[1536,128]{1,0:T(8,128)(2,1)S(1)} %get-tuple-element.60), channel_id=1, source_target_pairs={{0,2},{1,3},{2,0},{3,1},{4,6},{5,7},{6,4},{7,5},{8,10},{9,11},{10,... | collective-permute-start | bytes 1179656 | tf_op jit(solution)/shard_map/ppermute | solution.py:426
  94.2 1.9 %collective-permute-start.5 = (bf16[1536,128]{1,0:T(8,128)(2,1)S(1)}, bf16[1536,128]{1,0:T(8,128)(2,1)S(1)}, u32[]{:S(2)}, u32[]{:S(2)}) collective-permute-start(bf16[1536,128]{1,0:T(8,128)(2,1)S(1)} %get-tuple-element.61), channel_id=1, source_target_pairs={{0,1},{1,2},{2,3},{3,0},{4,5},{5,6},{6,7},{7,4},{8,9},{9,10},{10,1... | collective-permute-start | bytes 1179656 | tf_op jit(solution)/shard_map/ppermute | solution.py:426
  96.2 12.2 %all-to-all-done.2 = f32[128,1,1280]{2,1,0:T(1,128)S(1)} async-done(((f32[128,1,1280]{2,1,0:T(1,128)}), f32[128,1,1280]{2,1,0:T(1,128)S(1)}, u32[]{:S(2)}, u32[]{:S(2)}) %all-to-all-start.2) | async-done | bytes 655392 | tf_op jit(solution)/shard_map/all_to_all | solution.py:403
  108.3 2.8 %shard_map.110 = f32[1024,128]{1,0:T(8,128)} custom-call(s32[4,1024]{1,0:T(4,128)S(1)} %bitcast.21, f32[1280,128]{1,0:T(8,128)S(1)} %bitcast.15), custom_call_target="tpu_custom_call" | custom-call | tf_op jit(solution)/shard_map/pallas_call | solution.py:377
  111.1 10.1 %all-to-all-start.3 = ((f32[512,2,128]{2,1,0:T(2,128)}), f32[512,2,128]{2,1,0:T(2,128)S(1)}, u32[]{:S(2)}, u32[]{:S(2)}) async-start(f32[512,2,128]{2,1,0:T(2,128)} %bitcast.10), calls=%async_computation.3 | async-start | bytes 1048576 | tf_op jit(solution)/shard_map/all_to_all | solution.py:403
  121.2 1.0 copy-done.10
  122.2 1.6 %shard_map.109 = (bf16[128,32,128]{2,1,0:T(8,128)(2,1)}, f32[2,128,4,128]{3,2,1,0:T(4,128)S(1)}) custom-call(s32[1]{0:T(128)} %bitcast.head_ref, bf16[1536,128]{1,0:T(8,128)(2,1)S(1)} %copy-done.10, bf16[1536,128]{1,0:T(8,128)(2,1)S(1)} %collective-permute-done.3.refs_1_, bf16[1536,128]{1,0:T(8,128)(2,1)S(1)} %collective-permute-done.4.refs_2_, ...), custom_call_target="tpu_custom_call" | custom-call | flops 20000000000 | bytes 60000000 | tf_op jit(solution)/shard_map/pallas_call | solution.py:283
  123.8 19.4 %all-to-all-done.3 = f32[512,2,128]{2,1,0:T(2,128)S(1)} async-done(((f32[512,2,128]{2,1,0:T(2,128)}), f32[512,2,128]{2,1,0:T(2,128)S(1)}, u32[]{:S(2)}, u32[]{:S(2)}) %all-to-all-start.3) | async-done | bytes 524320 | tf_op jit(solution)/shard_map/all_to_all | solution.py:403
  (29 shorter events, 3.1 us)
Async XLA Ops:
  0.6 38.3 %copy-start = (s32[1024,4]{0,1:T(4,128)S(1)}, s32[1024,4]{0,1:T(4,128)}, u32[]{:S(2)}) copy-start(s32[1024,4]{0,1:T(4,128)} %param.15) | copy-start | bytes 49156
  2.4 38.4 %all-to-all-start = ((bf16[512,2,128]{2,1,0:T(2,128)(2,1)}), bf16[512,2,128]{2,1,0:T(2,128)(2,1)S(1)}, u32[]{:S(2)}, u32[]{:S(2)}) async-start(bf16[512,2,128]{2,1,0:T(2,128)(2,1)} %bitcast.22), calls=%async_computation | async-start | bytes 524288 | tf_op jit(solution)/shard_map/all_to_all | solution.py:403
  28.2 12.6 %copy-start.1 = (s32[1024,4]{0,1:T(4,128)S(1)}, s32[1024,4]{0,1:T(4,128)}, u32[]{:S(2)}) copy-start(s32[1024,4]{0,1:T(4,128)} %param.14) | copy-start | bytes 49156
  28.2 28.8 %collective-permute-start = (bf16[2304,128]{1,0:T(8,128)(2,1)}, bf16[2304,128]{1,0:T(8,128)(2,1)S(1)}, u32[]{:S(2)}, u32[]{:S(2)}) collective-permute-start(bf16[2304,128]{1,0:T(8,128)(2,1)} %get-tuple-element.44), channel_id=1, source_target_pairs={{0,1},{1,2},{2,3},{3,0},{4,5},{5,6},{6,7},{7,4},{8,9},{9,10},{10,1... | collective-permute-start | bytes 1769480 | tf_op jit(solution)/shard_map/ppermute | solution.py:415
  31.5 29.6 %collective-permute-start.1 = (bf16[2304,128]{1,0:T(8,128)(2,1)}, bf16[2304,128]{1,0:T(8,128)(2,1)S(1)}, u32[]{:S(2)}, u32[]{:S(2)}) collective-permute-start(bf16[2304,128]{1,0:T(8,128)(2,1)} %get-tuple-element.45), channel_id=1, source_target_pairs={{0,2},{1,3},{2,0},{3,1},{4,6},{5,7},{6,4},{7,5},{8,10},{9,11},{10,... | collective-permute-start | bytes 1769480 | tf_op jit(solution)/shard_map/ppermute | solution.py:415
  35.8 25.5 %collective-permute-start.2 = (bf16[2304,128]{1,0:T(8,128)(2,1)}, bf16[2304,128]{1,0:T(8,128)(2,1)S(1)}, u32[]{:S(2)}, u32[]{:S(2)}) collective-permute-start(bf16[2304,128]{1,0:T(8,128)(2,1)} %get-tuple-element.46), channel_id=1, source_target_pairs={{0,3},{1,0},{2,1},{3,2},{4,7},{5,4},{6,5},{7,6},{8,11},{9,8},{10,9... | collective-permute-start | bytes 1769480 | tf_op jit(solution)/shard_map/ppermute | solution.py:415
  42.2 19.1 %copy-start.2 = (f32[8,512]{1,0:T(8,128)S(1)}, f32[8,512]{1,0:T(8,128)}, u32[]{:S(2)}) copy-start(f32[8,512]{1,0:T(8,128)} %refs_0_.1) | copy-start | bytes 49156
  42.2 19.1 %copy-start.3 = (f32[8,512]{1,0:T(8,128)S(1)}, f32[8,512]{1,0:T(8,128)}, u32[]{:S(2)}) copy-start(f32[8,512]{1,0:T(8,128)} %refs_1_.1) | copy-start | bytes 49156
  42.2 30.3 %all-to-all-start.1 = ((bf16[128,5,2,128]{3,2,1,0:T(2,128)(2,1)}), bf16[128,5,2,128]{3,2,1,0:T(2,128)(2,1)S(1)}, u32[]{:S(2)}, u32[]{:S(2)}) async-start(bf16[128,5,2,128]{3,2,1,0:T(2,128)(2,1)} %bitcast.6), calls=%async_computation.1 | async-start | bytes 655360 | tf_op jit(solution)/shard_map/all_to_all | solution.py:403
  57.0 15.5 %copy-start.6 = (bf16[2304,128]{1,0:T(8,128)(2,1)S(1)}, bf16[2304,128]{1,0:T(8,128)(2,1)}, u32[]{:S(2)}) copy-start(bf16[2304,128]{1,0:T(8,128)(2,1)} %get-tuple-element.47.refs_0_) | copy-start | bytes 1769476
  77.0 1.0 copy-start.4
  77.9 0.8 copy-start.7
  78.7 7.2 %copy-start.8 = (f32[4,2,128,128]{3,2,1,0:T(8,128)S(1)}, f32[4,2,128,128]{3,2,1,0:T(8,128)}, u32[]{:S(2)}) copy-start(f32[4,2,128,128]{3,2,1,0:T(8,128)} %copy-done.7) | copy-start | bytes 1572868
  78.7 29.6 %all-to-all-start.2 = ((f32[128,1,1280]{2,1,0:T(1,128)}), f32[128,1,1280]{2,1,0:T(1,128)S(1)}, u32[]{:S(2)}, u32[]{:S(2)}) async-start(f32[128,1,1280]{2,1,0:T(1,128)} %bitcast.8), calls=%async_computation.2 | async-start | bytes 1310720 | tf_op jit(solution)/shard_map/all_to_all | solution.py:403
  85.9 1.2 copy-start.5
  87.3 0.7 copy-start.9
  88.0 33.2 %collective-permute-start.3 = (bf16[1536,128]{1,0:T(8,128)(2,1)S(1)}, bf16[1536,128]{1,0:T(8,128)(2,1)S(1)}, u32[]{:S(2)}, u32[]{:S(2)}) collective-permute-start(bf16[1536,128]{1,0:T(8,128)(2,1)S(1)} %get-tuple-element.59), channel_id=1, source_target_pairs={{0,3},{1,0},{2,1},{3,2},{4,7},{5,4},{6,5},{7,6},{8,11},{9,8},{10,9... | collective-permute-start | bytes 1179656 | tf_op jit(solution)/shard_map/ppermute | solution.py:426
  90.8 30.4 %collective-permute-start.4 = (bf16[1536,128]{1,0:T(8,128)(2,1)S(1)}, bf16[1536,128]{1,0:T(8,128)(2,1)S(1)}, u32[]{:S(2)}, u32[]{:S(2)}) collective-permute-start(bf16[1536,128]{1,0:T(8,128)(2,1)S(1)} %get-tuple-element.60), channel_id=1, source_target_pairs={{0,2},{1,3},{2,0},{3,1},{4,6},{5,7},{6,4},{7,5},{8,10},{9,11},{10,... | collective-permute-start | bytes 1179656 | tf_op jit(solution)/shard_map/ppermute | solution.py:426
  94.2 27.0 %collective-permute-start.5 = (bf16[1536,128]{1,0:T(8,128)(2,1)S(1)}, bf16[1536,128]{1,0:T(8,128)(2,1)S(1)}, u32[]{:S(2)}, u32[]{:S(2)}) collective-permute-start(bf16[1536,128]{1,0:T(8,128)(2,1)S(1)} %get-tuple-element.61), channel_id=1, source_target_pairs={{0,1},{1,2},{2,3},{3,0},{4,5},{5,6},{6,7},{7,4},{8,9},{9,10},{10,1... | collective-permute-start | bytes 1179656 | tf_op jit(solution)/shard_map/ppermute | solution.py:426
  111.1 32.1 %all-to-all-start.3 = ((f32[512,2,128]{2,1,0:T(2,128)}), f32[512,2,128]{2,1,0:T(2,128)S(1)}, u32[]{:S(2)}, u32[]{:S(2)}) async-start(f32[512,2,128]{2,1,0:T(2,128)} %bitcast.10), calls=%async_computation.3 | async-start | bytes 1048576 | tf_op jit(solution)/shard_map/all_to_all | solution.py:403
  121.2 1.0 copy-start.10

commit v6 on v5

--- a/solution.py
+++ b/solution.py
@@ -12,6 +12,7 @@
 PAIR = 2
 SLOTS = SPLIT * PAIR + 2
 HUB, BEFORE = SLOTS - 2, SLOTS - 1
+SPARE = 16
 VMEM_BYTES = 20 * 1024 * 1024
 WHOLE_VMEM = 60 * 1024 * 1024
 SLOW = pl.CostEstimate(flops=20_000_000_000, bytes_accessed=60_000_000, transcendentals=0)
@@ -35,13 +36,13 @@
 
 
 def interleave(k_ref, v_ref, pieces_ref, wide_ref):
-    half = wide_ref.shape[0] // 4
+    half = pieces_ref.shape[0] // 4
     for kv, ref in enumerate((k_ref, v_ref)):
         wide = ref[...].astype(jnp.float32)
         for blk in range(PAIR):
             start = 2 * kv * half + blk
             wide_ref[pl.ds(start, half, stride=PAIR)] = wide[blk * half : (blk + 1) * half]
-    pieces_ref[...] = wide_ref[...].astype(jnp.bfloat16)
+    pieces_ref[...] = wide_ref[: pieces_ref.shape[0]].astype(jnp.bfloat16)
 
 
 def interleaved(keys, values):
@@ -49,7 +50,7 @@
     return pl.pallas_call(
         interleave,
         out_shape=jax.ShapeDtypeStruct(both, jnp.bfloat16),
-        scratch_shapes=[pltpu.VMEM(both, jnp.float32)],
+        scratch_shapes=[pltpu.VMEM((both[0] + SPARE, WIDTH), jnp.float32)],
         compiler_params=pltpu.CompilerParams(vmem_limit_bytes=WHOLE_VMEM),
     )(keys, values)
 
@@ -68,14 +69,17 @@
         here = slice(start, start + tokens * width)
         start = start + tokens * width
         loads[i].wait()
+        for head in range(SPLIT):
+
+            @pl.when(head_ref[0] == head)
+            def _(i=i, head=head, width=width, here=here):
+                whole = held[i][...]
+                for k in range(SPLIT):
+                    to = (head + k) % SPLIT
+                    part = whole[:, to * width : (to + 1) * width, :]
+                    part_ref[k, here] = part.reshape(tokens * width, WIDTH)
+
         for k in range(SPLIT):
-            for to in range(SPLIT):
-
-                @pl.when(lax.rem(head_ref[0] + k, SPLIT) == to)
-                def _(i=i, k=k, to=to, width=width, here=here):
-                    heads = slice(to * width, (to + 1) * width)
-                    part_ref[k, here] = held[i][:, heads, :].reshape(tokens * width, WIDTH)
-
             stores.append(
                 pltpu.make_async_copy(part_ref.at[k, here], outs[k].at[here], out_sems.at[i, k])
             )
@@ -138,9 +142,9 @@
 
 
 def attend(head_ref, kinds, *refs):
-    parts, (got_ref, log_ref, delta_ref), (dq_ref, own_ref, sent_ref) = refs[:4], refs[4:7], refs[7:10]
-    wide_ref = refs[10]
-    wide_ref[...] = got_ref[...].astype(jnp.float32)
+    parts, (got_ref, log_ref, delta_ref), (*backs, sent_ref) = refs[:4], refs[4:7], refs[7:12]
+    wide_ref, held_ref = refs[12:]
+    wide_ref[: got_ref.shape[0]] = got_ref[...].astype(jnp.float32)
     tokens = PAIR * BLOCK
     group = (parts[0].shape[0] - 2 * tokens) // (2 * tokens)
     rows = BLOCK * group
@@ -186,7 +190,7 @@
             dvalue = dot(weights.astype(jnp.bfloat16), grads)
             dkey = dot(dscore, queries) * scale
             dquery = dot(dscore, keys, ((0,), (0,))) * scale
-            dq_ref[k, blk * rows : (blk + 1) * rows] = dquery.astype(jnp.bfloat16)
+            backs[k][blk * rows : (blk + 1) * rows] = dquery.astype(jnp.bfloat16)
             terms[k, blk] = (dkey, dvalue)
     for kv in range(2):
 
@@ -197,16 +201,22 @@
         outside = 0.0
         for k in range(SPLIT):
             for blk in range(PAIR):
-                sent_ref[strided(owner[k] * PAIR + blk, kv)] = piece(k, blk, 3)
+                held_ref[strided(owner[k] * PAIR + blk, kv)] = piece(k, blk, 3)
                 hub = hub + piece(k, blk, 2)
             outside = outside + jnp.where(owner[k] == 0, piece(k, 0, 1), 0.0)
             later = (k + SPLIT - 1) % SPLIT
-            own_ref[k, kv, :BLOCK] = piece(k, 0, 0) + piece(k, 1, 1)
-            own_ref[k, kv, BLOCK:] = piece(k, 1, 0) + jnp.where(
-                owner[later] == 0, 0.0, piece(later, 0, 1)
-            )
-        sent_ref[strided(HUB, kv)] = hub
-        sent_ref[strided(BEFORE, kv)] = outside
+            first = piece(k, 0, 0) + piece(k, 1, 1)
+            second = piece(k, 1, 0) + jnp.where(owner[later] == 0, 0.0, piece(later, 0, 1))
+            for blk, total in enumerate((first, second)):
+                high = total.astype(jnp.bfloat16)
+                low = (total - high.astype(jnp.float32)).astype(jnp.bfloat16)
+                start = tokens * group + kv * tokens + blk * BLOCK
+                backs[k][start : start + BLOCK] = high
+                start = start + 2 * tokens
+                backs[k][start : start + BLOCK] = low
+        held_ref[strided(HUB, kv)] = hub
+        held_ref[strided(BEFORE, kv)] = outside
+    sent_ref[...] = held_ref[: sent_ref.shape[0]]
 
 
 def attention(head, kinds, parts, got, logs, deltas):
@@ -217,45 +227,15 @@
     return pl.pallas_call(
         attend,
         in_specs=[smem, smem] + [vmem] * (SPLIT + 3),
-        out_specs=[vmem] * 3,
-        out_shape=[
-            jax.ShapeDtypeStruct((SPLIT, tokens * group, WIDTH), jnp.bfloat16),
-            jax.ShapeDtypeStruct((SPLIT, 2, tokens, WIDTH), jnp.float32),
-            jax.ShapeDtypeStruct(got.shape, jnp.float32),
-        ],
-        scratch_shapes=[pltpu.VMEM(got.shape, jnp.float32)],
+        out_specs=[vmem] * (SPLIT + 1),
+        out_shape=[jax.ShapeDtypeStruct((tokens * group + 4 * tokens, WIDTH), jnp.bfloat16)] * SPLIT
+        + [jax.ShapeDtypeStruct(got.shape, jnp.float32)],
+        scratch_shapes=[pltpu.VMEM((got.shape[0] + SPARE, WIDTH), jnp.float32)] * 2,
         compiler_params=pltpu.CompilerParams(vmem_limit_bytes=VMEM_BYTES),
         cost_estimate=pl.CostEstimate(
             flops=1_400_000_000, bytes_accessed=8_000_000, transcendentals=1_000_000
         ),
     )(head, kinds, *parts, got, logs, deltas)
-
-
-def pack_back(dq_ref, own_ref, *out_refs):
-    rows, tokens = dq_ref.shape[1], own_ref.shape[2]
-    for k in range(SPLIT):
-        out_refs[k][:rows] = dq_ref[k]
-        for kv in range(2):
-            total = own_ref[k, kv]
-            high = total.astype(jnp.bfloat16)
-            low = (total - high.astype(jnp.float32)).astype(jnp.bfloat16)
-            start = rows + kv * tokens
-            out_refs[k][start : start + tokens] = high
-            start = start + 2 * tokens
-            out_refs[k][start : start + tokens] = low
-
-
-def packed_back(dquery, own):
-    part = jax.ShapeDtypeStruct((dquery.shape[1] + 4 * own.shape[2], WIDTH), jnp.bfloat16)
-    vmem = pl.BlockSpec(memory_space=pltpu.VMEM)
-    return pl.pallas_call(
-        pack_back,
-        in_specs=[vmem] * 2,
-        out_specs=[vmem] * SPLIT,
-        out_shape=[part] * SPLIT,
-        compiler_params=pltpu.CompilerParams(vmem_limit_bytes=VMEM_BYTES),
-        cost_estimate=SLOW,
-    )(dquery, own)
 
 
 def unpack(head_ref, *refs):
@@ -263,18 +243,21 @@
     tokens = dq_ref.shape[0]
     group = dq_ref.shape[1] // SPLIT
     rows = tokens * group
-    for k in range(SPLIT):
-        for source in range(SPLIT):
-
-            @pl.when(lax.rem(head_ref[0] + k, SPLIT) == source)
-            def _(k=k, source=source):
-                heads = slice(source * group, (source + 1) * group)
-                dq_ref[:, heads, :] = parts[k][:rows].reshape(tokens, group, WIDTH)
+    for head in range(SPLIT):
+
+        @pl.when(head_ref[0] == head)
+        def _(head=head):
+            senders = [parts[(source - head) % SPLIT] for source in range(SPLIT)]
+            for source in range(0, SPLIT, 2):
+                pair = [senders[source + i][:rows].reshape(tokens, group, WIDTH) for i in range(2)]
+                heads = slice(source * group, (source + 2) * group)
+                dq_ref[:, heads, :] = jnp.concatenate(pair, axis=1)
+            for source, sender in enumerate(senders):
                 for kv in range(2):
                     start = rows + kv * tokens
-                    high = parts[k][start : start + tokens].astype(jnp.float32)
+                    high = sender[start : start + tokens].astype(jnp.float32)
                     start = start + 2 * tokens
-                    low = parts[k][start : start + tokens].astype(jnp.float32)
+                    low = sender[start : start + tokens].astype(jnp.float32)
                     own_ref[kv, :, source, :] = high + low
 
 
@@ -318,7 +301,7 @@
     here = SPLIT * PAIR
     askers = blocks // here
     rows = rows_ref[...]
-    all_ref[...] = rows.astype(jnp.float32)
+    all_ref[:blocks] = rows.astype(jnp.float32)
     chunk = 256
     block_at = lax.broadcasted_iota(jnp.int32, (blocks, chunk), 0)
     for start in range(0, blocks, chunk):
@@ -341,9 +324,9 @@
         pick_rows,
         out_shape=jax.ShapeDtypeStruct((asked, WIDTH), jnp.bfloat16),
         scratch_shapes=[
-            pltpu.VMEM((blocks, WIDTH), jnp.float32),
-            pltpu.VMEM((blocks, WIDTH), jnp.float32),
-            pltpu.VMEM((asked + 16, WIDTH), jnp.float32),
+            pltpu.VMEM((blocks + SPARE, WIDTH), jnp.float32),
+            pltpu.VMEM((blocks + SPARE, WIDTH), jnp.float32),
+            pltpu.VMEM((asked + 2 * SPARE, WIDTH), jnp.float32),
         ],
         compiler_params=pltpu.CompilerParams(vmem_limit_bytes=VMEM_BYTES),
         cost_estimate=pl.CostEstimate(
@@ -352,19 +335,34 @@
     )(pairs, rows)
 
 
-def add_rows(pairs_ref, rows_ref, out_ref, far_ref, shift_ref):
+def mark(pairs_ref, out_ref):
+    blocks = out_ref.shape[0]
+    chunk = 256
+    for start in range(0, blocks, chunk):
+        block_at = lax.broadcasted_iota(jnp.int32, (chunk, blocks), 0) + start
+        chosen = jnp.where(block_at == pairs_ref[3:4, :], 1.0, 0.0)
+        out_ref[start : start + chunk] = chosen.astype(jnp.bfloat16)
+
+
+def marked(pairs):
+    return pl.pallas_call(
+        mark,
+        out_shape=jax.ShapeDtypeStruct((pairs.shape[1], pairs.shape[1]), jnp.bfloat16),
+        compiler_params=pltpu.CompilerParams(vmem_limit_bytes=VMEM_BYTES),
+        cost_estimate=SLOW,
+    )(pairs)
+
+
+def add_rows(chosen_ref, rows_ref, out_ref, far_ref, shift_ref):
     blocks = out_ref.shape[0]
     here = SPLIT * PAIR
     askers = blocks // here
     for slot in range(here):
         far_ref[pl.ds(slot, askers, stride=here)] = rows_ref[pl.ds(slot, askers, stride=SLOTS)]
-    high, middle, low = three_parts(far_ref[...])
+    parts = jnp.concatenate(three_parts(far_ref[:blocks]), axis=1)
     hub = jnp.sum(rows_ref[pl.ds(HUB, askers, stride=SLOTS)], axis=0, keepdims=True)
-    chunk = 256
-    for start in range(0, blocks, chunk):
-        block_at = lax.broadcasted_iota(jnp.int32, (chunk, blocks), 0) + start
-        chosen = jnp.where(block_at == pairs_ref[3:4, :], 1.0, 0.0).astype(jnp.bfloat16)
-        out_ref[start : start + chunk] = dot(chosen, high) + dot(chosen, middle) + dot(chosen, low)
+    sums = dot(chosen_ref[...], parts)
+    out_ref[...] = sums[:, :WIDTH] + sums[:, WIDTH : 2 * WIDTH] + sums[:, 2 * WIDTH :]
     out_ref[:1] = out_ref[:1] + hub
     shift_ref[:askers] = rows_ref[pl.ds(BEFORE, askers, stride=SLOTS)]
     shift_ref[askers:] = jnp.zeros((8, WIDTH), jnp.float32)
@@ -372,17 +370,17 @@
     out_ref[last] = out_ref[last] + shift_ref[1 : askers + 1]
 
 
-def scatter_rows(pairs, rows, blocks):
+def scatter_rows(chosen, rows, blocks):
     askers = blocks // (SPLIT * PAIR)
     return pl.pallas_call(
         add_rows,
         out_shape=jax.ShapeDtypeStruct((blocks, WIDTH), jnp.float32),
         scratch_shapes=[
-            pltpu.VMEM((blocks, WIDTH), jnp.float32),
+            pltpu.VMEM((blocks + SPARE, WIDTH), jnp.float32),
             pltpu.VMEM((askers + 8, WIDTH), jnp.float32),
         ],
         compiler_params=pltpu.CompilerParams(vmem_limit_bytes=VMEM_BYTES),
-    )(pairs, rows)
+    )(chosen, rows)
 
 
 def shards(
@@ -411,17 +409,17 @@
     pairs, *parts = lax.optimization_barrier((block_pairs.T, *parts))
     got = exchange(gather_rows(pairs, rows).reshape(wire), "ctx")
 
-    for k in range(1, SPLIT):
+    for k in (2, 1, 3):
         parts[k] = lax.ppermute(parts[k], "head", [(i, (i + k) % SPLIT) for i in range(SPLIT)])
     log_sums, row_deltas, *parts = lax.optimization_barrier((log_sums, row_deltas, *parts))
     logs, deltas = spread_rows(log_sums, row_deltas)
-    dquery, own, sent = attention(head_at, kinds, parts, got.reshape(-1, width), logs, deltas)
+    *parts, sent = attention(head_at, kinds, parts, got.reshape(-1, width), logs, deltas)
 
     back = exchange(sent.reshape(shard_count, 1, SLOTS * width), "ctx")
-    sums = scatter_rows(pairs, back.reshape(-1, width), blocks)
+    pairs, parts[0] = lax.optimization_barrier((pairs, parts[0]))
+    sums = scatter_rows(marked(pairs), back.reshape(-1, width), blocks)
     home = exchange(sums.reshape(devices, PAIR, width), AXES)
 
-    parts = list(packed_back(dquery, own))
     for k in range(1, SPLIT):
         parts[k] = lax.ppermute(parts[k], "head", [(i, (i - k) % SPLIT) for i in range(SPLIT)])
     dquery, own = unpacked(head_at, parts, queries, key_states)

time: 145 us -> 143 us (0.986)
    unnamed x23 -> x21, local copies, waits for them, and re-layouts: 4.84 us -> 3.9 us
where the time goes in v6:
time: 143 us; the launch traced here: 142 us
  starting transfers between devices  72.8 us (51%)
  waiting for transfers between devices  47.7 us (33%)
  Pallas kernels  17 us (12%)
  local copies, waits for them, and re-layouts  3.98 us (3%)
    all_to_all x4, starting transfers between devices, exchange(): return lax.all_to_all(array, axes, split_axis=0, concat_axis=0, tiled=True)  53.3 us
    all_to_all x4, waiting for transfers between devices, exchange(): return lax.all_to_all(array, axes, split_axis=0, concat_axis=0, tiled=True)  43.1 us
    ppermute x3, starting transfers between devices, shards(): lax.ppermute(parts[k], 'head', [(i, (i + k) % SPLIT) for i in range(SPLIT)])  10.7 us
    ppermute x3, starting transfers between devices, shards(): lax.ppermute(parts[k], 'head', [(i, (i - k) % SPLIT) for i in range(SPLIT)])  8.86 us
    ppermute x3, waiting for transfers between devices, shards(): lax.ppermute(parts[k], 'head', [(i, (i + k) % SPLIT) for i in range(SPLIT)])  4.62 us
    pallas_call x1, Pallas kernels, attention(): pl.pallas_call(attend, in_specs=[smem, smem] + [vmem] * (SPLIT + 3), out_...  4.53 us
    unnamed x21, local copies, waits for them, and re-layouts  3.9 us
    pallas_call x1, Pallas kernels, packed(): pl.pallas_call(pack, in_specs=[pl.BlockSpec(memory_space=pltpu.SMEM)] + [...  3.01 us
  transfers between devices with their start and end apart: 10, of which 6 were waited for; matrix products, arithmetic and copies ran while one was open for 0% of the time, Pallas kernels for 7%

profile of v6, /device:TPU:1, one launch (start us, length us, event | category | flops | bytes accessed | tf_op | source)
XLA Modules:
  0.0 142.3 jit_solution(7524926403834324816)
XLA Ops:
  0.6 1.7 %shard_map.103 = bf16[1024,128]{1,0:T(8,128)(2,1)} custom-call(bf16[512,128]{1,0:T(8,128)(2,1)} %bitcast.23, bf16[512,128]{1,0:T(8,128)(2,1)} %bitcast.24), custom_call_target="tpu_custom_call" | custom-call | tf_op jit(solution)/shard_map/pallas_call | solution.py:50
  2.4 22.2 %all-to-all-start = ((bf16[512,2,128]{2,1,0:T(2,128)(2,1)}), bf16[512,2,128]{2,1,0:T(2,128)(2,1)S(1)}, u32[]{:S(2)}, u32[]{:S(2)}) async-start(bf16[512,2,128]{2,1,0:T(2,128)(2,1)} %bitcast.22), calls=%async_computation | async-start | bytes 524288 | tf_op jit(solution)/shard_map/all_to_all | solution.py:401
  24.6 3.0 %shard_map.104 = (bf16[2304,128]{1,0:T(8,128)(2,1)}, bf16[2304,128]{1,0:T(8,128)(2,1)}, bf16[2304,128]{1,0:T(8,128)(2,1)}, bf16[2304,128]{1,0:T(8,128)(2,1)}) custom-call(s32[1]{0:T(128)} %bitcast.head_ref, bf16[128,32,128]{2,1,0:T(8,128)(2,1)} %refs_0_, bf16[128,32,128]{2,1,0:T(8,128)(2,1)} %refs_1_, bf16[128,4,128]{2,1,0:T(4,128)(2,1)} %refs_2_, ...), custom_call_target="tpu_custom_call" | custom-call | flops 20000000000 | bytes 60000000 | tf_op jit(solution)/shard_map/pallas_call | solution.py:96
  27.6 3.3 %collective-permute-start = (bf16[2304,128]{1,0:T(8,128)(2,1)}, bf16[2304,128]{1,0:T(8,128)(2,1)S(1)}, u32[]{:S(2)}, u32[]{:S(2)}) collective-permute-start(bf16[2304,128]{1,0:T(8,128)(2,1)} %get-tuple-element.45), channel_id=1, source_target_pairs={{0,1},{1,2},{2,3},{3,0},{4,5},{5,6},{6,7},{7,4},{8,9},{9,10},{10,1... | collective-permute-start | bytes 1769480 | tf_op jit(solution)/shard_map/ppermute | solution.py:413
  30.9 4.3 %collective-permute-start.1 = (bf16[2304,128]{1,0:T(8,128)(2,1)}, bf16[2304,128]{1,0:T(8,128)(2,1)S(1)}, u32[]{:S(2)}, u32[]{:S(2)}) collective-permute-start(bf16[2304,128]{1,0:T(8,128)(2,1)} %get-tuple-element.46), channel_id=1, source_target_pairs={{0,2},{1,3},{2,0},{3,1},{4,6},{5,7},{6,4},{7,5},{8,10},{9,11},{10,... | collective-permute-start | bytes 1769480 | tf_op jit(solution)/shard_map/ppermute | solution.py:413
  35.2 3.1 %collective-permute-start.2 = (bf16[2304,128]{1,0:T(8,128)(2,1)}, bf16[2304,128]{1,0:T(8,128)(2,1)S(1)}, u32[]{:S(2)}, u32[]{:S(2)}) collective-permute-start(bf16[2304,128]{1,0:T(8,128)(2,1)} %get-tuple-element.47), channel_id=1, source_target_pairs={{0,3},{1,0},{2,1},{3,2},{4,7},{5,4},{6,5},{7,6},{8,11},{9,8},{10,9... | collective-permute-start | bytes 1769480 | tf_op jit(solution)/shard_map/ppermute | solution.py:413
  38.5 2.3 %all-to-all-done = bf16[512,2,128]{2,1,0:T(2,128)(2,1)S(1)} async-done(((bf16[512,2,128]{2,1,0:T(2,128)(2,1)}), bf16[512,2,128]{2,1,0:T(2,128)(2,1)S(1)}, u32[]{:S(2)}, u32[]{:S(2)}) %all-to-all-start) | async-done | bytes 262176 | tf_op jit(solution)/shard_map/all_to_all | solution.py:401
  40.8 1.4 shard_map.105
  42.2 14.0 %all-to-all-start.1 = ((bf16[128,5,2,128]{3,2,1,0:T(2,128)(2,1)}), bf16[128,5,2,128]{3,2,1,0:T(2,128)(2,1)S(1)}, u32[]{:S(2)}, u32[]{:S(2)}) async-start(bf16[128,5,2,128]{3,2,1,0:T(2,128)(2,1)} %bitcast.6), calls=%async_computation.1 | async-start | bytes 655360 | tf_op jit(solution)/shard_map/all_to_all | solution.py:401
  56.2 4.6 %collective-permute-done.1.refs_2_ = bf16[2304,128]{1,0:T(8,128)(2,1)S(1)} collective-permute-done((bf16[2304,128]{1,0:T(8,128)(2,1)}, bf16[2304,128]{1,0:T(8,128)(2,1)S(1)}, u32[]{:S(2)}, u32[]{:S(2)}) %collective-permute-start.1) | collective-permute-done | bytes 589856 | tf_op jit(solution)/shard_map/ppermute | solution.py:413
  61.8 10.0 %all-to-all-done.1 = bf16[128,5,2,128]{3,2,1,0:T(2,128)(2,1)S(1)} async-done(((bf16[128,5,2,128]{3,2,1,0:T(2,128)(2,1)}), bf16[128,5,2,128]{3,2,1,0:T(2,128)(2,1)S(1)}, u32[]{:S(2)}, u32[]{:S(2)}) %all-to-all-start.1) | async-done | bytes 327712 | tf_op jit(solution)/shard_map/all_to_all | solution.py:401
  72.4 4.5 %shard_map.107 = (bf16[1536,128]{1,0:T(8,128)(2,1)S(1)}, bf16[1536,128]{1,0:T(8,128)(2,1)}, bf16[1536,128]{1,0:T(8,128)(2,1)S(1)}, bf16[1536,128]{1,0:T(8,128)(2,1)S(1)}, f32[1280,128]{1,0:T(8,128)}) custom-call(s32[1]{0:T(128)} %bitcast.head_ref, s32[8,4]{1,0:T(8,128)S(1)} %copy.14.kinds, bf16[2304,128]{1,0:T(8,128)(2,1)S(1)} %copy-done.5, ...), custom_call_target="tpu_custom_call" | custom-call | flops 1400000000 | bytes 8000000 | tf_op jit(solution)/shard_map/pallas_call | solution.py:227
  77.0 0.8 copy-done.6
  77.7 7.0 %all-to-all-start.2 = ((f32[128,1,1280]{2,1,0:T(1,128)}), f32[128,1,1280]{2,1,0:T(1,128)S(1)}, u32[]{:S(2)}, u32[]{:S(2)}) async-start(f32[128,1,1280]{2,1,0:T(1,128)} %bitcast.8), calls=%async_computation.2 | async-start | bytes 1310720 | tf_op jit(solution)/shard_map/all_to_all | solution.py:401
  84.8 3.5 %collective-permute-start.3 = (bf16[1536,128]{1,0:T(8,128)(2,1)}, bf16[1536,128]{1,0:T(8,128)(2,1)}, u32[]{:S(2)}, u32[]{:S(2)}) collective-permute-start(bf16[1536,128]{1,0:T(8,128)(2,1)} %get-tuple-element.58), channel_id=1, source_target_pairs={{0,3},{1,0},{2,1},{3,2},{4,7},{5,4},{6,5},{7,6},{8,11},{9,8},{10,9... | collective-permute-start | bytes 1179656 | tf_op jit(solution)/shard_map/ppermute | solution.py:424
  88.3 3.4 %collective-permute-start.4 = (bf16[1536,128]{1,0:T(8,128)(2,1)S(1)}, bf16[1536,128]{1,0:T(8,128)(2,1)}, u32[]{:S(2)}, u32[]{:S(2)}) collective-permute-start(bf16[1536,128]{1,0:T(8,128)(2,1)S(1)} %get-tuple-element.59), channel_id=1, source_target_pairs={{0,2},{1,3},{2,0},{3,1},{4,6},{5,7},{6,4},{7,5},{8,10},{9,11},{10,... | collective-permute-start | bytes 1179656 | tf_op jit(solution)/shard_map/ppermute | solution.py:424
  91.7 1.9 %collective-permute-start.5 = (bf16[1536,128]{1,0:T(8,128)(2,1)S(1)}, bf16[1536,128]{1,0:T(8,128)(2,1)}, u32[]{:S(2)}, u32[]{:S(2)}) collective-permute-start(bf16[1536,128]{1,0:T(8,128)(2,1)S(1)} %get-tuple-element.60), channel_id=1, source_target_pairs={{0,1},{1,2},{2,3},{3,0},{4,5},{5,6},{6,7},{7,4},{8,9},{9,10},{10,1... | collective-permute-start | bytes 1179656 | tf_op jit(solution)/shard_map/ppermute | solution.py:424
  94.8 12.5 %all-to-all-done.2 = f32[128,1,1280]{2,1,0:T(1,128)S(1)} async-done(((f32[128,1,1280]{2,1,0:T(1,128)}), f32[128,1,1280]{2,1,0:T(1,128)S(1)}, u32[]{:S(2)}, u32[]{:S(2)}) %all-to-all-start.2) | async-done | bytes 655392 | tf_op jit(solution)/shard_map/all_to_all | solution.py:401
  107.2 2.2 %shard_map.110 = f32[1024,128]{1,0:T(8,128)} custom-call(bf16[1024,1024]{1,0:T(8,128)(2,1)S(1)} %shard_map.109.chosen_ref, f32[1280,128]{1,0:T(8,128)S(1)} %bitcast.15), custom_call_target="tpu_custom_call" | custom-call | tf_op jit(solution)/shard_map/pallas_call | solution.py:375
  109.4 10.1 %all-to-all-start.3 = ((f32[512,2,128]{2,1,0:T(2,128)}), f32[512,2,128]{2,1,0:T(2,128)S(1)}, u32[]{:S(2)}, u32[]{:S(2)}) async-start(f32[512,2,128]{2,1,0:T(2,128)} %bitcast.10), calls=%async_computation.3 | async-start | bytes 1048576 | tf_op jit(solution)/shard_map/all_to_all | solution.py:401
  119.5 1.0 copy-done.7
  120.5 2.7 %shard_map.108 = (bf16[128,32,128]{2,1,0:T(8,128)(2,1)}, f32[2,128,4,128]{3,2,1,0:T(4,128)S(1)}) custom-call(s32[1]{0:T(128)} %bitcast.head_ref, bf16[1536,128]{1,0:T(8,128)(2,1)S(1)} %copy-done.7, bf16[1536,128]{1,0:T(8,128)(2,1)} %collective-permute-done.3.refs_1_, bf16[1536,128]{1,0:T(8,128)(2,1)} %collective-permute-done.4.refs_2_, ...), custom_call_target="tpu_custom_call" | custom-call | flops 20000000000 | bytes 60000000 | tf_op jit(solution)/shard_map/pallas_call | solution.py:266
  123.2 18.3 %all-to-all-done.3 = f32[512,2,128]{2,1,0:T(2,128)S(1)} async-done(((f32[512,2,128]{2,1,0:T(2,128)}), f32[512,2,128]{2,1,0:T(2,128)S(1)}, u32[]{:S(2)}, u32[]{:S(2)}) %all-to-all-start.3) | async-done | bytes 524320 | tf_op jit(solution)/shard_map/all_to_all | solution.py:401
  141.5 0.8 shard_map.111
  (27 shorter events, 3.0 us)
Async XLA Ops:
  0.6 37.7 %copy-start = (s32[1024,4]{0,1:T(4,128)S(1)}, s32[1024,4]{0,1:T(4,128)}, u32[]{:S(2)}) copy-start(s32[1024,4]{0,1:T(4,128)} %param.15) | copy-start | bytes 49156
  2.4 38.4 %all-to-all-start = ((bf16[512,2,128]{2,1,0:T(2,128)(2,1)}), bf16[512,2,128]{2,1,0:T(2,128)(2,1)S(1)}, u32[]{:S(2)}, u32[]{:S(2)}) async-start(bf16[512,2,128]{2,1,0:T(2,128)(2,1)} %bitcast.22), calls=%async_computation | async-start | bytes 524288 | tf_op jit(solution)/shard_map/all_to_all | solution.py:401
  24.6 16.2 %copy-start.3 = (s32[1024,4]{0,1:T(4,128)S(1)}, s32[1024,4]{0,1:T(4,128)}, u32[]{:S(2)}) copy-start(s32[1024,4]{0,1:T(4,128)} %param.14) | copy-start | bytes 49156
  27.6 28.6 %collective-permute-start = (bf16[2304,128]{1,0:T(8,128)(2,1)}, bf16[2304,128]{1,0:T(8,128)(2,1)S(1)}, u32[]{:S(2)}, u32[]{:S(2)}) collective-permute-start(bf16[2304,128]{1,0:T(8,128)(2,1)} %get-tuple-element.45), channel_id=1, source_target_pairs={{0,1},{1,2},{2,3},{3,0},{4,5},{5,6},{6,7},{7,4},{8,9},{9,10},{10,1... | collective-permute-start | bytes 1769480 | tf_op jit(solution)/shard_map/ppermute | solution.py:413
  30.9 29.9 %collective-permute-start.1 = (bf16[2304,128]{1,0:T(8,128)(2,1)}, bf16[2304,128]{1,0:T(8,128)(2,1)S(1)}, u32[]{:S(2)}, u32[]{:S(2)}) collective-permute-start(bf16[2304,128]{1,0:T(8,128)(2,1)} %get-tuple-element.46), channel_id=1, source_target_pairs={{0,2},{1,3},{2,0},{3,1},{4,6},{5,7},{6,4},{7,5},{8,10},{9,11},{10,... | collective-permute-start | bytes 1769480 | tf_op jit(solution)/shard_map/ppermute | solution.py:413
  35.2 25.7 %collective-permute-start.2 = (bf16[2304,128]{1,0:T(8,128)(2,1)}, bf16[2304,128]{1,0:T(8,128)(2,1)S(1)}, u32[]{:S(2)}, u32[]{:S(2)}) collective-permute-start(bf16[2304,128]{1,0:T(8,128)(2,1)} %get-tuple-element.47), channel_id=1, source_target_pairs={{0,3},{1,0},{2,1},{3,2},{4,7},{5,4},{6,5},{7,6},{8,11},{9,8},{10,9... | collective-permute-start | bytes 1769480 | tf_op jit(solution)/shard_map/ppermute | solution.py:413
  40.8 20.0 %copy-start.1 = (f32[8,512]{1,0:T(8,128)S(1)}, f32[8,512]{1,0:T(8,128)}, u32[]{:S(2)}) copy-start(f32[8,512]{1,0:T(8,128)} %refs_0_.1) | copy-start | bytes 49156
  40.8 20.0 %copy-start.2 = (f32[8,512]{1,0:T(8,128)S(1)}, f32[8,512]{1,0:T(8,128)}, u32[]{:S(2)}) copy-start(f32[8,512]{1,0:T(8,128)} %refs_1_.1) | copy-start | bytes 49156
  42.2 29.5 %all-to-all-start.1 = ((bf16[128,5,2,128]{3,2,1,0:T(2,128)(2,1)}), bf16[128,5,2,128]{3,2,1,0:T(2,128)(2,1)S(1)}, u32[]{:S(2)}, u32[]{:S(2)}) async-start(bf16[128,5,2,128]{3,2,1,0:T(2,128)(2,1)} %bitcast.6), calls=%async_computation.1 | async-start | bytes 655360 | tf_op jit(solution)/shard_map/all_to_all | solution.py:401
  56.2 15.5 %copy-start.5 = (bf16[2304,128]{1,0:T(8,128)(2,1)S(1)}, bf16[2304,128]{1,0:T(8,128)(2,1)}, u32[]{:S(2)}) copy-start(bf16[2304,128]{1,0:T(8,128)(2,1)} %get-tuple-element.48.refs_0_) | copy-start | bytes 1769476
  61.2 0.6 copy-start.8
  71.7 0.7 copy-start.9
  77.0 0.8 copy-start.6
  77.7 29.5 %all-to-all-start.2 = ((f32[128,1,1280]{2,1,0:T(1,128)}), f32[128,1,1280]{2,1,0:T(1,128)S(1)}, u32[]{:S(2)}, u32[]{:S(2)}) async-start(f32[128,1,1280]{2,1,0:T(1,128)} %bitcast.8), calls=%async_computation.2 | async-start | bytes 1310720 | tf_op jit(solution)/shard_map/all_to_all | solution.py:401
  84.8 34.7 %collective-permute-start.3 = (bf16[1536,128]{1,0:T(8,128)(2,1)}, bf16[1536,128]{1,0:T(8,128)(2,1)}, u32[]{:S(2)}, u32[]{:S(2)}) collective-permute-start(bf16[1536,128]{1,0:T(8,128)(2,1)} %get-tuple-element.58), channel_id=1, source_target_pairs={{0,3},{1,0},{2,1},{3,2},{4,7},{5,4},{6,5},{7,6},{8,11},{9,8},{10,9... | collective-permute-start | bytes 1179656 | tf_op jit(solution)/shard_map/ppermute | solution.py:424
  88.3 31.2 %collective-permute-start.4 = (bf16[1536,128]{1,0:T(8,128)(2,1)S(1)}, bf16[1536,128]{1,0:T(8,128)(2,1)}, u32[]{:S(2)}, u32[]{:S(2)}) collective-permute-start(bf16[1536,128]{1,0:T(8,128)(2,1)S(1)} %get-tuple-element.59), channel_id=1, source_target_pairs={{0,2},{1,3},{2,0},{3,1},{4,6},{5,7},{6,4},{7,5},{8,10},{9,11},{10,... | collective-permute-start | bytes 1179656 | tf_op jit(solution)/shard_map/ppermute | solution.py:424
  91.7 27.8 %collective-permute-start.5 = (bf16[1536,128]{1,0:T(8,128)(2,1)S(1)}, bf16[1536,128]{1,0:T(8,128)(2,1)}, u32[]{:S(2)}, u32[]{:S(2)}) collective-permute-start(bf16[1536,128]{1,0:T(8,128)(2,1)S(1)} %get-tuple-element.60), channel_id=1, source_target_pairs={{0,1},{1,2},{2,3},{3,0},{4,5},{5,6},{6,7},{7,4},{8,9},{9,10},{10,1... | collective-permute-start | bytes 1179656 | tf_op jit(solution)/shard_map/ppermute | solution.py:424
  93.7 0.7 copy-start.4
  109.4 32.2 %all-to-all-start.3 = ((f32[512,2,128]{2,1,0:T(2,128)}), f32[512,2,128]{2,1,0:T(2,128)S(1)}, u32[]{:S(2)}, u32[]{:S(2)}) async-start(f32[512,2,128]{2,1,0:T(2,128)} %bitcast.10), calls=%async_computation.3 | async-start | bytes 1048576 | tf_op jit(solution)/shard_map/all_to_all | solution.py:401
  119.5 1.0 copy-start.7
